TPU v7x, 128 devices: a whole 4x4x4 slice. The times are simulated.
128 devices in a mesh: front: 64 (over z, y, x), panel: 2 (over core).
Axes of the slice: x: 4, y: 4, z: 4, core: 2. Of those that a mesh axis runs over, the one named last changes fastest.
Arguments:
- sep_factor: bfloat16 [65536, 1024], P(('front', 'panel')), may hold values from -3 to 3, as said below
- coup_factor: bfloat16 [131072, 1024], P(('front', 'panel')), may hold values from -0.1875 to 0.1875
- coup_list: int32 [64, 16], replicated, may hold values from -1 to 15, as said below
- slot_tiles: int32 [64, 16], replicated, may hold values from 0 to 1023, as said below
- anc_tiles: bfloat16 [32768, 128], P('front'), may hold values from -50 to 50
Outputs:
- selected_inverse: float32 [65536, 1024], P(('front', 'panel'))
- variances: float32 [65536], P(('front', 'panel'))
Inputs may be any that keep to these rules, and one draw needn't show every extreme that they name: `sep_factor`: each front's block of 1024 rows is lower triangular with a diagonal of 1 or more. `coup_list`: a front's entries name distinct blocks; live entries come first and the rest are -1; every front has 4 or more live entries and some front has 16. `slot_tiles`: every strip id of 0 to 1023 appears in exactly one slot; every group holds exactly one strip of each block row.
All inputs are finite; a program needn't handle non-finite values.
Results may differ from a plain program's by a relative error of at most 0.0056.
Values may be sent and summed in bfloat16 or wider, within the bound.
No kernel may reach another device: no remote copies, remote signals or barrier semaphores. Data moves between devices by JAX's collectives and lax.ppermute only.
A program may use at most 128 MiB of HBM per device.

v0:
```python
import jax
import jax.numpy as jnp
import numpy as np
from jax import lax
from jax.experimental import pallas as pl
from jax.experimental.pallas import tpu as pltpu
from jax.sharding import PartitionSpec as P

AXES = ("front", "panel")
BLOCK = 128
STRIP = 32
NABOVE = 16
HALF = NABOVE // 2
SIDE = 1024
ROWS = SIDE // 2
F32 = jnp.float32
BF16 = jnp.bfloat16
VMEM = pl.BlockSpec(memory_space=pltpu.VMEM)
SMEM = pl.BlockSpec(memory_space=pltpu.SMEM)
LIMIT = 56 * 1024 * 1024


def params():
    return pltpu.CompilerParams(vmem_limit_bytes=LIMIT)


def cost(macs, moved):
    return pl.CostEstimate(flops=2 * macs, bytes_accessed=moved, transcendentals=0)


def dot(a, b):
    return jnp.dot(a, b, preferred_element_type=F32)


def dot_tn(a, b):
    return lax.dot_general(a, b, (((0,), (0,)), ((), ())), preferred_element_type=F32)


def split(x):
    hi = x.astype(BF16)
    return hi, (x - hi.astype(F32)).astype(BF16)


def spread(bits, step):
    return step * ((((bits >> 2) & 1) << 4) | (((bits >> 1) & 1) << 2) | (bits & 1))


def steps_of(core):
    return ((1, 3), (3, 1))[core]


def lowest(group, step):
    if step == 1:
        return group & 0b101010
    return group ^ (3 * ((group >> 1) & 0b010101))


def cubes(phase):
    out = []
    for core in range(2):
        step = steps_of(core)[phase]
        for first in range(64):
            if lowest(first, step) == first:
                out.append([(first ^ spread(bits, step)) * 2 + core for bits in range(8)])
    return out


def gather_cube(parts, phase):
    return lax.all_to_all(
        parts, AXES, split_axis=0, concat_axis=0, tiled=True, axis_index_groups=cubes(phase)
    )


def pick_kernel(where_ref, slots_ref, strips_ref, out_ref):
    core, group = where_ref[0], where_ref[1]
    for slot in range(NABOVE):
        row = slots_ref[group * NABOVE + slot] // 64 - core * HALF

        @pl.when((row >= 0) & (row < HALF))
        def _():
            strip = strips_ref[slot * STRIP : (slot + 1) * STRIP, :]
            for copy in range(8):
                at = pl.multiple_of(copy * HALF * STRIP + row * STRIP, STRIP)
                out_ref[pl.ds(at, STRIP), :] = strip


def pick_strips(where, slots, strips):
    return pl.pallas_call(
        pick_kernel,
        out_shape=jax.ShapeDtypeStruct((8 * HALF * STRIP, BLOCK), BF16),
        in_specs=[SMEM, SMEM, VMEM],
        out_specs=VMEM,
        compiler_params=params(),
        cost_estimate=cost(0, 1 << 20),
        name="pick_strips",
    )(where, slots, strips)


def invert_kernel(where_ref, mine_ref, other_ref, hi_ref, lo_ref, low_ref):
    core = where_ref[0]
    low_ref[pl.ds(pl.multiple_of(core * ROWS, ROWS), ROWS), :] = mine_ref[...]
    low_ref[pl.ds(pl.multiple_of((1 - core) * ROWS, ROWS), ROWS), :] = other_ref[...]
    hi_ref[...] = jnp.zeros_like(hi_ref)
    lo_ref[...] = jnp.zeros_like(lo_ref)
    row = lax.broadcasted_iota(jnp.int32, (BLOCK, BLOCK), 0)
    col = lax.broadcasted_iota(jnp.int32, (BLOCK, BLOCK), 1)
    differ = row ^ col
    below = row > col
    factors, inverses = [], []
    for b in range(8):
        at = slice(b * BLOCK, (b + 1) * BLOCK)
        factor = low_ref[at, at].astype(F32)
        diag = jnp.where(row == col, factor, 0.0)
        by_row = 1.0 / jnp.sum(diag, axis=1, keepdims=True)
        by_col = 1.0 / jnp.sum(diag, axis=0, keepdims=True)
        next_to = jnp.where(below & (differ < 2), factor, 0.0)
        inverses.append(jnp.where(row == col, by_row, 0.0) - by_row * next_to * by_col)
        factors.append(factor)
    size = 2
    while size < BLOCK:
        mask = below & (differ >= size) & (differ < 2 * size)
        for b in range(8):
            hi, lo = split(inverses[b])
            corner = jnp.where(mask, factors[b], 0.0).astype(BF16)
            both = dot(corner, jnp.concatenate([hi, lo], axis=1))
            t_hi, t_lo = split(both[:, :BLOCK] + both[:, BLOCK:])
            stacked = jnp.concatenate(
                [
                    jnp.concatenate([t_hi, t_lo], axis=1),
                    jnp.concatenate([t_hi, jnp.zeros_like(t_hi)], axis=1),
                ],
                axis=0,
            )
            both = dot(jnp.concatenate([hi, lo], axis=1), stacked)
            inverses[b] = inverses[b] - (both[:, :BLOCK] + both[:, BLOCK:])
        size *= 2
    for b in range(8):
        at = slice(b * BLOCK, (b + 1) * BLOCK)
        hi_ref[at, at], lo_ref[at, at] = split(inverses[b])
    while size < SIDE:
        for start in range(0, SIDE, 2 * size):
            first, second = slice(start, start + size), slice(start + size, start + 2 * size)
            corner = low_ref[second, first]
            t_hi, t_lo = split(dot(corner, hi_ref[first, first]) + dot(corner, lo_ref[first, first]))
            hi, lo = hi_ref[second, second], lo_ref[second, second]
            hi_ref[second, first], lo_ref[second, first] = split(
                -(dot(hi, t_hi) + dot(hi, t_lo) + dot(lo, t_hi))
            )
        size *= 2


def invert(where, mine, other):
    full = jax.ShapeDtypeStruct((SIDE, SIDE), BF16)
    return pl.pallas_call(
        invert_kernel,
        out_shape=(full, full),
        in_specs=[SMEM, VMEM, VMEM],
        out_specs=(VMEM, VMEM),
        scratch_shapes=[pltpu.VMEM((SIDE, SIDE), BF16)],
        compiler_params=params(),
        cost_estimate=cost(5 << 30, 6 << 20),
        name="invert",
    )(where, mine, other)


def wide_kernel(coupling_ref, hi_ref, out_ref):
    tile = 256
    for n in range(0, SIDE, tile):
        out_ref[:, n : n + tile] = dot(coupling_ref[:, n:], hi_ref[n:, n : n + tile]).astype(BF16)


def make_wide(coupling, hi):
    return pl.pallas_call(
        wide_kernel,
        out_shape=jax.ShapeDtypeStruct((SIDE, SIDE), BF16),
        in_specs=[VMEM, VMEM],
        out_specs=VMEM,
        compiler_params=params(),
        cost_estimate=cost(1 << 30, 6 << 20),
        name="make_wide",
    )(coupling, hi)


def square_kernel(where_ref, hi_ref, lo_ref, out_ref):
    mine = pl.ds(pl.multiple_of(where_ref[0] * ROWS, ROWS), ROWS)
    tile = 256
    for n in range(0, SIDE, tile):
        columns = slice(n, n + tile)
        hi, lo = hi_ref[n:, columns], lo_ref[n:, columns]
        left = hi_ref[n:, mine]
        out_ref[:, columns] = dot_tn(left, hi) + dot_tn(left, lo) + dot_tn(lo_ref[n:, mine], hi)


def make_square(where, hi, lo):
    return pl.pallas_call(
        square_kernel,
        out_shape=jax.ShapeDtypeStruct((ROWS, SIDE), F32),
        in_specs=[SMEM, VMEM, VMEM],
        out_specs=VMEM,
        compiler_params=params(),
        cost_estimate=cost(1 << 30, 6 << 20),
        name="make_square",
    )(where, hi, lo)


def place_kernel(where_ref, list_ref, mine_ref, other_ref, out_ref):
    core, group = where_ref[0], where_ref[1]
    out_ref[...] = jnp.zeros_like(out_ref)
    for a in range(NABOVE):
        owner, at = a // HALF, (a % HALF) * BLOCK
        block = list_ref[group * NABOVE + a]
        rows = pl.ds(pl.multiple_of(jnp.maximum(block, 0) * BLOCK, BLOCK), BLOCK)

        @pl.when((block >= 0) & (core == owner))
        def _():
            out_ref[rows, :] = mine_ref[at : at + BLOCK, :]

        @pl.when((block >= 0) & (core != owner))
        def _():
            out_ref[rows, :] = other_ref[at : at + BLOCK, :]


def place_wide(where, lists, mine, other):
    return pl.pallas_call(
        place_kernel,
        out_shape=jax.ShapeDtypeStruct((NABOVE * BLOCK, SIDE), BF16),
        in_specs=[SMEM, SMEM, VMEM, VMEM],
        out_specs=VMEM,
        compiler_params=params(),
        cost_estimate=cost(0, 8 << 20),
        name="place_wide",
    )(where, lists, mine, other)


def carry_kernel(where_ref, places_ref, strips_ref, wide_ref, carried_ref, send_ref, sigma_ref):
    core, group = where_ref[0], where_ref[1]
    first, second = jnp.where(core == 0, 1, 3), jnp.where(core == 0, 3, 1)

    def base(g, step):
        return jnp.where(step == 1, g & 0b101010, g ^ (3 * ((g >> 1) & 0b010101)))

    @pl.loop(0, 64)
    def _(n):
        middle = base(group, second) ^ spread(n >> 3, second)
        source = base(middle, first) ^ spread(n & 7, first)
        for row in range(HALF):
            place = places_ref[source * HALF + row]
            to = pl.multiple_of(row * BLOCK + (place & 3) * STRIP, STRIP)
            across = pl.multiple_of((place >> 2) * BLOCK, BLOCK)
            at = pl.multiple_of(n * HALF * STRIP + row * STRIP, STRIP)
            sigma_ref[pl.ds(to, STRIP), pl.ds(across, BLOCK)] = strips_ref[pl.ds(at, STRIP), :]

    tile = 256
    for n in range(0, SIDE, tile):
        carried_ref[:, n : n + tile] = dot(sigma_ref[...], wide_ref[:, n : n + tile]).astype(BF16)
    mine = pl.ds(pl.multiple_of(core * SIDE, SIDE), SIDE)
    theirs = pl.ds(pl.multiple_of((1 - core) * ROWS, ROWS), ROWS)
    for n in range(0, SIDE, tile):
        send_ref[:, n : n + tile] = dot_tn(wide_ref[mine, theirs], carried_ref[:, n : n + tile]).astype(BF16)


def carry(where, places, strips, wide):
    return pl.pallas_call(
        carry_kernel,
        out_shape=(
            jax.ShapeDtypeStruct((SIDE, SIDE), BF16),
            jax.ShapeDtypeStruct((ROWS, SIDE), BF16),
        ),
        in_specs=[SMEM, SMEM, VMEM, VMEM],
        out_specs=(VMEM, VMEM),
        scratch_shapes=[pltpu.VMEM((SIDE, NABOVE * BLOCK), BF16)],
        compiler_params=params(),
        cost_estimate=cost(5 << 29, 12 << 20),
        name="carry",
    )(where, places, strips, wide)


def own_kernel(where_ref, wide_ref, carried_ref, square_ref, out_ref):
    core = where_ref[0]
    rows = pl.ds(pl.multiple_of(core * SIDE, SIDE), SIDE)
    mine = pl.ds(pl.multiple_of(core * ROWS, ROWS), ROWS)
    tile = 256
    for n in range(0, SIDE, tile):
        columns = slice(n, n + tile)
        out_ref[:, columns] = square_ref[:, columns] + dot_tn(wide_ref[rows, mine], carried_ref[:, columns])


def own_product(where, wide, carried, square):
    return pl.pallas_call(
        own_kernel,
        out_shape=jax.ShapeDtypeStruct((ROWS, SIDE), F32),
        in_specs=[SMEM, VMEM, VMEM, VMEM],
        out_specs=VMEM,
        compiler_params=params(),
        cost_estimate=cost(1 << 29, 8 << 20),
        name="own_product",
    )(where, wide, carried, square)


def finish_kernel(where_ref, own_ref, received_ref, out_ref, diag_ref):
    out_ref[...] = own_ref[...] + received_ref[...].astype(F32)
    block = out_ref[:, pl.ds(pl.multiple_of(where_ref[0] * ROWS, ROWS), ROWS)]
    row = lax.broadcasted_iota(jnp.int32, (ROWS, ROWS), 0)
    col = lax.broadcasted_iota(jnp.int32, (ROWS, ROWS), 1)
    diag_ref[...] = jnp.sum(jnp.where(row == col, block, 0.0), axis=0, keepdims=True)


def finish(where, own, received):
    return pl.pallas_call(
        finish_kernel,
        out_shape=(
            jax.ShapeDtypeStruct((ROWS, SIDE), F32),
            jax.ShapeDtypeStruct((1, ROWS), F32),
        ),
        in_specs=[SMEM, VMEM, VMEM],
        out_specs=(VMEM, VMEM),
        compiler_params=params(),
        cost_estimate=cost(0, 6 << 20),
        name="finish",
    )(where, own, received)


def swap(x):
    return lax.ppermute(x, "panel", [(0, 1), (1, 0)])


def on_device(sep_factor, coup_factor, coup_list, slot_tiles, anc_tiles):
    core = lax.axis_index("panel")
    group = lax.axis_index("front")
    where = jnp.stack([core, group]).astype(jnp.int32)
    lists = coup_list.reshape(-1)
    slots = slot_tiles.reshape(-1)
    wanted = core * HALF + jnp.arange(HALF, dtype=jnp.int32)
    hit = (slot_tiles // 64)[:, None, :] == wanted[None, :, None]
    places = jnp.sum(jnp.where(hit, (slot_tiles % 64)[:, None, :], 0), axis=2).reshape(-1)

    sep_other = swap(sep_factor)
    picked = pick_strips(where, slots, anc_tiles)
    near = gather_cube(picked, 0)
    strips = gather_cube(jnp.broadcast_to(near[None], (8,) + near.shape).reshape(-1, BLOCK), 1)

    hi, lo = invert(where, sep_factor, sep_other)
    wide_mine = make_wide(coup_factor, hi)
    wide_other = swap(wide_mine)
    square = make_square(where, hi, lo)
    wide = place_wide(where, lists, wide_mine, wide_other)
    carried, to_send = carry(where, places, strips, wide)
    received = swap(to_send)
    own = own_product(where, wide, carried, square)
    selected, variances = finish(where, own, received)
    return selected, variances.reshape(ROWS)


def solution(mesh):
    placed = (P(AXES, None), P(AXES, None), P(), P(), P("front", None))
    return jax.shard_map(
        on_device,
        mesh=mesh,
        in_specs=placed,
        out_specs=(P(AXES, None), P(AXES)),
        check_vma=False,
    )
```

profile of v0, /device:TPU:1, one launch (start us, length us, event | category | flops | bytes accessed | tf_op | source)
XLA Modules:
  0.0 93.1 jit_solution(5484389245997700818)
XLA Ops:
  0.6 1.5 %collective-permute-start = (bf16[512,1024]{1,0:T(8,128)(2,1)}, bf16[512,1024]{1,0:T(8,128)(2,1)S(1)}, u32[]{:S(2)}, u32[]{:S(2)}) collective-permute-start(bf16[512,1024]{1,0:T(8,128)(2,1)} %mine_ref.1), channel_id=1, source_target_pairs={{0,1},{1,0},{2,3},{3,2},{4,5},{5,4},{6,7},{7,6},{8,9},{9,8},{10,11... | collective-permute-start | bytes 3145736 | tf_op jit(solution)/shard_map/ppermute | solution.py:324
  2.1 0.8 copy.15
  2.9 0.7 reshape.32.slots_ref
  3.6 0.6 pad_add_fusion.where_ref
  4.2 2.0 %pick_strips.1 = bf16[2048,128]{1,0:T(8,128)(2,1)} custom-call(s32[2]{0:T(128)} %pad_add_fusion.where_ref, s32[1024]{0:T(1024)} %reshape.32.slots_ref, bf16[512,128]{1,0:T(8,128)(2,1)} %strips_ref.1), custom_call_target="tpu_custom_call" | custom-call | bytes 1048576 | tf_op jit(solution)/shard_map/pick_strips/pallas_call | solution.py:88
  6.3 20.6 %all_to_all.17 = bf16[8,256,128]{2,1,0:T(8,128)(2,1)S(1)} all-to-all(bf16[8,256,128]{2,1,0:T(8,128)(2,1)} %bitcast.7), channel_id=1, replica_groups={{0,2,8,10,32,34,40,42},{4,6,12,14,36,38,44,46},{16,18,24,26,48,50,56,58..., dimensions={0} | all-to-all | bytes 1048576 | tf_op jit(solution)/shard_map/all_to_all | solution.py:69
  26.9 2.5 %broadcast_in_dim.26 = bf16[8,2048,128]{2,1,0:T(8,128)(2,1)} broadcast(bf16[2048,128]{1,0:T(8,128)(2,1)S(1)} %bitcast.6), dimensions={1,2} | broadcast | bytes 4718592 | tf_op jit(solution)/shard_map/broadcast_in_dim | solution.py:340
  29.4 4.5 %all-to-all-start.1 = ((bf16[8,2048,128]{2,1,0:T(8,128)(2,1)}), bf16[8,2048,128]{2,1,0:T(8,128)(2,1)}, u32[]{:S(2)}, u32[]{:S(2)}) async-start(bf16[8,2048,128]{2,1,0:T(8,128)(2,1)} %broadcast_in_dim.26), calls=%async_computation.1 | async-start | bytes 8388608 | tf_op jit(solution)/shard_map/all_to_all | solution.py:69
  33.9 0.0 collective-permute-done.other_ref
  33.9 0.0 copy-start.4
  34.0 1.1 %copy-done.4 = bf16[512,1024]{1,0:T(8,128)(2,1)} copy-done((bf16[512,1024]{1,0:T(8,128)(2,1)}, bf16[512,1024]{1,0:T(8,128)(2,1)S(1)}, u32[]{:S(2)}) %copy-start.4) | copy-done | bytes 1048600
  35.0 8.6 %invert.1 = (bf16[1024,1024]{1,0:T(8,128)(2,1)}, bf16[1024,1024]{1,0:T(8,128)(2,1)}) custom-call(s32[2]{0:T(128)} %pad_add_fusion.where_ref, bf16[512,1024]{1,0:T(8,128)(2,1)} %mine_ref.1, bf16[512,1024]{1,0:T(8,128)(2,1)} %copy-done.4), custom_call_target="tpu_custom_call" | custom-call | flops 10737418240 | bytes 6291456 | tf_op jit(solution)/shard_map/invert/pallas_call | solution.py:154
  43.6 0.0 copy-start.2
  43.6 0.0 copy-start.3
  43.6 5.1 %make_wide.1.mine_ref = bf16[1024,1024]{1,0:T(8,128)(2,1)} custom-call(bf16[1024,1024]{1,0:T(8,128)(2,1)} %coupling_ref.1, bf16[1024,1024]{1,0:T(8,128)(2,1)} %get-tuple-element.8.hi_ref), custom_call_target="tpu_custom_call" | custom-call | flops 2147483648 | bytes 6291456 | tf_op jit(solution)/shard_map/make_wide/pallas_call | solution.py:173
  48.7 0.0 collective-permute-start.1
  48.7 0.0 copy-done.2
  48.7 0.1 select_reduce_fusion
  48.8 0.1 copy.14
  48.9 0.7 reshape.31.places_ref
  49.6 0.0 copy-done.3
  49.6 0.1 copy.13
  49.7 0.7 reshape.30.list_ref
  50.3 2.7 %collective-permute-done.1.other_ref = bf16[1024,1024]{1,0:T(8,128)(2,1)S(1)} collective-permute-done((bf16[1024,1024]{1,0:T(8,128)(2,1)}, bf16[1024,1024]{1,0:T(8,128)(2,1)S(1)}, u32[]{:S(2)}, u32[]{:S(2)}) %collective-permute-start.1) | collective-permute-done | bytes 2097184 | tf_op jit(solution)/shard_map/ppermute | solution.py:324
  53.1 0.0 copy-start
  53.1 1.3 %copy-done = bf16[1024,1024]{1,0:T(8,128)(2,1)} copy-done((bf16[1024,1024]{1,0:T(8,128)(2,1)}, bf16[1024,1024]{1,0:T(8,128)(2,1)S(1)}, u32[]{:S(2)}) %copy-start) | copy-done | bytes 2097176
  54.4 5.1 %place_wide.1.wide_ref = bf16[2048,1024]{1,0:T(8,128)(2,1)} custom-call(s32[2]{0:T(128)} %pad_add_fusion.where_ref, s32[1024]{0:T(1024)} %reshape.30.list_ref, bf16[1024,1024]{1,0:T(8,128)(2,1)} %make_wide.1.mine_ref, bf16[1024,1024]{1,0:T(8,128)(2,1)} %copy-done), custom_call_target="tpu_custom_call" | custom-call | bytes 8388608 | tf_op jit(solution)/shard_map/place_wide/pallas_call | solution.py:224
  59.5 3.2 %all-to-all-done.1 = bf16[8,2048,128]{2,1,0:T(8,128)(2,1)} async-done(((bf16[8,2048,128]{2,1,0:T(8,128)(2,1)}), bf16[8,2048,128]{2,1,0:T(8,128)(2,1)}, u32[]{:S(2)}, u32[]{:S(2)}) %all-to-all-start.1) | async-done | bytes 4194336 | tf_op jit(solution)/shard_map/all_to_all | solution.py:69
  62.7 13.9 %carry.1 = (bf16[1024,1024]{1,0:T(8,128)(2,1)}, bf16[512,1024]{1,0:T(8,128)(2,1)}) custom-call(s32[2]{0:T(128)} %pad_add_fusion.where_ref, s32[512]{0:T(512)} %reshape.31.places_ref, bf16[16384,128]{1,0:T(8,128)(2,1)} %bitcast.4.strips_ref, bf16[2048,1024]{1,0:T(8,128)(2,1)} %place_wide.1.wide_ref), custom_call_target="tpu_custom_call" | custom-call | flops 5368709120 | bytes 12582912 | tf_op jit(solution)/shard_map/carry/pallas_call | solution.py:263
  76.6 0.0 collective-permute-start.2
  76.6 5.9 %make_square.1.square_ref = f32[512,1024]{1,0:T(8,128)} custom-call(s32[2]{0:T(128)} %pad_add_fusion.where_ref, bf16[1024,1024]{1,0:T(8,128)(2,1)} %get-tuple-element.8.hi_ref, bf16[1024,1024]{1,0:T(8,128)(2,1)} %get-tuple-element.10.lo_ref), custom_call_target="tpu_custom_call" | custom-call | flops 2147483648 | bytes 6291456 | tf_op jit(solution)/shard_map/make_square/pallas_call | solution.py:195
  82.5 6.1 %own_product.1.own_ref = f32[512,1024]{1,0:T(8,128)} custom-call(s32[2]{0:T(128)} %pad_add_fusion.where_ref, bf16[2048,1024]{1,0:T(8,128)(2,1)} %place_wide.1.wide_ref, bf16[1024,1024]{1,0:T(8,128)(2,1)} %get-tuple-element.9.carried_ref, f32[512,1024]{1,0:T(8,128)} %make_square.1.square_ref), custom_call_target="tpu_custom_call" | custom-call | flops 1073741824 | bytes 8388608 | tf_op jit(solution)/shard_map/own_product/pallas_call | solution.py:289
  88.6 0.0 collective-permute-done.2.received_ref
  88.6 0.0 copy-start.1
  88.6 1.0 %copy-done.1 = bf16[512,1024]{1,0:T(8,128)(2,1)} copy-done((bf16[512,1024]{1,0:T(8,128)(2,1)}, bf16[512,1024]{1,0:T(8,128)(2,1)S(1)}, u32[]{:S(2)}) %copy-start.1) | copy-done | bytes 1048600
  89.6 3.5 %finish.1 = (f32[512,1024]{1,0:T(8,128)}, f32[1,512]{1,0:T(1,128)}) custom-call(s32[2]{0:T(128)} %pad_add_fusion.where_ref, f32[512,1024]{1,0:T(8,128)} %own_product.1.own_ref, bf16[512,1024]{1,0:T(8,128)(2,1)} %copy-done.1), custom_call_target="tpu_custom_call" | custom-call | bytes 6291456 | tf_op jit(solution)/shard_map/finish/pallas_call | solution.py:309
  (2 shorter events, 0.0 us)
Async XLA Ops:
  0.6 33.3 %collective-permute-start = (bf16[512,1024]{1,0:T(8,128)(2,1)}, bf16[512,1024]{1,0:T(8,128)(2,1)S(1)}, u32[]{:S(2)}, u32[]{:S(2)}) collective-permute-start(bf16[512,1024]{1,0:T(8,128)(2,1)} %mine_ref.1), channel_id=1, source_target_pairs={{0,1},{1,0},{2,3},{3,2},{4,5},{5,4},{6,7},{7,6},{8,9},{9,8},{10,11... | collective-permute-start | bytes 3145736 | tf_op jit(solution)/shard_map/ppermute | solution.py:324
  29.4 33.3 %all-to-all-start.1 = ((bf16[8,2048,128]{2,1,0:T(8,128)(2,1)}), bf16[8,2048,128]{2,1,0:T(8,128)(2,1)}, u32[]{:S(2)}, u32[]{:S(2)}) async-start(bf16[8,2048,128]{2,1,0:T(8,128)(2,1)} %broadcast_in_dim.26), calls=%async_computation.1 | async-start | bytes 8388608 | tf_op jit(solution)/shard_map/all_to_all | solution.py:69
  33.9 1.1 %copy-start.4 = (bf16[512,1024]{1,0:T(8,128)(2,1)}, bf16[512,1024]{1,0:T(8,128)(2,1)S(1)}, u32[]{:S(2)}) copy-start(bf16[512,1024]{1,0:T(8,128)(2,1)S(1)} %collective-permute-done.other_ref) | copy-start | bytes 3145732
  43.6 5.1 %copy-start.2 = (s32[64,16]{0,1:T(8,128)S(1)}, s32[64,16]{0,1:T(8,128)}, u32[]{:S(2)}) copy-start(s32[64,16]{0,1:T(8,128)} %param.8) | copy-start | bytes 12292
  43.6 6.0 %copy-start.3 = (s32[64,16]{0,1:T(8,128)S(1)}, s32[64,16]{0,1:T(8,128)}, u32[]{:S(2)}) copy-start(s32[64,16]{0,1:T(8,128)} %param.7) | copy-start | bytes 12292
  48.7 4.4 %collective-permute-start.1 = (bf16[1024,1024]{1,0:T(8,128)(2,1)}, bf16[1024,1024]{1,0:T(8,128)(2,1)S(1)}, u32[]{:S(2)}, u32[]{:S(2)}) collective-permute-start(bf16[1024,1024]{1,0:T(8,128)(2,1)} %make_wide.1.mine_ref), channel_id=1, source_target_pairs={{0,1},{1,0},{2,3},{3,2},{4,5},{5,4},{6,7},{7,6},{8,9},{9,8},{10,11... | collective-permute-start | bytes 6291464 | tf_op jit(solution)/shard_map/ppermute | solution.py:324
  53.1 1.3 %copy-start = (bf16[1024,1024]{1,0:T(8,128)(2,1)}, bf16[1024,1024]{1,0:T(8,128)(2,1)S(1)}, u32[]{:S(2)}) copy-start(bf16[1024,1024]{1,0:T(8,128)(2,1)S(1)} %collective-permute-done.1.other_ref) | copy-start | bytes 6291460
  76.6 12.0 %collective-permute-start.2 = (bf16[512,1024]{1,0:T(8,128)(2,1)}, bf16[512,1024]{1,0:T(8,128)(2,1)S(1)}, u32[]{:S(2)}, u32[]{:S(2)}) collective-permute-start(bf16[512,1024]{1,0:T(8,128)(2,1)} %get-tuple-element.11), channel_id=1, source_target_pairs={{0,1},{1,0},{2,3},{3,2},{4,5},{5,4},{6,7},{7,6},{8,9},{9,8},{10,11... | collective-permute-start | bytes 3145736 | tf_op jit(solution)/shard_map/ppermute | solution.py:324
  88.6 1.0 %copy-start.1 = (bf16[512,1024]{1,0:T(8,128)(2,1)}, bf16[512,1024]{1,0:T(8,128)(2,1)S(1)}, u32[]{:S(2)}) copy-start(bf16[512,1024]{1,0:T(8,128)(2,1)S(1)} %collective-permute-done.2.received_ref) | copy-start | bytes 3145732
where the time goes:
time: 93.4 us; the launch traced here: 93.1 us
  Pallas kernels  50.2 us (54%)
  blocking collectives  20.6 us (22%)
  local copies, waits for them, and re-layouts  8.82 us (9%)
  starting transfers between devices  6.05 us (6%)
  waiting for transfers between devices  5.96 us (6%)
    all_to_all x1, blocking collectives, gather_cube(): lax.all_to_all(parts, AXES, split_axis=0, concat_axis=0, tiled=True, axis...  20.6 us
    pallas_call x1, Pallas kernels, carry(): pl.pallas_call(carry_kernel, out_shape=(jax.ShapeDtypeStruct((SIDE, SIDE)...  13.9 us
    pallas_call x1, Pallas kernels, invert(): pl.pallas_call(invert_kernel, out_shape=(full, full), in_specs=[SMEM, VME...  8.61 us
    pallas_call x1, Pallas kernels, own_product(): pl.pallas_call(own_kernel, out_shape=jax.ShapeDtypeStruct((ROWS, SIDE), F...  6.13 us
    pallas_call x1, Pallas kernels, make_square(): pl.pallas_call(square_kernel, out_shape=jax.ShapeDtypeStruct((ROWS, SIDE)...  5.91 us
    pallas_call x1, Pallas kernels, place_wide(): pl.pallas_call(place_kernel, out_shape=jax.ShapeDtypeStruct((NABOVE * BLO...  5.08 us
    pallas_call x1, Pallas kernels, make_wide(): pl.pallas_call(wide_kernel, out_shape=jax.ShapeDtypeStruct((SIDE, SIDE),...  5.08 us
    all_to_all x1, starting transfers between devices, gather_cube(): lax.all_to_all(parts, AXES, split_axis=0, concat_axis=0, tiled=True, axis...  4.54 us
  transfers between devices with their start and end apart: 4, of which 2 were waited for; matrix products, arithmetic and copies ran while one was open for 7% of the time, Pallas kernels for 35%

commit v1 on v0

v1 whole, which is shorter than its diff:
```python
import jax
import jax.numpy as jnp
import numpy as np
from jax import lax
from jax.experimental import pallas as pl
from jax.experimental.pallas import tpu as pltpu
from jax.sharding import PartitionSpec as P

AXES = ("front", "panel")
BLOCK = 128
STRIP = 32
NABOVE = 16
HALF = NABOVE // 2
SIDE = 1024
ROWS = SIDE // 2
F32 = jnp.float32
BF16 = jnp.bfloat16
VMEM = pl.BlockSpec(memory_space=pltpu.VMEM)
SMEM = pl.BlockSpec(memory_space=pltpu.SMEM)
MIB = 1024 * 1024


def params(mib):
    return pltpu.CompilerParams(vmem_limit_bytes=mib * MIB)


def cost(macs, moved):
    return pl.CostEstimate(flops=2 * macs, bytes_accessed=moved, transcendentals=0)


def dot(a, b):
    return jnp.dot(a, b, preferred_element_type=F32)


def dot_tn(a, b):
    return lax.dot_general(a, b, (((0,), (0,)), ((), ())), preferred_element_type=F32)


def split(x):
    hi = x.astype(BF16)
    return hi, (x - hi.astype(F32)).astype(BF16)


def spread(bits, step):
    return step * ((((bits >> 2) & 1) << 4) | (((bits >> 1) & 1) << 2) | (bits & 1))


def steps_of(core):
    return ((1, 3), (3, 1))[core]


def lowest(group, step):
    if step == 1:
        return group & 0b101010
    return group ^ (3 * ((group >> 1) & 0b010101))


def cubes(phase):
    out = []
    for core in range(2):
        step = steps_of(core)[phase]
        for first in range(64):
            if lowest(first, step) == first:
                out.append([(first ^ spread(bits, step)) * 2 + core for bits in range(8)])
    return out


def gather_cube(parts, phase):
    return lax.all_to_all(
        parts, AXES, split_axis=0, concat_axis=0, tiled=True, axis_index_groups=cubes(phase)
    )


def pick_kernel(slots_ref, table_ref, strips_ref, out_ref, places_ref):
    core, group = lax.axis_index("panel"), lax.axis_index("front")
    for slot in range(NABOVE):
        row = slots_ref[slot, group] // 64 - core * HALF

        @pl.when((row >= 0) & (row < HALF))
        def _():
            strip = strips_ref[slot * STRIP : (slot + 1) * STRIP, :]
            for copy in range(8):
                at = pl.multiple_of(copy * HALF * STRIP + row * STRIP, STRIP)
                out_ref[pl.ds(at, STRIP), :] = strip

    ids = table_ref[...]
    for row in range(HALF):
        hit = (ids >> 6) == core * HALF + row
        places_ref[row : row + 1, :] = jnp.sum(jnp.where(hit, ids & 63, 0), axis=0, keepdims=True)


def pick_strips(slots, strips):
    return pl.pallas_call(
        pick_kernel,
        out_shape=(
            jax.ShapeDtypeStruct((8 * HALF * STRIP, BLOCK), BF16),
            jax.ShapeDtypeStruct((HALF, 64), jnp.int32),
        ),
        in_specs=[SMEM, VMEM, VMEM],
        out_specs=(VMEM, VMEM),
        compiler_params=params(4),
        cost_estimate=cost(0, 1 << 20),
        name="pick_strips",
    )(slots, slots, strips)


def solve_kernel(mine_ref, other_ref, coupling_ref, wide_ref, square_ref, low_ref, hi_ref, lo_ref):
    core = lax.axis_index("panel")
    low_ref[pl.ds(pl.multiple_of(core * ROWS, ROWS), ROWS), :] = mine_ref[...]
    low_ref[pl.ds(pl.multiple_of((1 - core) * ROWS, ROWS), ROWS), :] = other_ref[...]
    hi_ref[...] = jnp.zeros_like(hi_ref)
    lo_ref[...] = jnp.zeros_like(lo_ref)
    row = lax.broadcasted_iota(jnp.int32, (BLOCK, BLOCK), 0)
    col = lax.broadcasted_iota(jnp.int32, (BLOCK, BLOCK), 1)
    differ = row ^ col
    below = row > col
    factors, inverses = [], []
    for b in range(8):
        at = slice(b * BLOCK, (b + 1) * BLOCK)
        factor = low_ref[at, at].astype(F32)
        diag = jnp.where(row == col, factor, 0.0)
        by_row = 1.0 / jnp.sum(diag, axis=1, keepdims=True)
        by_col = 1.0 / jnp.sum(diag, axis=0, keepdims=True)
        next_to = jnp.where(below & (differ < 2), factor, 0.0)
        inverses.append(jnp.where(row == col, by_row, 0.0) - by_row * next_to * by_col)
        factors.append(factor)
    size = 2
    while size < BLOCK:
        mask = below & (differ >= size) & (differ < 2 * size)
        for b in range(8):
            hi, lo = split(inverses[b])
            corner = jnp.where(mask, factors[b], 0.0).astype(BF16)
            both = dot(corner, jnp.concatenate([hi, lo], axis=1))
            t_hi, t_lo = split(both[:, :BLOCK] + both[:, BLOCK:])
            stacked = jnp.concatenate(
                [
                    jnp.concatenate([t_hi, t_lo], axis=1),
                    jnp.concatenate([t_hi, jnp.zeros_like(t_hi)], axis=1),
                ],
                axis=0,
            )
            both = dot(jnp.concatenate([hi, lo], axis=1), stacked)
            inverses[b] = inverses[b] - (both[:, :BLOCK] + both[:, BLOCK:])
        size *= 2
    for b in range(8):
        at = slice(b * BLOCK, (b + 1) * BLOCK)
        hi_ref[at, at], lo_ref[at, at] = split(inverses[b])
    while size < SIDE:
        for start in range(0, SIDE, 2 * size):
            first, second = slice(start, start + size), slice(start + size, start + 2 * size)
            corner = low_ref[second, first]
            t_hi, t_lo = split(dot(corner, hi_ref[first, first]) + dot(corner, lo_ref[first, first]))
            hi, lo = hi_ref[second, second], lo_ref[second, second]
            hi_ref[second, first], lo_ref[second, first] = split(
                -(dot(hi, t_hi) + dot(hi, t_lo) + dot(lo, t_hi))
            )
        size *= 2
    tile = 256
    for n in range(0, SIDE, tile):
        columns = slice(n, n + tile)
        wide_ref[:, columns] = dot(coupling_ref[:, n:], hi_ref[n:, columns]).astype(BF16)
    mine = pl.ds(pl.multiple_of(core * ROWS, ROWS), ROWS)
    for n in range(0, SIDE, tile):
        columns = slice(n, n + tile)
        hi, lo = hi_ref[n:, columns], lo_ref[n:, columns]
        left = hi_ref[n:, mine]
        square_ref[:, columns] = dot_tn(left, hi) + dot_tn(left, lo) + dot_tn(lo_ref[n:, mine], hi)


def solve(mine, other, coupling):
    return pl.pallas_call(
        solve_kernel,
        out_shape=(
            jax.ShapeDtypeStruct((SIDE, SIDE), BF16),
            jax.ShapeDtypeStruct((ROWS, SIDE), F32),
        ),
        in_specs=[VMEM, VMEM, VMEM],
        out_specs=(VMEM, VMEM),
        scratch_shapes=[pltpu.VMEM((SIDE, SIDE), BF16)] * 3,
        compiler_params=params(20),
        cost_estimate=cost(4 << 30, 8 << 20),
        name="solve",
    )(mine, other, coupling)


def turn_kernel(list_ref, mine_ref, other_ref, out_ref):
    core, group = lax.axis_index("panel"), lax.axis_index("front")
    out_ref[...] = jnp.zeros_like(out_ref)
    for a in range(NABOVE):
        owner, at = a // HALF, (a % HALF) * BLOCK
        row = list_ref[a, group] - core * HALF
        columns = pl.ds(pl.multiple_of(jnp.clip(row, 0, HALF - 1) * BLOCK, BLOCK), BLOCK)
        wanted = (row >= 0) & (row < HALF) & (list_ref[a, group] >= 0)

        @pl.when(wanted & (core == owner))
        def _():
            out_ref[:, columns] = mine_ref[at : at + BLOCK, :].astype(F32).T.astype(BF16)

        @pl.when(wanted & (core != owner))
        def _():
            out_ref[:, columns] = other_ref[at : at + BLOCK, :].astype(F32).T.astype(BF16)


def turn_wide(lists, mine, other):
    return pl.pallas_call(
        turn_kernel,
        out_shape=jax.ShapeDtypeStruct((SIDE, SIDE), BF16),
        in_specs=[SMEM, VMEM, VMEM],
        out_specs=VMEM,
        compiler_params=params(12),
        cost_estimate=cost(0, 8 << 20),
        name="turn_wide",
    )(lists, mine, other)


def carry_kernel(
    list_ref, places_ref, strips_ref, mine_ref, other_ref, turned_ref, carried_ref, send_ref, sigma_ref, column_ref
):
    core, group = lax.axis_index("panel"), lax.axis_index("front")
    first, second = jnp.where(core == 0, 1, 3), jnp.where(core == 0, 3, 1)

    def base(g, step):
        return jnp.where(step == 1, g & 0b101010, g ^ (3 * ((g >> 1) & 0b010101)))

    for block in range(NABOVE):
        column_ref[block] = NABOVE * BLOCK
    for a in range(NABOVE):
        block = list_ref[a, group]
        column = pl.multiple_of((a ^ (core * HALF)) * BLOCK, BLOCK)

        @pl.when(block >= 0)
        def _():
            column_ref[block] = column

        @pl.when(block < 0)
        def _():
            sigma_ref[:, pl.ds(column, BLOCK)] = jnp.zeros((SIDE, BLOCK), BF16)

    @pl.loop(0, 64)
    def _(n):
        middle = base(group, second) ^ spread(n >> 3, second)
        source = base(middle, first) ^ spread(n & 7, first)
        for row in range(HALF):
            place = places_ref[row, source]
            to = pl.multiple_of(row * BLOCK + (place & 3) * STRIP, STRIP)
            across = pl.multiple_of(column_ref[place >> 2], BLOCK)
            at = pl.multiple_of(n * HALF * STRIP + row * STRIP, STRIP)
            sigma_ref[pl.ds(to, STRIP), pl.ds(across, BLOCK)] = strips_ref[pl.ds(at, STRIP), :]

    tile = 256
    for n in range(0, SIDE, tile):
        columns = slice(n, n + tile)
        carried_ref[:, columns] = (
            dot(sigma_ref[:, :SIDE], mine_ref[:, columns])
            + dot(sigma_ref[:, SIDE : 2 * SIDE], other_ref[:, columns])
        ).astype(BF16)
    theirs = pl.ds(pl.multiple_of((1 - core) * ROWS, ROWS), ROWS)
    for n in range(0, SIDE, tile):
        columns = slice(n, n + tile)
        send_ref[:, columns] = dot(turned_ref[theirs, :], carried_ref[:, columns]).astype(BF16)


def carry(lists, places, strips, mine, other, turned):
    return pl.pallas_call(
        carry_kernel,
        out_shape=(
            jax.ShapeDtypeStruct((SIDE, SIDE), BF16),
            jax.ShapeDtypeStruct((ROWS, SIDE), BF16),
        ),
        in_specs=[SMEM, SMEM, VMEM, VMEM, VMEM, VMEM],
        out_specs=(VMEM, VMEM),
        scratch_shapes=[
            pltpu.VMEM((SIDE, (NABOVE + 1) * BLOCK), BF16),
            pltpu.SMEM((NABOVE,), jnp.int32),
        ],
        compiler_params=params(24),
        cost_estimate=cost(5 << 29, 12 << 20),
        name="carry",
    )(lists, places, strips, mine, other, turned)


def own_kernel(turned_ref, carried_ref, square_ref, out_ref):
    mine = pl.ds(pl.multiple_of(lax.axis_index("panel") * ROWS, ROWS), ROWS)
    tile = 256
    for n in range(0, SIDE, tile):
        columns = slice(n, n + tile)
        out_ref[:, columns] = square_ref[:, columns] + dot(turned_ref[mine, :], carried_ref[:, columns])


def own_product(turned, carried, square):
    return pl.pallas_call(
        own_kernel,
        out_shape=jax.ShapeDtypeStruct((ROWS, SIDE), F32),
        in_specs=[VMEM, VMEM, VMEM],
        out_specs=VMEM,
        compiler_params=params(12),
        cost_estimate=cost(1 << 29, 8 << 20),
        name="own_product",
    )(turned, carried, square)


def finish_kernel(own_ref, received_ref, out_ref, diag_ref):
    out_ref[...] = own_ref[...] + received_ref[...].astype(F32)
    at = lax.axis_index("panel") * ROWS + pl.program_id(0) * BLOCK
    block = out_ref[:, pl.ds(pl.multiple_of(at, BLOCK), BLOCK)]
    row = lax.broadcasted_iota(jnp.int32, (BLOCK, BLOCK), 0)
    col = lax.broadcasted_iota(jnp.int32, (BLOCK, BLOCK), 1)
    diag_ref[...] = jnp.sum(jnp.where(row == col, block, 0.0), axis=0, keepdims=True)


def finish(own, received):
    rows = pl.BlockSpec((BLOCK, SIDE), lambda t: (t, 0))
    return pl.pallas_call(
        finish_kernel,
        grid=(ROWS // BLOCK,),
        out_shape=(
            jax.ShapeDtypeStruct((ROWS, SIDE), F32),
            jax.ShapeDtypeStruct((1, ROWS), F32),
        ),
        in_specs=[rows, rows],
        out_specs=(rows, pl.BlockSpec((1, BLOCK), lambda t: (0, t))),
        compiler_params=params(6),
        cost_estimate=cost(0, 6 << 20),
        name="finish",
    )(own, received)


def swap(x):
    return lax.ppermute(x, "panel", [(0, 1), (1, 0)])


def on_device(sep_factor, coup_factor, coup_list, slot_tiles, anc_tiles):
    lists, slots = coup_list.T, slot_tiles.T
    sep_other = swap(sep_factor)
    picked, places = pick_strips(slots, anc_tiles)
    near = gather_cube(picked, 0)
    strips = gather_cube(jnp.broadcast_to(near[None], (8,) + near.shape).reshape(-1, BLOCK), 1)
    wide_mine, square = solve(sep_factor, sep_other, coup_factor)
    wide_other = swap(wide_mine)
    turned = turn_wide(lists, wide_mine, wide_other)
    carried, to_send = carry(lists, places, strips, wide_mine, wide_other, turned)
    received = swap(to_send)
    own = own_product(turned, carried, square)
    selected, variances = finish(own, received)
    return selected, variances.reshape(ROWS)


def solution(mesh):
    placed = (P(AXES, None), P(AXES, None), P(), P(), P("front", None))
    return jax.shard_map(
        on_device,
        mesh=mesh,
        in_specs=placed,
        out_specs=(P(AXES, None), P(AXES)),
        check_vma=False,
    )
```

time: 93.4 us -> 82.2 us (0.88)
  Pallas kernels: 50.2 us -> 29 us
  blocking collectives: 20.6 us -> 0 us
  waiting for transfers between devices: 5.96 us -> 25.2 us
  starting transfers between devices: 6.05 us -> 15.4 us
  local copies, waits for them, and re-layouts: 8.82 us -> 11.4 us
    all_to_all x1 -> x0, blocking collectives: 20.6 us -> none  [gather_cube(): lax.all_to_all(parts, AXES, split_axis=0, concat_axis=0, tiled=True, axis...]
    all_to_all x1 -> x2, waiting for transfers between devices: 3.23 us -> 19.6 us  [gather_cube(): lax.all_to_all(parts, AXES, split_axis=0, concat_axis=0, tiled=True, axis...]
    pallas_call x6 -> x4, Pallas kernels: 30.2 us -> 15.4 us  [the longest x1 10.2 us: solve(): pl.pallas_call(solve_kernel, out_shape=(jax.ShapeDtypeStruct((SIDE, SIDE)...]
    all_to_all x1 -> x2, starting transfers between devices: 4.54 us -> 15.3 us  [gather_cube(): lax.all_to_all(parts, AXES, split_axis=0, concat_axis=0, tiled=True, axis...]
    pallas_call x1, Pallas kernels: 6.13 us -> 1.27 us  [own_product(): pl.pallas_call(own_kernel, out_shape=jax.ShapeDtypeStruct((ROWS, SIDE), F...]
    unnamed x12 -> x22, local copies, waits for them, and re-layouts: 4.22 us -> 8.82 us
    ppermute x3, waiting for transfers between devices: 2.73 us -> 5.52 us  [swap(): return lax.ppermute(x, 'panel', [(0, 1), (1, 0)])]
    reshape x3 -> x0, local copies, waits for them, and re-layouts: 2.01 us -> none  [the longest x1 0.67 us: on_device(): lists = coup_list.reshape(-1)]
  transfers between devices with their start and end apart: 4 -> 5, of which waited for: 2 -> 4; matrix products, arithmetic and copies ran while one was open for 7% -> 3% of each run, Pallas kernels for 35% -> 16%
where the time goes in v1:
time: 82.2 us; the launch traced here: 81.7 us
  Pallas kernels  29 us (35%)
  waiting for transfers between devices  25.2 us (31%)
  starting transfers between devices  15.4 us (19%)
  local copies, waits for them, and re-layouts  11.4 us (14%)
    all_to_all x2, waiting for transfers between devices, gather_cube(): lax.all_to_all(parts, AXES, split_axis=0, concat_axis=0, tiled=True, axis...  19.6 us
    all_to_all x2, starting transfers between devices, gather_cube(): lax.all_to_all(parts, AXES, split_axis=0, concat_axis=0, tiled=True, axis...  15.3 us
    pallas_call x1, Pallas kernels, carry(): pl.pallas_call(carry_kernel, out_shape=(jax.ShapeDtypeStruct((SIDE, SIDE)...  12.3 us
    pallas_call x1, Pallas kernels, solve(): pl.pallas_call(solve_kernel, out_shape=(jax.ShapeDtypeStruct((SIDE, SIDE)...  10.2 us
    unnamed x22, local copies, waits for them, and re-layouts  8.82 us
    ppermute x3, waiting for transfers between devices, swap(): return lax.ppermute(x, 'panel', [(0, 1), (1, 0)])  5.52 us
    broadcast_in_dim x1, local copies, waits for them, and re-layouts, on_device(): jnp.broadcast_to(near[None], (8,) + near.shape).reshape(-1, BLOCK)  2.53 us
    pallas_call x1, Pallas kernels, finish(): pl.pallas_call(finish_kernel, grid=(ROWS // BLOCK,), out_shape=(jax.Shape...  1.89 us
  transfers between devices with their start and end apart: 5, of which 4 were waited for; matrix products, arithmetic and copies ran while one was open for 3% of the time, Pallas kernels for 16%

profile of v1, /device:TPU:1, one launch (start us, length us, event | category | flops | bytes accessed | tf_op | source)
XLA Modules:
  0.0 81.7 jit_solution(16154848053087450088)
XLA Ops:
  0.6 0.0 copy-start.6
  0.6 0.9 %copy-done.6 = bf16[512,128]{1,0:T(8,128)(2,1)S(1)} copy-done((bf16[512,128]{1,0:T(8,128)(2,1)S(1)}, bf16[512,128]{1,0:T(8,128)(2,1)}, u32[]{:S(2)}) %copy-start.6) | copy-done | bytes 131096
  1.5 0.0 copy-start.7
  1.5 0.7 copy-done.7
  2.2 1.8 %pick_strips.1 = (bf16[2048,128]{1,0:T(8,128)(2,1)}, s32[8,64]{1,0:T(8,128)S(1)}) custom-call(s32[16,64]{1,0:T(8,128)S(1)} %bitcast.6, s32[16,64]{1,0:T(8,128)S(1)} %bitcast.7, bf16[512,128]{1,0:T(8,128)(2,1)S(1)} %copy-done.6), custom_call_target="tpu_custom_call" | custom-call | bytes 1048576 | tf_op jit(solution)/shard_map/pick_strips/pallas_call | solution.py:93
  4.0 10.5 %all-to-all-start = ((bf16[8,256,128]{2,1,0:T(8,128)(2,1)}), bf16[8,256,128]{2,1,0:T(8,128)(2,1)S(1)}, u32[]{:S(2)}, u32[]{:S(2)}) async-start(bf16[8,256,128]{2,1,0:T(8,128)(2,1)} %bitcast.2), calls=%async_computation | async-start | bytes 1048576 | tf_op jit(solution)/shard_map/all_to_all | solution.py:69
  14.6 0.0 collective-permute-start
  14.6 10.8 %all-to-all-done = bf16[8,256,128]{2,1,0:T(8,128)(2,1)S(1)} async-done(((bf16[8,256,128]{2,1,0:T(8,128)(2,1)}), bf16[8,256,128]{2,1,0:T(8,128)(2,1)S(1)}, u32[]{:S(2)}, u32[]{:S(2)}) %all-to-all-start) | async-done | bytes 524320 | tf_op jit(solution)/shard_map/all_to_all | solution.py:69
  25.4 2.5 %broadcast_in_dim.9 = bf16[8,2048,128]{2,1,0:T(8,128)(2,1)} broadcast(bf16[2048,128]{1,0:T(8,128)(2,1)S(1)} %bitcast.10), dimensions={1,2} | broadcast | bytes 4718592 | tf_op jit(solution)/shard_map/broadcast_in_dim | solution.py:337
  27.9 0.0 copy-start.9
  28.0 0.0 copy-start.10
  28.0 4.8 %all-to-all-start.1 = ((bf16[8,2048,128]{2,1,0:T(8,128)(2,1)}), bf16[8,2048,128]{2,1,0:T(8,128)(2,1)}, u32[]{:S(2)}, u32[]{:S(2)}) async-start(bf16[8,2048,128]{2,1,0:T(8,128)(2,1)} %broadcast_in_dim.9), calls=%async_computation.1 | async-start | bytes 8388608 | tf_op jit(solution)/shard_map/all_to_all | solution.py:69
  32.8 0.0 copy-start.8
  32.8 0.0 collective-permute-done.other_ref
  32.8 0.0 copy-done.9
  32.8 0.0 copy-done.10
  32.8 10.2 %solve.1 = (bf16[1024,1024]{1,0:T(8,128)(2,1)S(1)}, f32[512,1024]{1,0:T(8,128)S(1)}) custom-call(bf16[512,1024]{1,0:T(8,128)(2,1)S(1)} %copy-done.10, bf16[512,1024]{1,0:T(8,128)(2,1)} %collective-permute-done.other_ref, bf16[1024,1024]{1,0:T(8,128)(2,1)S(1)} %copy-done.9), custom_call_target="tpu_custom_call" | custom-call | flops 8589934592 | bytes 8388608 | tf_op jit(solution)/shard_map/solve/pallas_call | solution.py:171
  43.0 0.0 copy-start.4
  43.0 1.4 %copy-done.4 = f32[512,1024]{1,0:T(8,128)} copy-done((f32[512,1024]{1,0:T(8,128)}, f32[512,1024]{1,0:T(8,128)S(1)}, u32[]{:S(2)}) %copy-start.4) | copy-done | bytes 2097176
  44.4 0.0 collective-permute-start.1
  44.4 4.2 %collective-permute-done.1.other_ref = bf16[1024,1024]{1,0:T(8,128)(2,1)S(1)} collective-permute-done((bf16[1024,1024]{1,0:T(8,128)(2,1)S(1)}, bf16[1024,1024]{1,0:T(8,128)(2,1)S(1)}, u32[]{:S(2)}, u32[]{:S(2)}) %collective-permute-start.1) | collective-permute-done | bytes 2097184 | tf_op jit(solution)/shard_map/ppermute | solution.py:329
  48.5 0.0 copy-done.8
  48.5 1.6 %turn_wide.1.turned_ref = bf16[1024,1024]{1,0:T(8,128)(2,1)S(1)} custom-call(s32[16,64]{1,0:T(8,128)S(1)} %bitcast.8, bf16[1024,1024]{1,0:T(8,128)(2,1)S(1)} %get-tuple-element.10.mine_ref, bf16[1024,1024]{1,0:T(8,128)(2,1)S(1)} %collective-permute-done.1.other_ref), custom_call_target="tpu_custom_call" | custom-call | bytes 8388608 | tf_op jit(solution)/shard_map/turn_wide/pallas_call | solution.py:205
  50.1 0.0 copy-start
  50.1 1.3 %copy-done = bf16[1024,1024]{1,0:T(8,128)(2,1)} copy-done((bf16[1024,1024]{1,0:T(8,128)(2,1)}, bf16[1024,1024]{1,0:T(8,128)(2,1)S(1)}, u32[]{:S(2)}) %copy-start) | copy-done | bytes 2097176
  51.4 0.0 copy-start.2
  51.4 1.3 %copy-done.2 = bf16[1024,1024]{1,0:T(8,128)(2,1)} copy-done((bf16[1024,1024]{1,0:T(8,128)(2,1)}, bf16[1024,1024]{1,0:T(8,128)(2,1)S(1)}, u32[]{:S(2)}) %copy-start.2) | copy-done | bytes 2097176
  52.8 8.8 %all-to-all-done.1 = bf16[8,2048,128]{2,1,0:T(8,128)(2,1)} async-done(((bf16[8,2048,128]{2,1,0:T(8,128)(2,1)}), bf16[8,2048,128]{2,1,0:T(8,128)(2,1)}, u32[]{:S(2)}, u32[]{:S(2)}) %all-to-all-start.1) | async-done | bytes 4194336 | tf_op jit(solution)/shard_map/all_to_all | solution.py:69
  61.6 0.0 copy-start.1
  61.6 1.6 %copy-done.1 = bf16[1024,1024]{1,0:T(8,128)(2,1)S(1)} copy-done((bf16[1024,1024]{1,0:T(8,128)(2,1)S(1)}, bf16[1024,1024]{1,0:T(8,128)(2,1)}, u32[]{:S(2)}) %copy-start.1) | copy-done | bytes 2097176
  63.2 0.0 copy-start.3
  63.2 1.6 %copy-done.3 = bf16[1024,1024]{1,0:T(8,128)(2,1)S(1)} copy-done((bf16[1024,1024]{1,0:T(8,128)(2,1)S(1)}, bf16[1024,1024]{1,0:T(8,128)(2,1)}, u32[]{:S(2)}) %copy-start.3) | copy-done | bytes 2097176
  64.7 0.0 copy-start.5
  64.7 12.3 %carry.1 = (bf16[1024,1024]{1,0:T(8,128)(2,1)S(1)}, bf16[512,1024]{1,0:T(8,128)(2,1)S(1)}) custom-call(s32[16,64]{1,0:T(8,128)S(1)} %bitcast.9, s32[8,64]{1,0:T(8,128)S(1)} %get-tuple-element.11.places_ref, bf16[16384,128]{1,0:T(8,128)(2,1)} %bitcast.4.strips_ref, bf16[1024,1024]{1,0:T(8,128)(2,1)S(1)} %copy-done.1, bf16[1024,1024]{1,0:T(8,128)(2,1)S(1)} %copy-done.3, ...), custom_call_target="tpu_custom_call" | custom-call | flops 5368709120 | bytes 12582912 | tf_op jit(solution)/shard_map/carry/pallas_call | solution.py:264
  77.1 0.1 collective-permute-start.2
  77.2 0.0 copy-done.5
  77.2 1.3 %own_product.1.own_ref = f32[512,1024]{1,0:T(8,128)S(1)} custom-call(bf16[1024,1024]{1,0:T(8,128)(2,1)S(1)} %turn_wide.1.turned_ref, bf16[1024,1024]{1,0:T(8,128)(2,1)S(1)} %get-tuple-element.13.carried_ref, f32[512,1024]{1,0:T(8,128)S(1)} %copy-done.5), custom_call_target="tpu_custom_call" | custom-call | flops 1073741824 | bytes 8388608 | tf_op jit(solution)/shard_map/own_product/pallas_call | solution.py:291
  78.5 1.4 %collective-permute-done.2.received_ref = bf16[512,1024]{1,0:T(8,128)(2,1)S(1)} collective-permute-done((bf16[512,1024]{1,0:T(8,128)(2,1)S(1)}, bf16[512,1024]{1,0:T(8,128)(2,1)S(1)}, u32[]{:S(2)}, u32[]{:S(2)}) %collective-permute-start.2) | collective-permute-done | bytes 1048608 | tf_op jit(solution)/shard_map/ppermute | solution.py:329
  79.8 1.9 %finish.1 = (f32[512,1024]{1,0:T(8,128)}, f32[1,512]{1,0:T(1,128)}) custom-call(f32[512,1024]{1,0:T(8,128)S(1)} %own_product.1.own_ref, bf16[512,1024]{1,0:T(8,128)(2,1)S(1)} %collective-permute-done.2.received_ref), custom_call_target="tpu_custom_call" | custom-call | bytes 6291456 | tf_op jit(solution)/shard_map/finish/pallas_call | solution.py:313
Async XLA Ops:
  0.6 0.9 %copy-start.6 = (bf16[512,128]{1,0:T(8,128)(2,1)S(1)}, bf16[512,128]{1,0:T(8,128)(2,1)}, u32[]{:S(2)}) copy-start(bf16[512,128]{1,0:T(8,128)(2,1)} %strips_ref.1) | copy-start | bytes 393220
  1.5 0.7 copy-start.7
  4.0 21.4 %all-to-all-start = ((bf16[8,256,128]{2,1,0:T(8,128)(2,1)}), bf16[8,256,128]{2,1,0:T(8,128)(2,1)S(1)}, u32[]{:S(2)}, u32[]{:S(2)}) async-start(bf16[8,256,128]{2,1,0:T(8,128)(2,1)} %bitcast.2), calls=%async_computation | async-start | bytes 1048576 | tf_op jit(solution)/shard_map/all_to_all | solution.py:69
  14.6 18.2 %collective-permute-start = (bf16[512,1024]{1,0:T(8,128)(2,1)}, bf16[512,1024]{1,0:T(8,128)(2,1)}, u32[]{:S(2)}, u32[]{:S(2)}) collective-permute-start(bf16[512,1024]{1,0:T(8,128)(2,1)} %mine_ref.1), channel_id=1, source_target_pairs={{0,1},{1,0},{2,3},{3,2},{4,5},{5,4},{6,7},{7,6},{8,9},{9,8},{10,11... | collective-permute-start | bytes 3145736 | tf_op jit(solution)/shard_map/ppermute | solution.py:329
  27.9 4.9 %copy-start.9 = (bf16[1024,1024]{1,0:T(8,128)(2,1)S(1)}, bf16[1024,1024]{1,0:T(8,128)(2,1)}, u32[]{:S(2)}) copy-start(bf16[1024,1024]{1,0:T(8,128)(2,1)} %coupling_ref.1) | copy-start | bytes 6291460
  28.0 4.9 %copy-start.10 = (bf16[512,1024]{1,0:T(8,128)(2,1)S(1)}, bf16[512,1024]{1,0:T(8,128)(2,1)}, u32[]{:S(2)}) copy-start(bf16[512,1024]{1,0:T(8,128)(2,1)} %mine_ref.1) | copy-start | bytes 3145732
  28.0 33.6 %all-to-all-start.1 = ((bf16[8,2048,128]{2,1,0:T(8,128)(2,1)}), bf16[8,2048,128]{2,1,0:T(8,128)(2,1)}, u32[]{:S(2)}, u32[]{:S(2)}) async-start(bf16[8,2048,128]{2,1,0:T(8,128)(2,1)} %broadcast_in_dim.9), calls=%async_computation.1 | async-start | bytes 8388608 | tf_op jit(solution)/shard_map/all_to_all | solution.py:69
  32.8 15.8 %copy-start.8 = (s32[64,16]{0,1:T(8,128)S(1)}, s32[64,16]{0,1:T(8,128)}, u32[]{:S(2)}) copy-start(s32[64,16]{0,1:T(8,128)} %param.7) | copy-start | bytes 12292
  43.0 1.4 %copy-start.4 = (f32[512,1024]{1,0:T(8,128)}, f32[512,1024]{1,0:T(8,128)S(1)}, u32[]{:S(2)}) copy-start(f32[512,1024]{1,0:T(8,128)S(1)} %get-tuple-element.14.square_ref) | copy-start | bytes 6291460
  44.4 4.2 %collective-permute-start.1 = (bf16[1024,1024]{1,0:T(8,128)(2,1)S(1)}, bf16[1024,1024]{1,0:T(8,128)(2,1)S(1)}, u32[]{:S(2)}, u32[]{:S(2)}) collective-permute-start(bf16[1024,1024]{1,0:T(8,128)(2,1)S(1)} %get-tuple-element.10.mine_ref), channel_id=1, source_target_pairs={{0,1},{1,0},{2,3},{3,2},{4,5},{5,4},{6,7},{7,6},{8,9},{9,8},{10,11... | collective-permute-start | bytes 6291464 | tf_op jit(solution)/shard_map/ppermute | solution.py:329
  50.1 1.3 %copy-start = (bf16[1024,1024]{1,0:T(8,128)(2,1)}, bf16[1024,1024]{1,0:T(8,128)(2,1)S(1)}, u32[]{:S(2)}) copy-start(bf16[1024,1024]{1,0:T(8,128)(2,1)S(1)} %get-tuple-element.10.mine_ref) | copy-start | bytes 6291460
  51.4 1.3 %copy-start.2 = (bf16[1024,1024]{1,0:T(8,128)(2,1)}, bf16[1024,1024]{1,0:T(8,128)(2,1)S(1)}, u32[]{:S(2)}) copy-start(bf16[1024,1024]{1,0:T(8,128)(2,1)S(1)} %collective-permute-done.1.other_ref) | copy-start | bytes 6291460
  61.6 1.6 %copy-start.1 = (bf16[1024,1024]{1,0:T(8,128)(2,1)S(1)}, bf16[1024,1024]{1,0:T(8,128)(2,1)}, u32[]{:S(2)}) copy-start(bf16[1024,1024]{1,0:T(8,128)(2,1)} %copy-done) | copy-start | bytes 6291460
  63.2 1.6 %copy-start.3 = (bf16[1024,1024]{1,0:T(8,128)(2,1)S(1)}, bf16[1024,1024]{1,0:T(8,128)(2,1)}, u32[]{:S(2)}) copy-start(bf16[1024,1024]{1,0:T(8,128)(2,1)} %copy-done.2) | copy-start | bytes 6291460
  64.7 12.4 %copy-start.5 = (f32[512,1024]{1,0:T(8,128)S(1)}, f32[512,1024]{1,0:T(8,128)}, u32[]{:S(2)}) copy-start(f32[512,1024]{1,0:T(8,128)} %copy-done.4) | copy-start | bytes 6291460
  77.1 2.7 %collective-permute-start.2 = (bf16[512,1024]{1,0:T(8,128)(2,1)S(1)}, bf16[512,1024]{1,0:T(8,128)(2,1)S(1)}, u32[]{:S(2)}, u32[]{:S(2)}) collective-permute-start(bf16[512,1024]{1,0:T(8,128)(2,1)S(1)} %get-tuple-element.15), channel_id=1, source_target_pairs={{0,1},{1,0},{2,3},{3,2},{4,5},{5,4},{6,7},{7,6},{8,9},{9,8},{10,11... | collective-permute-start | bytes 3145736 | tf_op jit(solution)/shard_map/ppermute | solution.py:329

commit v2 on v1

--- a/solution.py
+++ b/solution.py
@@ -16,6 +16,7 @@
 F32 = jnp.float32
 BF16 = jnp.bfloat16
 VMEM = pl.BlockSpec(memory_space=pltpu.VMEM)
+ANY = pl.BlockSpec(memory_space=pl.ANY)
 SMEM = pl.BlockSpec(memory_space=pltpu.SMEM)
 MIB = 1024 * 1024
 
@@ -69,6 +70,15 @@
     return lax.all_to_all(
         parts, AXES, split_axis=0, concat_axis=0, tiled=True, axis_index_groups=cubes(phase)
     )
+
+
+def across(x, bits):
+    pairs = []
+    for group in range(64):
+        for core in range(2):
+            step = steps_of(core)[1]
+            pairs.append((group * 2 + core, (group ^ spread(bits, step)) * 2 + core))
+    return lax.ppermute(x, AXES, pairs)
 
 
 def pick_kernel(slots_ref, table_ref, strips_ref, out_ref, places_ref):
@@ -104,7 +114,7 @@
     )(slots, slots, strips)
 
 
-def solve_kernel(mine_ref, other_ref, coupling_ref, wide_ref, square_ref, low_ref, hi_ref, lo_ref):
+def invert_kernel(mine_ref, other_ref, after_ref, hi_ref, lo_ref, low_ref):
     core = lax.axis_index("panel")
     low_ref[pl.ds(pl.multiple_of(core * ROWS, ROWS), ROWS), :] = mine_ref[...]
     low_ref[pl.ds(pl.multiple_of((1 - core) * ROWS, ROWS), ROWS), :] = other_ref[...]
@@ -155,11 +165,44 @@
                 -(dot(hi, t_hi) + dot(hi, t_lo) + dot(lo, t_hi))
             )
         size *= 2
+
+
+def invert(mine, other, after):
+    full = jax.ShapeDtypeStruct((SIDE, SIDE), BF16)
+    return pl.pallas_call(
+        invert_kernel,
+        out_shape=(full, full),
+        in_specs=[VMEM, VMEM, ANY],
+        out_specs=(VMEM, VMEM),
+        scratch_shapes=[pltpu.VMEM((SIDE, SIDE), BF16)],
+        compiler_params=params(12),
+        cost_estimate=cost(1 << 20, 1 << 16),
+        name="invert",
+    )(mine, other, after)
+
+
+def wide_kernel(coupling_ref, hi_ref, x_ref, y_ref, z_ref, wide_ref):
     tile = 256
     for n in range(0, SIDE, tile):
         columns = slice(n, n + tile)
         wide_ref[:, columns] = dot(coupling_ref[:, n:], hi_ref[n:, columns]).astype(BF16)
-    mine = pl.ds(pl.multiple_of(core * ROWS, ROWS), ROWS)
+
+
+def make_wide(coupling, hi, after):
+    return pl.pallas_call(
+        wide_kernel,
+        out_shape=jax.ShapeDtypeStruct((SIDE, SIDE), BF16),
+        in_specs=[VMEM, VMEM, ANY, ANY, ANY],
+        out_specs=VMEM,
+        compiler_params=params(10),
+        cost_estimate=cost(1 << 20, 1 << 16),
+        name="make_wide",
+    )(coupling, hi, *after)
+
+
+def square_kernel(hi_ref, lo_ref, x_ref, y_ref, z_ref, square_ref):
+    mine = pl.ds(pl.multiple_of(lax.axis_index("panel") * ROWS, ROWS), ROWS)
+    tile = 256
     for n in range(0, SIDE, tile):
         columns = slice(n, n + tile)
         hi, lo = hi_ref[n:, columns], lo_ref[n:, columns]
@@ -167,24 +210,26 @@
         square_ref[:, columns] = dot_tn(left, hi) + dot_tn(left, lo) + dot_tn(lo_ref[n:, mine], hi)
 
 
-def solve(mine, other, coupling):
-    return pl.pallas_call(
-        solve_kernel,
-        out_shape=(
-            jax.ShapeDtypeStruct((SIDE, SIDE), BF16),
-            jax.ShapeDtypeStruct((ROWS, SIDE), F32),
-        ),
-        in_specs=[VMEM, VMEM, VMEM],
-        out_specs=(VMEM, VMEM),
-        scratch_shapes=[pltpu.VMEM((SIDE, SIDE), BF16)] * 3,
-        compiler_params=params(20),
-        cost_estimate=cost(4 << 30, 8 << 20),
-        name="solve",
-    )(mine, other, coupling)
-
-
-def turn_kernel(list_ref, mine_ref, other_ref, out_ref):
+def make_square(hi, lo, after):
+    return pl.pallas_call(
+        square_kernel,
+        out_shape=jax.ShapeDtypeStruct((ROWS, SIDE), F32),
+        in_specs=[VMEM, VMEM, ANY, ANY, ANY],
+        out_specs=VMEM,
+        compiler_params=params(10),
+        cost_estimate=cost(1 << 20, 1 << 16),
+        name="make_square",
+    )(hi, lo, *after)
+
+
+def turn_kernel(list_ref, places_ref, mine_ref, other_ref, x_ref, y_ref, z_ref, square_ref, out_ref, table_ref):
     core, group = lax.axis_index("panel"), lax.axis_index("front")
+    places = places_ref[...]
+    column = jnp.full(places.shape, NABOVE, jnp.int32)
+    for a in range(NABOVE):
+        column = jnp.where((places >> 2) == list_ref[a, group], a ^ (core * HALF), column)
+    row = lax.broadcasted_iota(jnp.int32, places.shape, 0)
+    table_ref[...] = column * SIDE + row * BLOCK + (places & 3) * STRIP
     out_ref[...] = jnp.zeros_like(out_ref)
     for a in range(NABOVE):
         owner, at = a // HALF, (a % HALF) * BLOCK
@@ -201,58 +246,54 @@
             out_ref[:, columns] = other_ref[at : at + BLOCK, :].astype(F32).T.astype(BF16)
 
 
-def turn_wide(lists, mine, other):
+def turn_wide(lists, places, mine, other, after):
     return pl.pallas_call(
         turn_kernel,
-        out_shape=jax.ShapeDtypeStruct((SIDE, SIDE), BF16),
-        in_specs=[SMEM, VMEM, VMEM],
-        out_specs=VMEM,
+        out_shape=(
+            jax.ShapeDtypeStruct((SIDE, SIDE), BF16),
+            jax.ShapeDtypeStruct((HALF, 64), jnp.int32),
+        ),
+        in_specs=[SMEM, VMEM, VMEM, VMEM, ANY, ANY, ANY, ANY],
+        out_specs=(VMEM, VMEM),
         compiler_params=params(12),
-        cost_estimate=cost(0, 8 << 20),
+        cost_estimate=cost(1 << 20, 1 << 16),
         name="turn_wide",
-    )(lists, mine, other)
-
-
-def carry_kernel(
-    list_ref, places_ref, strips_ref, mine_ref, other_ref, turned_ref, carried_ref, send_ref, sigma_ref, column_ref
-):
+    )(lists, places, mine, other, *after)
+
+
+def carry_kernel(list_ref, table_ref, *refs):
+    strips_refs, refs = refs[:8], refs[8:]
+    mine_ref, other_ref, turned_ref, carried_ref, send_ref, sigma_ref = refs
     core, group = lax.axis_index("panel"), lax.axis_index("front")
     first, second = jnp.where(core == 0, 1, 3), jnp.where(core == 0, 3, 1)
-
-    def base(g, step):
-        return jnp.where(step == 1, g & 0b101010, g ^ (3 * ((g >> 1) & 0b010101)))
-
-    for block in range(NABOVE):
-        column_ref[block] = NABOVE * BLOCK
     for a in range(NABOVE):
-        block = list_ref[a, group]
-        column = pl.multiple_of((a ^ (core * HALF)) * BLOCK, BLOCK)
-
-        @pl.when(block >= 0)
+        column = pl.multiple_of((a ^ (core * HALF)) * SIDE, SIDE)
+
+        @pl.when(list_ref[a, group] < 0)
         def _():
-            column_ref[block] = column
-
-        @pl.when(block < 0)
-        def _():
-            sigma_ref[:, pl.ds(column, BLOCK)] = jnp.zeros((SIDE, BLOCK), BF16)
-
-    @pl.loop(0, 64)
-    def _(n):
-        middle = base(group, second) ^ spread(n >> 3, second)
-        source = base(middle, first) ^ spread(n & 7, first)
-        for row in range(HALF):
-            place = places_ref[row, source]
-            to = pl.multiple_of(row * BLOCK + (place & 3) * STRIP, STRIP)
-            across = pl.multiple_of(column_ref[place >> 2], BLOCK)
-            at = pl.multiple_of(n * HALF * STRIP + row * STRIP, STRIP)
-            sigma_ref[pl.ds(to, STRIP), pl.ds(across, BLOCK)] = strips_ref[pl.ds(at, STRIP), :]
+            sigma_ref[pl.ds(column, SIDE), :] = jnp.zeros((SIDE, BLOCK), BF16)
+
+    for bits in range(8):
+        middle = group ^ spread(bits, second)
+        start = jnp.where(first == 1, middle & 0b101010, middle ^ (3 * ((middle >> 1) & 0b010101)))
+
+        @pl.loop(0, 8)
+        def _(n):
+            source = start ^ spread(n, first)
+            for row in range(HALF):
+                to = pl.multiple_of(table_ref[row, source], STRIP)
+                at = pl.multiple_of(n * HALF * STRIP + row * STRIP, STRIP)
+                sigma_ref[pl.ds(to, STRIP), :] = strips_refs[bits][pl.ds(at, STRIP), :]
+
+    def sigma(at):
+        blocks = [sigma_ref[c * SIDE : (c + 1) * SIDE, :] for c in range(at, at + HALF)]
+        return jnp.concatenate(blocks, axis=1)
 
     tile = 256
     for n in range(0, SIDE, tile):
         columns = slice(n, n + tile)
         carried_ref[:, columns] = (
-            dot(sigma_ref[:, :SIDE], mine_ref[:, columns])
-            + dot(sigma_ref[:, SIDE : 2 * SIDE], other_ref[:, columns])
+            dot(sigma(0), mine_ref[:, columns]) + dot(sigma(HALF), other_ref[:, columns])
         ).astype(BF16)
     theirs = pl.ds(pl.multiple_of((1 - core) * ROWS, ROWS), ROWS)
     for n in range(0, SIDE, tile):
@@ -260,23 +301,20 @@
         send_ref[:, columns] = dot(turned_ref[theirs, :], carried_ref[:, columns]).astype(BF16)
 
 
-def carry(lists, places, strips, mine, other, turned):
+def carry(lists, table, strips, mine, other, turned):
     return pl.pallas_call(
         carry_kernel,
         out_shape=(
             jax.ShapeDtypeStruct((SIDE, SIDE), BF16),
             jax.ShapeDtypeStruct((ROWS, SIDE), BF16),
         ),
-        in_specs=[SMEM, SMEM, VMEM, VMEM, VMEM, VMEM],
+        in_specs=[SMEM, SMEM] + [VMEM] * 11,
         out_specs=(VMEM, VMEM),
-        scratch_shapes=[
-            pltpu.VMEM((SIDE, (NABOVE + 1) * BLOCK), BF16),
-            pltpu.SMEM((NABOVE,), jnp.int32),
-        ],
+        scratch_shapes=[pltpu.VMEM(((NABOVE + 1) * SIDE, BLOCK), BF16)],
         compiler_params=params(24),
         cost_estimate=cost(5 << 29, 12 << 20),
         name="carry",
-    )(lists, places, strips, mine, other, turned)
+    )(lists, table, *strips, mine, other, turned)
 
 
 def own_kernel(turned_ref, carried_ref, square_ref, out_ref):
@@ -334,11 +372,15 @@
     sep_other = swap(sep_factor)
     picked, places = pick_strips(slots, anc_tiles)
     near = gather_cube(picked, 0)
-    strips = gather_cube(jnp.broadcast_to(near[None], (8,) + near.shape).reshape(-1, BLOCK), 1)
-    wide_mine, square = solve(sep_factor, sep_other, coup_factor)
+    hi, lo = invert(sep_factor, sep_other, near)
+    x, y, z = across(near, 1), across(near, 2), across(near, 4)
+    wide_mine = make_wide(coup_factor, hi, (x, y, z))
     wide_other = swap(wide_mine)
-    turned = turn_wide(lists, wide_mine, wide_other)
-    carried, to_send = carry(lists, places, strips, wide_mine, wide_other, turned)
+    xy, yz, zx = across(x, 2), across(y, 4), across(z, 1)
+    square = make_square(hi, lo, (x, y, z))
+    strips = [near, x, y, xy, z, zx, yz, across(xy, 4)]
+    turned, table = turn_wide(lists, places, wide_mine, wide_other, (xy, yz, zx, square))
+    carried, to_send = carry(lists, table, strips, wide_mine, wide_other, turned)
     received = swap(to_send)
     own = own_product(turned, carried, square)
     selected, variances = finish(own, received)

time: 82.2 us -> 69.4 us (0.84)
  blocking collectives: 0 us -> 20.5 us
  waiting for transfers between devices: 25.2 us -> 11.2 us
  local copies, waits for them, and re-layouts: 11.4 us -> 2.83 us
  Pallas kernels: 29 us -> 23.4 us
  starting transfers between devices: 15.4 us -> 10.7 us
    all_to_all x0 -> x1, blocking collectives: none -> 20.5 us  [gather_cube(): lax.all_to_all(parts, AXES, split_axis=0, concat_axis=0, tiled=True, axis...]
    all_to_all x2 -> x0, waiting for transfers between devices: 19.6 us -> none  [gather_cube(): lax.all_to_all(parts, AXES, split_axis=0, concat_axis=0, tiled=True, axis...]
    all_to_all x2 -> x0, starting transfers between devices: 15.3 us -> none  [gather_cube(): lax.all_to_all(parts, AXES, split_axis=0, concat_axis=0, tiled=True, axis...]
    ppermute x0 -> x7, waiting for transfers between devices: none -> 10.2 us  [across(): return lax.ppermute(x, AXES, pairs)]
    ppermute x3, starting transfers between devices: 0.09 us -> 6.3 us  [swap(): return lax.ppermute(x, 'panel', [(0, 1), (1, 0)])]
    unnamed x22 -> x10, local copies, waits for them, and re-layouts: 8.82 us -> 2.83 us
    ppermute x3, waiting for transfers between devices: 5.52 us -> 1.03 us  [swap(): return lax.ppermute(x, 'panel', [(0, 1), (1, 0)])]
    ppermute x0 -> x7, starting transfers between devices: none -> 4.4 us  [across(): return lax.ppermute(x, AXES, pairs)]
  transfers between devices with their start and end apart: 5 -> 10, of which waited for: 4 -> 4; matrix products, arithmetic and copies ran while one was open for 3% -> 0% of each run, Pallas kernels for 16% -> 16%
where the time goes in v2:
time: 69.4 us; the launch traced here: 69.3 us
  Pallas kernels  23.4 us (34%)
  blocking collectives  20.5 us (30%)
  waiting for transfers between devices  11.2 us (16%)
  starting transfers between devices  10.7 us (15%)
  local copies, waits for them, and re-layouts  2.83 us (4%)
  between operations  0.75 us (1%)
    all_to_all x1, blocking collectives, gather_cube(): lax.all_to_all(parts, AXES, split_axis=0, concat_axis=0, tiled=True, axis...  20.5 us
    ppermute x7, waiting for transfers between devices, across(): return lax.ppermute(x, AXES, pairs)  10.2 us
    pallas_call x1, Pallas kernels, carry(): pl.pallas_call(carry_kernel, out_shape=(jax.ShapeDtypeStruct((SIDE, SIDE)...  8.85 us
    ppermute x3, starting transfers between devices, swap(): return lax.ppermute(x, 'panel', [(0, 1), (1, 0)])  6.3 us
    pallas_call x1, Pallas kernels, invert(): pl.pallas_call(invert_kernel, out_shape=(full, full), in_specs=[VMEM, VME...  5.04 us
    ppermute x7, starting transfers between devices, across(): return lax.ppermute(x, AXES, pairs)  4.4 us
    unnamed x10, local copies, waits for them, and re-layouts  2.83 us
    pallas_call x1, Pallas kernels, make_square(): pl.pallas_call(square_kernel, out_shape=jax.ShapeDtypeStruct((ROWS, SIDE)...  2.35 us
  transfers between devices with their start and end apart: 10, of which 4 were waited for; matrix products, arithmetic and copies ran while one was open for 0% of the time, Pallas kernels for 16%

profile of v2, /device:TPU:1, one launch (start us, length us, event | category | flops | bytes accessed | tf_op | source)
XLA Modules:
  0.0 69.3 jit_solution(2248222812742777962)
XLA Ops:
  0.6 0.0 copy-start
  0.6 1.5 %collective-permute-start = (bf16[512,1024]{1,0:T(8,128)(2,1)}, bf16[512,1024]{1,0:T(8,128)(2,1)S(1)}, u32[]{:S(2)}, u32[]{:S(2)}) collective-permute-start(bf16[512,1024]{1,0:T(8,128)(2,1)} %mine_ref.1), channel_id=1, source_target_pairs={{0,1},{1,0},{2,3},{3,2},{4,5},{5,4},{6,7},{7,6},{8,9},{9,8},{10,11... | collective-permute-start | bytes 3145736 | tf_op jit(solution)/shard_map/ppermute | solution.py:367
  2.1 0.0 copy-start.2
  2.1 0.9 %copy-done.2 = bf16[512,128]{1,0:T(8,128)(2,1)S(1)} copy-done((bf16[512,128]{1,0:T(8,128)(2,1)S(1)}, bf16[512,128]{1,0:T(8,128)(2,1)}, u32[]{:S(2)}) %copy-start.2) | copy-done | bytes 131096
  3.0 0.0 copy-start.3
  3.0 0.7 %copy-done.3 = s32[64,16]{0,1:T(8,128)S(1)} copy-done((s32[64,16]{0,1:T(8,128)S(1)}, s32[64,16]{0,1:T(8,128)}, u32[]{:S(2)}) %copy-start.3) | copy-done | bytes 4120
  3.7 1.0 %pick_strips.1 = (bf16[2048,128]{1,0:T(8,128)(2,1)S(1)}, s32[8,64]{1,0:T(8,128)S(1)}) custom-call(s32[16,64]{1,0:T(8,128)S(1)} %bitcast.11, s32[16,64]{1,0:T(8,128)S(1)} %bitcast.12, bf16[512,128]{1,0:T(8,128)(2,1)S(1)} %copy-done.2), custom_call_target="tpu_custom_call" | custom-call | bytes 1048576 | tf_op jit(solution)/shard_map/pick_strips/pallas_call | solution.py:103
  4.8 20.5 %all_to_all.11 = bf16[8,256,128]{2,1,0:T(8,128)(2,1)S(1)} all-to-all(bf16[8,256,128]{2,1,0:T(8,128)(2,1)S(1)} %bitcast.10), channel_id=1, replica_groups={{0,2,8,10,32,34,40,42},{4,6,12,14,36,38,44,46},{16,18,24,26,48,50,56,58..., dimensions={0} | all-to-all | bytes 1048576 | tf_op jit(solution)/shard_map/all_to_all | solution.py:70
  25.3 0.0 collective-permute-start.3
  25.3 0.0 collective-permute-start.2
  25.3 0.0 collective-permute-start.1
  25.3 0.0 collective-permute-done.other_ref
  25.3 0.0 copy-start.1
  25.3 1.2 %copy-done.1 = bf16[512,1024]{1,0:T(8,128)(2,1)S(1)} copy-done((bf16[512,1024]{1,0:T(8,128)(2,1)S(1)}, bf16[512,1024]{1,0:T(8,128)(2,1)}, u32[]{:S(2)}) %copy-start.1) | copy-done | bytes 1048600
  26.5 5.0 %invert.1 = (bf16[1024,1024]{1,0:T(8,128)(2,1)S(1)}, bf16[1024,1024]{1,0:T(8,128)(2,1)S(1)}) custom-call(bf16[512,1024]{1,0:T(8,128)(2,1)S(1)} %copy-done.1, bf16[512,1024]{1,0:T(8,128)(2,1)S(1)} %collective-permute-done.other_ref, bf16[2048,128]{1,0:T(8,128)(2,1)S(1)} %bitcast.8), custom_call_target="tpu_custom_call" | custom-call | flops 2097152 | bytes 65536 | tf_op jit(solution)/shard_map/invert/pallas_call | solution.py:172
  31.6 1.7 %collective-permute-done.3.z_ref.refs_4_ = bf16[2048,128]{1,0:T(8,128)(2,1)S(1)} collective-permute-done((bf16[2048,128]{1,0:T(8,128)(2,1)S(1)}, bf16[2048,128]{1,0:T(8,128)(2,1)S(1)}, u32[]{:S(2)}, u32[]{:S(2)}) %collective-permute-start.3) | collective-permute-done | bytes 524320 | tf_op jit(solution)/shard_map/ppermute | solution.py:81
  33.3 0.0 collective-permute-done.2.y_ref.refs_2_
  33.3 0.0 collective-permute-done.1.x_ref.refs_1_
  33.3 0.0 copy-done
  33.3 1.5 %make_wide.1.mine_ref.refs_8_ = bf16[1024,1024]{1,0:T(8,128)(2,1)S(1)} custom-call(bf16[1024,1024]{1,0:T(8,128)(2,1)S(1)} %copy-done, bf16[1024,1024]{1,0:T(8,128)(2,1)S(1)} %get-tuple-element.14.hi_ref, bf16[2048,128]{1,0:T(8,128)(2,1)S(1)} %collective-permute-done.1.x_ref.refs_1_, bf16[2048,128]{1,0:T(8,128)(2,1)S(1)} %collective-permute-done.2.y_ref.refs_2_, ...), custom_call_target="tpu_custom_call" | custom-call | flops 2097152 | bytes 65536 | tf_op jit(solution)/shard_map/make_wide/pallas_call | solution.py:192
  34.8 0.2 collective-permute-start.4
  35.0 1.4 %collective-permute-start.5 = (bf16[2048,128]{1,0:T(8,128)(2,1)S(1)}, bf16[2048,128]{1,0:T(8,128)(2,1)S(1)}, u32[]{:S(2)}, u32[]{:S(2)}) collective-permute-start(bf16[2048,128]{1,0:T(8,128)(2,1)S(1)} %collective-permute-done.1.x_ref.refs_1_), channel_id=1, source_target_pairs={{0,24},{1,9},{2,26},{3,11},{4,28},{5,13},{6,30},{7,15},{8,16},{9,1... | collective-permute-start | bytes 1572872 | tf_op jit(solution)/shard_map/ppermute | solution.py:81
  36.5 0.0 collective-permute-start.7
  36.5 1.5 %collective-permute-start.6 = (bf16[2048,128]{1,0:T(8,128)(2,1)S(1)}, bf16[2048,128]{1,0:T(8,128)(2,1)S(1)}, u32[]{:S(2)}, u32[]{:S(2)}) collective-permute-start(bf16[2048,128]{1,0:T(8,128)(2,1)S(1)} %collective-permute-done.2.y_ref.refs_2_), channel_id=1, source_target_pairs={{0,96},{1,33},{2,98},{3,35},{4,100},{5,37},{6,102},{7,39},{8,104},... | collective-permute-start | bytes 1572872 | tf_op jit(solution)/shard_map/ppermute | solution.py:81
  37.9 5.4 %collective-permute-done.5.x_ref.refs_3_ = bf16[2048,128]{1,0:T(8,128)(2,1)S(1)} collective-permute-done((bf16[2048,128]{1,0:T(8,128)(2,1)S(1)}, bf16[2048,128]{1,0:T(8,128)(2,1)S(1)}, u32[]{:S(2)}, u32[]{:S(2)}) %collective-permute-start.5) | collective-permute-done | bytes 524320 | tf_op jit(solution)/shard_map/ppermute | solution.py:81
  43.3 1.5 %collective-permute-start.8 = (bf16[2048,128]{1,0:T(8,128)(2,1)S(1)}, bf16[2048,128]{1,0:T(8,128)(2,1)S(1)}, u32[]{:S(2)}, u32[]{:S(2)}) collective-permute-start(bf16[2048,128]{1,0:T(8,128)(2,1)S(1)} %collective-permute-done.5.x_ref.refs_3_), channel_id=1, source_target_pairs={{0,96},{1,33},{2,98},{3,35},{4,100},{5,37},{6,102},{7,39},{8,104},... | collective-permute-start | bytes 1572872 | tf_op jit(solution)/shard_map/ppermute | solution.py:81
  44.8 0.0 copy-start.4
  44.8 2.3 %make_square.1.square_ref = f32[512,1024]{1,0:T(8,128)S(1)} custom-call(bf16[1024,1024]{1,0:T(8,128)(2,1)S(1)} %get-tuple-element.14.hi_ref, bf16[1024,1024]{1,0:T(8,128)(2,1)S(1)} %get-tuple-element.15.lo_ref, bf16[2048,128]{1,0:T(8,128)(2,1)S(1)} %collective-permute-done.1.x_ref.refs_1_, bf16[2048,128]{1,0:T(8,128)(2,1)S(1)} %collective-permute-done.2.y_ref.refs_2_, ...), custom_call_target="tpu_custom_call" | custom-call | flops 2097152 | bytes 65536 | tf_op jit(solution)/shard_map/make_square/pallas_call | solution.py:214
  47.2 0.0 collective-permute-done.7.z_ref.refs_5_
  47.2 0.0 collective-permute-done.6.y_ref.refs_6_
  47.2 0.0 collective-permute-done.4.other_ref.refs_9_
  47.2 0.0 copy-done.4
  47.2 1.4 %turn_wide.1 = (bf16[1024,1024]{1,0:T(8,128)(2,1)S(1)}, s32[8,64]{1,0:T(8,128)S(1)}) custom-call(s32[16,64]{1,0:T(8,128)S(1)} %bitcast.13, s32[8,64]{1,0:T(8,128)S(1)} %get-tuple-element.12.places_ref, bf16[1024,1024]{1,0:T(8,128)(2,1)S(1)} %make_wide.1.mine_ref.refs_8_, bf16[1024,1024]{1,0:T(8,128)(2,1)S(1)} %collective-permute-done.4.other_ref.refs_9_, ...), custom_call_target="tpu_custom_call" | custom-call | flops 2097152 | bytes 65536 | tf_op jit(solution)/shard_map/turn_wide/pallas_call | solution.py:250
  48.6 3.0 %collective-permute-done.8.refs_7_ = bf16[2048,128]{1,0:T(8,128)(2,1)S(1)} collective-permute-done((bf16[2048,128]{1,0:T(8,128)(2,1)S(1)}, bf16[2048,128]{1,0:T(8,128)(2,1)S(1)}, u32[]{:S(2)}, u32[]{:S(2)}) %collective-permute-start.8) | collective-permute-done | bytes 524320 | tf_op jit(solution)/shard_map/ppermute | solution.py:81
  51.7 8.8 %carry.1 = (bf16[1024,1024]{1,0:T(8,128)(2,1)S(1)}, bf16[512,1024]{1,0:T(8,128)(2,1)S(1)}) custom-call(s32[16,64]{1,0:T(8,128)S(1)} %bitcast.14, s32[8,64]{1,0:T(8,128)S(1)} %get-tuple-element.17.table_ref, bf16[2048,128]{1,0:T(8,128)(2,1)S(1)} %bitcast.9, bf16[2048,128]{1,0:T(8,128)(2,1)S(1)} %collective-permute-done.1.x_ref.refs_1_, ...), custom_call_target="tpu_custom_call" | custom-call | flops 5368709120 | bytes 12582912 | tf_op jit(solution)/shard_map/carry/pallas_call | solution.py:305
  60.5 4.6 %collective-permute-start.9 = (bf16[512,1024]{1,0:T(8,128)(2,1)S(1)}, bf16[512,1024]{1,0:T(8,128)(2,1)S(1)}, u32[]{:S(2)}, u32[]{:S(2)}) collective-permute-start(bf16[512,1024]{1,0:T(8,128)(2,1)S(1)} %get-tuple-element.19), channel_id=1, source_target_pairs={{0,1},{1,0},{2,3},{3,2},{4,5},{5,4},{6,7},{7,6},{8,9},{9,8},{10,11... | collective-permute-start | bytes 3145736 | tf_op jit(solution)/shard_map/ppermute | solution.py:367
  65.1 1.3 %own_product.1.own_ref = f32[512,1024]{1,0:T(8,128)S(1)} custom-call(bf16[1024,1024]{1,0:T(8,128)(2,1)S(1)} %get-tuple-element.16.refs_10_.turned_ref, bf16[1024,1024]{1,0:T(8,128)(2,1)S(1)} %get-tuple-element.18.carried_ref, f32[512,1024]{1,0:T(8,128)S(1)} %make_square.1.square_ref), custom_call_target="tpu_custom_call" | custom-call | flops 1073741824 | bytes 8388608 | tf_op jit(solution)/shard_map/own_product/pallas_call | solution.py:329
  66.4 1.0 %collective-permute-done.9.received_ref = bf16[512,1024]{1,0:T(8,128)(2,1)S(1)} collective-permute-done((bf16[512,1024]{1,0:T(8,128)(2,1)S(1)}, bf16[512,1024]{1,0:T(8,128)(2,1)S(1)}, u32[]{:S(2)}, u32[]{:S(2)}) %collective-permute-start.9) | collective-permute-done | bytes 1048608 | tf_op jit(solution)/shard_map/ppermute | solution.py:367
  67.4 1.9 %finish.1 = (f32[512,1024]{1,0:T(8,128)}, f32[1,512]{1,0:T(1,128)}) custom-call(f32[512,1024]{1,0:T(8,128)S(1)} %own_product.1.own_ref, bf16[512,1024]{1,0:T(8,128)(2,1)S(1)} %collective-permute-done.9.received_ref), custom_call_target="tpu_custom_call" | custom-call | bytes 6291456 | tf_op jit(solution)/shard_map/finish/pallas_call | solution.py:351
Async XLA Ops:
  0.6 32.7 %copy-start = (bf16[1024,1024]{1,0:T(8,128)(2,1)S(1)}, bf16[1024,1024]{1,0:T(8,128)(2,1)}, u32[]{:S(2)}) copy-start(bf16[1024,1024]{1,0:T(8,128)(2,1)} %coupling_ref.1) | copy-start | bytes 6291460
  0.6 24.6 %collective-permute-start = (bf16[512,1024]{1,0:T(8,128)(2,1)}, bf16[512,1024]{1,0:T(8,128)(2,1)S(1)}, u32[]{:S(2)}, u32[]{:S(2)}) collective-permute-start(bf16[512,1024]{1,0:T(8,128)(2,1)} %mine_ref.1), channel_id=1, source_target_pairs={{0,1},{1,0},{2,3},{3,2},{4,5},{5,4},{6,7},{7,6},{8,9},{9,8},{10,11... | collective-permute-start | bytes 3145736 | tf_op jit(solution)/shard_map/ppermute | solution.py:367
  2.1 0.9 %copy-start.2 = (bf16[512,128]{1,0:T(8,128)(2,1)S(1)}, bf16[512,128]{1,0:T(8,128)(2,1)}, u32[]{:S(2)}) copy-start(bf16[512,128]{1,0:T(8,128)(2,1)} %strips_ref.1) | copy-start | bytes 393220
  3.0 0.7 %copy-start.3 = (s32[64,16]{0,1:T(8,128)S(1)}, s32[64,16]{0,1:T(8,128)}, u32[]{:S(2)}) copy-start(s32[64,16]{0,1:T(8,128)} %param.8) | copy-start | bytes 12292
  25.3 8.0 %collective-permute-start.3 = (bf16[2048,128]{1,0:T(8,128)(2,1)S(1)}, bf16[2048,128]{1,0:T(8,128)(2,1)S(1)}, u32[]{:S(2)}, u32[]{:S(2)}) collective-permute-start(bf16[2048,128]{1,0:T(8,128)(2,1)S(1)} %bitcast.5), channel_id=1, source_target_pairs={{0,96},{1,33},{2,98},{3,35},{4,100},{5,37},{6,102},{7,39},{8,104},... | collective-permute-start | bytes 1572872 | tf_op jit(solution)/shard_map/ppermute | solution.py:81
  25.3 8.0 %collective-permute-start.2 = (bf16[2048,128]{1,0:T(8,128)(2,1)S(1)}, bf16[2048,128]{1,0:T(8,128)(2,1)S(1)}, u32[]{:S(2)}, u32[]{:S(2)}) collective-permute-start(bf16[2048,128]{1,0:T(8,128)(2,1)S(1)} %bitcast.6), channel_id=1, source_target_pairs={{0,24},{1,9},{2,26},{3,11},{4,28},{5,13},{6,30},{7,15},{8,16},{9,1... | collective-permute-start | bytes 1572872 | tf_op jit(solution)/shard_map/ppermute | solution.py:81
  25.3 8.0 %collective-permute-start.1 = (bf16[2048,128]{1,0:T(8,128)(2,1)S(1)}, bf16[2048,128]{1,0:T(8,128)(2,1)S(1)}, u32[]{:S(2)}, u32[]{:S(2)}) collective-permute-start(bf16[2048,128]{1,0:T(8,128)(2,1)S(1)} %bitcast.7), channel_id=1, source_target_pairs={{0,6},{1,3},{2,4},{3,1},{4,2},{5,7},{6,0},{7,5},{8,14},{9,11},{10,... | collective-permute-start | bytes 1572872 | tf_op jit(solution)/shard_map/ppermute | solution.py:81
  25.3 1.2 %copy-start.1 = (bf16[512,1024]{1,0:T(8,128)(2,1)S(1)}, bf16[512,1024]{1,0:T(8,128)(2,1)}, u32[]{:S(2)}) copy-start(bf16[512,1024]{1,0:T(8,128)(2,1)} %mine_ref.1) | copy-start | bytes 3145732
  34.8 12.4 %collective-permute-start.4 = (bf16[1024,1024]{1,0:T(8,128)(2,1)S(1)}, bf16[1024,1024]{1,0:T(8,128)(2,1)S(1)}, u32[]{:S(2)}, u32[]{:S(2)}) collective-permute-start(bf16[1024,1024]{1,0:T(8,128)(2,1)S(1)} %make_wide.1.mine_ref.refs_8_), channel_id=1, source_target_pairs={{0,1},{1,0},{2,3},{3,2},{4,5},{5,4},{6,7},{7,6},{8,9},{9,8},{10,11... | collective-permute-start | bytes 6291464 | tf_op jit(solution)/shard_map/ppermute | solution.py:367
  35.0 8.3 %collective-permute-start.5 = (bf16[2048,128]{1,0:T(8,128)(2,1)S(1)}, bf16[2048,128]{1,0:T(8,128)(2,1)S(1)}, u32[]{:S(2)}, u32[]{:S(2)}) collective-permute-start(bf16[2048,128]{1,0:T(8,128)(2,1)S(1)} %collective-permute-done.1.x_ref.refs_1_), channel_id=1, source_target_pairs={{0,24},{1,9},{2,26},{3,11},{4,28},{5,13},{6,30},{7,15},{8,16},{9,1... | collective-permute-start | bytes 1572872 | tf_op jit(solution)/shard_map/ppermute | solution.py:81
  36.5 10.7 %collective-permute-start.7 = (bf16[2048,128]{1,0:T(8,128)(2,1)S(1)}, bf16[2048,128]{1,0:T(8,128)(2,1)S(1)}, u32[]{:S(2)}, u32[]{:S(2)}) collective-permute-start(bf16[2048,128]{1,0:T(8,128)(2,1)S(1)} %collective-permute-done.3.z_ref.refs_4_), channel_id=1, source_target_pairs={{0,6},{1,3},{2,4},{3,1},{4,2},{5,7},{6,0},{7,5},{8,14},{9,11},{10,... | collective-permute-start | bytes 1572872 | tf_op jit(solution)/shard_map/ppermute | solution.py:81
  36.5 10.7 %collective-permute-start.6 = (bf16[2048,128]{1,0:T(8,128)(2,1)S(1)}, bf16[2048,128]{1,0:T(8,128)(2,1)S(1)}, u32[]{:S(2)}, u32[]{:S(2)}) collective-permute-start(bf16[2048,128]{1,0:T(8,128)(2,1)S(1)} %collective-permute-done.2.y_ref.refs_2_), channel_id=1, source_target_pairs={{0,96},{1,33},{2,98},{3,35},{4,100},{5,37},{6,102},{7,39},{8,104},... | collective-permute-start | bytes 1572872 | tf_op jit(solution)/shard_map/ppermute | solution.py:81
  43.3 8.3 %collective-permute-start.8 = (bf16[2048,128]{1,0:T(8,128)(2,1)S(1)}, bf16[2048,128]{1,0:T(8,128)(2,1)S(1)}, u32[]{:S(2)}, u32[]{:S(2)}) collective-permute-start(bf16[2048,128]{1,0:T(8,128)(2,1)S(1)} %collective-permute-done.5.x_ref.refs_3_), channel_id=1, source_target_pairs={{0,96},{1,33},{2,98},{3,35},{4,100},{5,37},{6,102},{7,39},{8,104},... | collective-permute-start | bytes 1572872 | tf_op jit(solution)/shard_map/ppermute | solution.py:81
  44.8 2.4 %copy-start.4 = (s32[64,16]{0,1:T(8,128)S(1)}, s32[64,16]{0,1:T(8,128)}, u32[]{:S(2)}) copy-start(s32[64,16]{0,1:T(8,128)} %param.7) | copy-start | bytes 12292
  60.5 6.9 %collective-permute-start.9 = (bf16[512,1024]{1,0:T(8,128)(2,1)S(1)}, bf16[512,1024]{1,0:T(8,128)(2,1)S(1)}, u32[]{:S(2)}, u32[]{:S(2)}) collective-permute-start(bf16[512,1024]{1,0:T(8,128)(2,1)S(1)} %get-tuple-element.19), channel_id=1, source_target_pairs={{0,1},{1,0},{2,3},{3,2},{4,5},{5,4},{6,7},{7,6},{8,9},{9,8},{10,11... | collective-permute-start | bytes 3145736 | tf_op jit(solution)/shard_map/ppermute | solution.py:367

commit v3 on v2

--- a/solution.py
+++ b/solution.py
@@ -16,6 +16,7 @@
 F32 = jnp.float32
 BF16 = jnp.bfloat16
 VMEM = pl.BlockSpec(memory_space=pltpu.VMEM)
+HBM = pl.BlockSpec(memory_space=pltpu.HBM)
 ANY = pl.BlockSpec(memory_space=pl.ANY)
 SMEM = pl.BlockSpec(memory_space=pltpu.SMEM)
 MIB = 1024 * 1024
@@ -81,45 +82,59 @@
     return lax.ppermute(x, AXES, pairs)
 
 
-def pick_kernel(slots_ref, table_ref, strips_ref, out_ref, places_ref):
+def pick_kernel(slots_hbm, strips_hbm, out_ref, slots_ref, held_ref, sems):
     core, group = lax.axis_index("panel"), lax.axis_index("front")
+    table = pltpu.make_async_copy(slots_hbm, slots_ref, sems.at[0])
+    fetch = pltpu.make_async_copy(strips_hbm, held_ref, sems.at[1])
+    table.start()
+    fetch.start()
+    table.wait()
+    fetch.wait()
     for slot in range(NABOVE):
         row = slots_ref[slot, group] // 64 - core * HALF
 
         @pl.when((row >= 0) & (row < HALF))
         def _():
-            strip = strips_ref[slot * STRIP : (slot + 1) * STRIP, :]
+            strip = held_ref[slot * STRIP : (slot + 1) * STRIP, :]
             for copy in range(8):
                 at = pl.multiple_of(copy * HALF * STRIP + row * STRIP, STRIP)
                 out_ref[pl.ds(at, STRIP), :] = strip
 
-    ids = table_ref[...]
-    for row in range(HALF):
-        hit = (ids >> 6) == core * HALF + row
-        places_ref[row : row + 1, :] = jnp.sum(jnp.where(hit, ids & 63, 0), axis=0, keepdims=True)
-
 
 def pick_strips(slots, strips):
     return pl.pallas_call(
         pick_kernel,
-        out_shape=(
-            jax.ShapeDtypeStruct((8 * HALF * STRIP, BLOCK), BF16),
-            jax.ShapeDtypeStruct((HALF, 64), jnp.int32),
-        ),
-        in_specs=[SMEM, VMEM, VMEM],
-        out_specs=(VMEM, VMEM),
+        out_shape=jax.ShapeDtypeStruct((8 * HALF * STRIP, BLOCK), BF16),
+        in_specs=[HBM, HBM],
+        out_specs=VMEM,
+        scratch_shapes=[
+            pltpu.SMEM((NABOVE, 64), jnp.int32),
+            pltpu.VMEM((NABOVE * STRIP, BLOCK), BF16),
+            pltpu.SemaphoreType.DMA((2,)),
+        ],
         compiler_params=params(4),
         cost_estimate=cost(0, 1 << 20),
         name="pick_strips",
-    )(slots, slots, strips)
-
-
-def invert_kernel(mine_ref, other_ref, after_ref, hi_ref, lo_ref, low_ref):
+    )(*(pltpu.with_memory_space_constraint(x, pltpu.HBM) for x in (slots, strips)))
+
+
+def solve_kernel(
+    mine_hbm, other_hbm, coupling_hbm, after_ref, hi_out, lo_out, wide_out,
+    hi_ref, lo_ref, low_ref, coupling_ref, wide_ref, sems,
+):
     core = lax.axis_index("panel")
-    low_ref[pl.ds(pl.multiple_of(core * ROWS, ROWS), ROWS), :] = mine_ref[...]
-    low_ref[pl.ds(pl.multiple_of((1 - core) * ROWS, ROWS), ROWS), :] = other_ref[...]
+    mine, other = (pl.ds(pl.multiple_of(half * ROWS, ROWS), ROWS) for half in (core, 1 - core))
+    fetches = [
+        pltpu.make_async_copy(mine_hbm, low_ref.at[mine], sems.at[0]),
+        pltpu.make_async_copy(other_hbm, low_ref.at[other], sems.at[1]),
+        pltpu.make_async_copy(coupling_hbm, coupling_ref, sems.at[2]),
+    ]
+    for fetch in fetches:
+        fetch.start()
     hi_ref[...] = jnp.zeros_like(hi_ref)
     lo_ref[...] = jnp.zeros_like(lo_ref)
+    fetches[0].wait()
+    fetches[1].wait()
     row = lax.broadcasted_iota(jnp.int32, (BLOCK, BLOCK), 0)
     col = lax.broadcasted_iota(jnp.int32, (BLOCK, BLOCK), 1)
     differ = row ^ col
@@ -165,39 +180,42 @@
                 -(dot(hi, t_hi) + dot(hi, t_lo) + dot(lo, t_hi))
             )
         size *= 2
-
-
-def invert(mine, other, after):
-    full = jax.ShapeDtypeStruct((SIDE, SIDE), BF16)
-    return pl.pallas_call(
-        invert_kernel,
-        out_shape=(full, full),
-        in_specs=[VMEM, VMEM, ANY],
-        out_specs=(VMEM, VMEM),
-        scratch_shapes=[pltpu.VMEM((SIDE, SIDE), BF16)],
-        compiler_params=params(12),
-        cost_estimate=cost(1 << 20, 1 << 16),
-        name="invert",
-    )(mine, other, after)
-
-
-def wide_kernel(coupling_ref, hi_ref, x_ref, y_ref, z_ref, wide_ref):
+    copies = [
+        pltpu.make_async_copy(hi_ref, hi_out, sems.at[3]),
+        pltpu.make_async_copy(lo_ref, lo_out, sems.at[4]),
+    ]
+    for copy in copies:
+        copy.start()
+    fetches[2].wait()
     tile = 256
     for n in range(0, SIDE, tile):
         columns = slice(n, n + tile)
         wide_ref[:, columns] = dot(coupling_ref[:, n:], hi_ref[n:, columns]).astype(BF16)
-
-
-def make_wide(coupling, hi, after):
-    return pl.pallas_call(
-        wide_kernel,
-        out_shape=jax.ShapeDtypeStruct((SIDE, SIDE), BF16),
-        in_specs=[VMEM, VMEM, ANY, ANY, ANY],
-        out_specs=VMEM,
-        compiler_params=params(10),
-        cost_estimate=cost(1 << 20, 1 << 16),
-        name="make_wide",
-    )(coupling, hi, *after)
+        copies.append(
+            pltpu.make_async_copy(wide_ref.at[:, columns], wide_out.at[:, columns], sems.at[5 + n // tile])
+        )
+        copies[-1].start()
+    for copy in copies:
+        copy.wait()
+
+
+def solve(mine, other, coupling, after):
+    full = jax.ShapeDtypeStruct((SIDE, SIDE), BF16)
+    return pl.pallas_call(
+        solve_kernel,
+        out_shape=(full, full, full),
+        in_specs=[HBM, HBM, HBM, ANY],
+        out_specs=(HBM, HBM, HBM),
+        scratch_shapes=[pltpu.VMEM((SIDE, SIDE), BF16)] * 5 + [pltpu.SemaphoreType.DMA((9,))],
+        compiler_params=params(60),
+        cost_estimate=cost(4 << 30, 12 << 20),
+        name="solve",
+    )(
+        pltpu.with_memory_space_constraint(mine, pltpu.HBM),
+        other,
+        pltpu.with_memory_space_constraint(coupling, pltpu.HBM),
+        after,
+    )
 
 
 def square_kernel(hi_ref, lo_ref, x_ref, y_ref, z_ref, square_ref):
@@ -222,9 +240,14 @@
     )(hi, lo, *after)
 
 
-def turn_kernel(list_ref, places_ref, mine_ref, other_ref, x_ref, y_ref, z_ref, square_ref, out_ref, table_ref):
+def turn_kernel(list_ref, slots_ref, mine_ref, other_ref, x_ref, y_ref, z_ref, square_ref, out_ref, table_ref):
     core, group = lax.axis_index("panel"), lax.axis_index("front")
-    places = places_ref[...]
+    ids = slots_ref[...]
+    rows = [
+        jnp.sum(jnp.where((ids >> 6) == core * HALF + row, ids & 63, 0), axis=0, keepdims=True)
+        for row in range(HALF)
+    ]
+    places = jnp.concatenate(rows, axis=0)
     column = jnp.full(places.shape, NABOVE, jnp.int32)
     for a in range(NABOVE):
         column = jnp.where((places >> 2) == list_ref[a, group], a ^ (core * HALF), column)
@@ -246,7 +269,7 @@
             out_ref[:, columns] = other_ref[at : at + BLOCK, :].astype(F32).T.astype(BF16)
 
 
-def turn_wide(lists, places, mine, other, after):
+def turn_wide(lists, slots, mine, other, after):
     return pl.pallas_call(
         turn_kernel,
         out_shape=(
@@ -258,14 +281,27 @@
         compiler_params=params(12),
         cost_estimate=cost(1 << 20, 1 << 16),
         name="turn_wide",
-    )(lists, places, mine, other, *after)
-
-
-def carry_kernel(list_ref, table_ref, *refs):
-    strips_refs, refs = refs[:8], refs[8:]
-    mine_ref, other_ref, turned_ref, carried_ref, send_ref, sigma_ref = refs
+    )(lists, slots, mine, other, *after)
+
+
+def place_strips(table_ref, sigma_ref, strips_ref, bits):
     core, group = lax.axis_index("panel"), lax.axis_index("front")
     first, second = jnp.where(core == 0, 1, 3), jnp.where(core == 0, 3, 1)
+    middle = group ^ spread(bits, second)
+    start = jnp.where(first == 1, middle & 0b101010, middle ^ (3 * ((middle >> 1) & 0b010101)))
+
+    @pl.loop(0, 8)
+    def _(n):
+        source = start ^ spread(n, first)
+        for row in range(HALF):
+            to = pl.multiple_of(table_ref[row, source], STRIP)
+            at = pl.multiple_of(n * HALF * STRIP + row * STRIP, STRIP)
+            sigma_ref[pl.ds(to, STRIP), :] = strips_ref[pl.ds(at, STRIP), :]
+
+
+def sigma_kernel(list_ref, table_ref, *refs):
+    strips_refs, sigma_ref = refs[:7], refs[7]
+    core, group = lax.axis_index("panel"), lax.axis_index("front")
     for a in range(NABOVE):
         column = pl.multiple_of((a ^ (core * HALF)) * SIDE, SIDE)
 
@@ -273,17 +309,30 @@
         def _():
             sigma_ref[pl.ds(column, SIDE), :] = jnp.zeros((SIDE, BLOCK), BF16)
 
-    for bits in range(8):
-        middle = group ^ spread(bits, second)
-        start = jnp.where(first == 1, middle & 0b101010, middle ^ (3 * ((middle >> 1) & 0b010101)))
-
-        @pl.loop(0, 8)
-        def _(n):
-            source = start ^ spread(n, first)
-            for row in range(HALF):
-                to = pl.multiple_of(table_ref[row, source], STRIP)
-                at = pl.multiple_of(n * HALF * STRIP + row * STRIP, STRIP)
-                sigma_ref[pl.ds(to, STRIP), :] = strips_refs[bits][pl.ds(at, STRIP), :]
+    for bits in range(7):
+        place_strips(table_ref, sigma_ref, strips_refs[bits], bits)
+
+
+SIGMA = jax.ShapeDtypeStruct(((NABOVE + 1) * SIDE, BLOCK), BF16)
+
+
+def make_sigma(lists, table, strips):
+    return pl.pallas_call(
+        sigma_kernel,
+        out_shape=SIGMA,
+        in_specs=[SMEM, SMEM] + [VMEM] * 7,
+        out_specs=VMEM,
+        compiler_params=params(12),
+        cost_estimate=cost(1 << 20, 1 << 16),
+        name="make_sigma",
+    )(lists, table, *strips)
+
+
+def carry_kernel(
+    table_ref, sigma_in_ref, strips_ref, mine_ref, other_ref, turned_ref, carried_ref, send_ref, sigma_ref
+):
+    core = lax.axis_index("panel")
+    place_strips(table_ref, sigma_ref, strips_ref, 7)
 
     def sigma(at):
         blocks = [sigma_ref[c * SIDE : (c + 1) * SIDE, :] for c in range(at, at + HALF)]
@@ -301,20 +350,21 @@
         send_ref[:, columns] = dot(turned_ref[theirs, :], carried_ref[:, columns]).astype(BF16)
 
 
-def carry(lists, table, strips, mine, other, turned):
+def carry(table, sigma, last, mine, other, turned):
     return pl.pallas_call(
         carry_kernel,
         out_shape=(
             jax.ShapeDtypeStruct((SIDE, SIDE), BF16),
             jax.ShapeDtypeStruct((ROWS, SIDE), BF16),
+            SIGMA,
         ),
-        in_specs=[SMEM, SMEM] + [VMEM] * 11,
-        out_specs=(VMEM, VMEM),
-        scratch_shapes=[pltpu.VMEM(((NABOVE + 1) * SIDE, BLOCK), BF16)],
-        compiler_params=params(24),
+        in_specs=[SMEM] + [VMEM] * 5,
+        out_specs=(VMEM, VMEM, VMEM),
+        input_output_aliases={1: 2},
+        compiler_params=params(20),
         cost_estimate=cost(5 << 29, 12 << 20),
         name="carry",
-    )(lists, table, *strips, mine, other, turned)
+    )(table, sigma, last, mine, other, turned)
 
 
 def own_kernel(turned_ref, carried_ref, square_ref, out_ref):
@@ -370,17 +420,18 @@
 def on_device(sep_factor, coup_factor, coup_list, slot_tiles, anc_tiles):
     lists, slots = coup_list.T, slot_tiles.T
     sep_other = swap(sep_factor)
-    picked, places = pick_strips(slots, anc_tiles)
+    picked = pick_strips(slots, anc_tiles)
     near = gather_cube(picked, 0)
-    hi, lo = invert(sep_factor, sep_other, near)
+    hi, lo, wide_mine = solve(sep_factor, sep_other, coup_factor, picked)
+    near, wide_mine = lax.optimization_barrier((near, wide_mine))
     x, y, z = across(near, 1), across(near, 2), across(near, 4)
-    wide_mine = make_wide(coup_factor, hi, (x, y, z))
     wide_other = swap(wide_mine)
     xy, yz, zx = across(x, 2), across(y, 4), across(z, 1)
     square = make_square(hi, lo, (x, y, z))
-    strips = [near, x, y, xy, z, zx, yz, across(xy, 4)]
-    turned, table = turn_wide(lists, places, wide_mine, wide_other, (xy, yz, zx, square))
-    carried, to_send = carry(lists, table, strips, wide_mine, wide_other, turned)
+    xy, square = lax.optimization_barrier((xy, square))
+    turned, table = turn_wide(lists, slots, wide_mine, wide_other, (x, y, z, square))
+    sigma = make_sigma(lists, table, (near, x, y, xy, z, zx, yz))
+    carried, to_send, _ = carry(table, sigma, across(xy, 4), wide_mine, wide_other, turned)
     received = swap(to_send)
     own = own_product(turned, carried, square)
     selected, variances = finish(own, received)

time: 69.4 us -> 70.2 us (1.012)
  blocking collectives: 20.5 us -> 0 us
  starting transfers between devices: 10.7 us -> 22.6 us
  Pallas kernels: 23.4 us -> 27.7 us
  waiting for transfers between devices: 11.2 us -> 14.8 us
  local copies, waits for them, and re-layouts: 2.83 us -> 4.16 us
    all_to_all x1 -> x0, blocking collectives: 20.5 us -> none  [gather_cube(): lax.all_to_all(parts, AXES, split_axis=0, concat_axis=0, tiled=True, axis...]
    all_to_all x0 -> x1, starting transfers between devices: none -> 9.81 us  [gather_cube(): lax.all_to_all(parts, AXES, split_axis=0, concat_axis=0, tiled=True, axis...]
    pallas_call x3, Pallas kernels: 7.61 us -> 13.9 us  [the longest x1 9.03 us: solve(): pl.pallas_call(solve_kernel, out_shape=(full, full, full), in_specs=[HBM,...]
    ppermute x3, starting transfers between devices: 6.3 us -> 11 us  [swap(): return lax.ppermute(x, 'panel', [(0, 1), (1, 0)])]
    ppermute x7, waiting for transfers between devices: 10.2 us -> 12.9 us  [across(): return lax.ppermute(x, AXES, pairs)]
    ppermute x7, starting transfers between devices: 4.4 us -> 1.8 us  [across(): return lax.ppermute(x, AXES, pairs)]
    pallas_call x1, Pallas kernels: 8.85 us -> 6.44 us  [carry(): pl.pallas_call(carry_kernel, out_shape=(jax.ShapeDtypeStruct((SIDE, SIDE)...]
    unnamed x10 -> x12, local copies, waits for them, and re-layouts: 2.83 us -> 4.16 us
  transfers between devices with their start and end apart: 10 -> 11, of which waited for: 4 -> 5; matrix products, arithmetic and copies ran while one was open for 0% -> 0% of each run, Pallas kernels for 16% -> 28%
where the time goes in v3:
time: 70.2 us; the launch traced here: 70 us
  Pallas kernels  27.7 us (39%)
  starting transfers between devices  22.6 us (32%)
  waiting for transfers between devices  14.8 us (21%)
  local copies, waits for them, and re-layouts  4.16 us (6%)
  between operations  0.75 us (1%)
    ppermute x7, waiting for transfers between devices, across(): return lax.ppermute(x, AXES, pairs)  12.9 us
    ppermute x3, starting transfers between devices, swap(): return lax.ppermute(x, 'panel', [(0, 1), (1, 0)])  11 us
    all_to_all x1, starting transfers between devices, gather_cube(): lax.all_to_all(parts, AXES, split_axis=0, concat_axis=0, tiled=True, axis...  9.81 us
    pallas_call x1, Pallas kernels, solve(): pl.pallas_call(solve_kernel, out_shape=(full, full, full), in_specs=[HBM,...  9.03 us
    pallas_call x1, Pallas kernels, carry(): pl.pallas_call(carry_kernel, out_shape=(jax.ShapeDtypeStruct((SIDE, SIDE)...  6.44 us
    unnamed x12, local copies, waits for them, and re-layouts  4.16 us
    pallas_call x1, Pallas kernels, make_sigma(): pl.pallas_call(sigma_kernel, out_shape=SIGMA, in_specs=[SMEM, SMEM] + [VM...  2.82 us
    pallas_call x1, Pallas kernels, make_square(): pl.pallas_call(square_kernel, out_shape=jax.ShapeDtypeStruct((ROWS, SIDE)...  2.34 us
  transfers between devices with their start and end apart: 11, of which 5 were waited for; matrix products, arithmetic and copies ran while one was open for 0% of the time, Pallas kernels for 28%

profile of v3, /device:TPU:1, one launch (start us, length us, event | category | flops | bytes accessed | tf_op | source)
XLA Modules:
  0.0 70.0 jit_solution(8474873633740679716)
XLA Ops:
  0.6 1.5 %collective-permute-start = (bf16[512,1024]{1,0:T(8,128)(2,1)}, bf16[512,1024]{1,0:T(8,128)(2,1)S(1)}, u32[]{:S(2)}, u32[]{:S(2)}) collective-permute-start(bf16[512,1024]{1,0:T(8,128)(2,1)} %mine_hbm.1), channel_id=1, source_target_pairs={{0,1},{1,0},{2,3},{3,2},{4,5},{5,4},{6,7},{7,6},{8,9},{9,8},{10,11... | collective-permute-start | bytes 3145736 | tf_op jit(solution)/shard_map/ppermute | solution.py:417
  2.1 2.0 %pick_strips.1.after_ref = bf16[2048,128]{1,0:T(8,128)(2,1)} custom-call(s32[16,64]{1,0:T(8,128)} %bitcast.9, bf16[512,128]{1,0:T(8,128)(2,1)} %strips_hbm.1), custom_call_target="tpu_custom_call" | custom-call | bytes 1048576 | tf_op jit(solution)/shard_map/pick_strips/pallas_call | solution.py:105
  4.2 9.8 %all-to-all-start = ((bf16[8,256,128]{2,1,0:T(8,128)(2,1)}), bf16[8,256,128]{2,1,0:T(8,128)(2,1)S(1)}, u32[]{:S(2)}, u32[]{:S(2)}) async-start(bf16[8,256,128]{2,1,0:T(8,128)(2,1)} %bitcast.2), calls=%async_computation | async-start | bytes 1048576 | tf_op jit(solution)/shard_map/all_to_all | solution.py:71
  14.0 0.0 collective-permute-done.other_hbm
  14.0 0.0 copy-start.5
  14.0 1.0 %copy-done.5 = bf16[512,1024]{1,0:T(8,128)(2,1)} copy-done((bf16[512,1024]{1,0:T(8,128)(2,1)}, bf16[512,1024]{1,0:T(8,128)(2,1)S(1)}, u32[]{:S(2)}) %copy-start.5) | copy-done | bytes 1048600
  15.0 9.0 %solve.1 = (bf16[1024,1024]{1,0:T(8,128)(2,1)}, bf16[1024,1024]{1,0:T(8,128)(2,1)}, bf16[1024,1024]{1,0:T(8,128)(2,1)}) custom-call(bf16[512,1024]{1,0:T(8,128)(2,1)} %mine_hbm.1, bf16[512,1024]{1,0:T(8,128)(2,1)} %copy-done.5, bf16[1024,1024]{1,0:T(8,128)(2,1)} %coupling_hbm.1, bf16[2048,128]{1,0:T(8,128)(2,1)} %pick_strips.1.after_ref), custom_call_target="tpu_custom_call" | custom-call | flops 8589934592 | bytes 12582912 | tf_op jit(solution)/shard_map/solve/pallas_call | solution.py:204
  24.0 0.8 %all-to-all-done = bf16[8,256,128]{2,1,0:T(8,128)(2,1)S(1)} async-done(((bf16[8,256,128]{2,1,0:T(8,128)(2,1)}), bf16[8,256,128]{2,1,0:T(8,128)(2,1)S(1)}, u32[]{:S(2)}, u32[]{:S(2)}) %all-to-all-start) | async-done | bytes 524320 | tf_op jit(solution)/shard_map/all_to_all | solution.py:71
  24.8 0.0 collective-permute-start.1
  24.8 0.0 collective-permute-start.2
  24.8 0.0 collective-permute-start.4
  24.8 0.1 collective-permute-start.3
  24.9 8.2 %collective-permute-done.2.x_ref.refs_1_ = bf16[2048,128]{1,0:T(8,128)(2,1)S(1)} collective-permute-done((bf16[2048,128]{1,0:T(8,128)(2,1)S(1)}, bf16[2048,128]{1,0:T(8,128)(2,1)S(1)}, u32[]{:S(2)}, u32[]{:S(2)}) %collective-permute-start.2) | collective-permute-done | bytes 524320 | tf_op jit(solution)/shard_map/ppermute | solution.py:82
  33.2 0.0 collective-permute-start.5
  33.2 0.0 collective-permute-done.4.z_ref.refs_4_
  33.2 1.5 %collective-permute-start.6 = (bf16[2048,128]{1,0:T(8,128)(2,1)S(1)}, bf16[2048,128]{1,0:T(8,128)(2,1)S(1)}, u32[]{:S(2)}, u32[]{:S(2)}) collective-permute-start(bf16[2048,128]{1,0:T(8,128)(2,1)S(1)} %collective-permute-done.4.z_ref.refs_4_), channel_id=1, source_target_pairs={{0,6},{1,3},{2,4},{3,1},{4,2},{5,7},{6,0},{7,5},{8,14},{9,11},{10,... | collective-permute-start | bytes 1572872 | tf_op jit(solution)/shard_map/ppermute | solution.py:82
  34.6 0.0 collective-permute-done.3.y_ref.refs_2_
  34.6 0.0 collective-permute-start.7
  34.6 0.0 copy-start.1
  34.6 1.6 %copy-done.1 = bf16[1024,1024]{1,0:T(8,128)(2,1)S(1)} copy-done((bf16[1024,1024]{1,0:T(8,128)(2,1)S(1)}, bf16[1024,1024]{1,0:T(8,128)(2,1)}, u32[]{:S(2)}) %copy-start.1) | copy-done | bytes 2097176
  36.2 0.0 copy-start.2
  36.2 1.6 %copy-done.2 = bf16[1024,1024]{1,0:T(8,128)(2,1)S(1)} copy-done((bf16[1024,1024]{1,0:T(8,128)(2,1)S(1)}, bf16[1024,1024]{1,0:T(8,128)(2,1)}, u32[]{:S(2)}) %copy-start.2) | copy-done | bytes 2097176
  37.8 0.0 copy-start
  37.8 0.0 copy-start.3
  37.8 0.0 copy-start.4
  37.8 2.3 %make_square.1.square_ref = f32[512,1024]{1,0:T(8,128)S(1)} custom-call(bf16[1024,1024]{1,0:T(8,128)(2,1)S(1)} %copy-done.1, bf16[1024,1024]{1,0:T(8,128)(2,1)S(1)} %copy-done.2, bf16[2048,128]{1,0:T(8,128)(2,1)S(1)} %collective-permute-done.2.x_ref.refs_1_, bf16[2048,128]{1,0:T(8,128)(2,1)S(1)} %collective-permute-done.3.y_ref.refs_2_, ...), custom_call_target="tpu_custom_call" | custom-call | flops 2097152 | bytes 65536 | tf_op jit(solution)/shard_map/make_square/pallas_call | solution.py:232
  40.2 1.3 %collective-permute-done.5.refs_3_ = bf16[2048,128]{1,0:T(8,128)(2,1)S(1)} collective-permute-done((bf16[2048,128]{1,0:T(8,128)(2,1)S(1)}, bf16[2048,128]{1,0:T(8,128)(2,1)S(1)}, u32[]{:S(2)}, u32[]{:S(2)}) %collective-permute-start.5) | collective-permute-done | bytes 524320 | tf_op jit(solution)/shard_map/ppermute | solution.py:82
  41.5 0.2 collective-permute-start.8
  41.7 0.0 collective-permute-done.1.other_ref
  41.7 0.0 copy-done
  41.7 0.0 copy-done.3
  41.7 0.0 copy-done.4
  41.8 1.9 %turn_wide.1 = (bf16[1024,1024]{1,0:T(8,128)(2,1)S(1)}, s32[8,64]{1,0:T(8,128)S(1)}) custom-call(s32[16,64]{1,0:T(8,128)S(1)} %bitcast.11, s32[16,64]{1,0:T(8,128)S(1)} %bitcast.10, bf16[1024,1024]{1,0:T(8,128)(2,1)S(1)} %copy-done, bf16[1024,1024]{1,0:T(8,128)(2,1)S(1)} %collective-permute-done.1.other_ref, ...), custom_call_target="tpu_custom_call" | custom-call | flops 2097152 | bytes 65536 | tf_op jit(solution)/shard_map/turn_wide/pallas_call | solution.py:273
  43.6 0.0 collective-permute-done.6.refs_5_
  43.6 0.0 collective-permute-done.7.refs_6_
  43.7 2.8 %make_sigma.1.sigma_in_ref = bf16[17408,128]{1,0:T(8,128)(2,1)S(1)} custom-call(s32[16,64]{1,0:T(8,128)S(1)} %bitcast.12, s32[8,64]{1,0:T(8,128)S(1)} %get-tuple-element.22.table_ref, bf16[2048,128]{1,0:T(8,128)(2,1)S(1)} %bitcast.8, bf16[2048,128]{1,0:T(8,128)(2,1)S(1)} %collective-permute-done.2.x_ref.refs_1_, ...), custom_call_target="tpu_custom_call" | custom-call | flops 2097152 | bytes 65536 | tf_op jit(solution)/shard_map/make_sigma/pallas_call | solution.py:320
  46.5 3.3 %collective-permute-done.8.strips_ref = bf16[2048,128]{1,0:T(8,128)(2,1)S(1)} collective-permute-done((bf16[2048,128]{1,0:T(8,128)(2,1)S(1)}, bf16[2048,128]{1,0:T(8,128)(2,1)S(1)}, u32[]{:S(2)}, u32[]{:S(2)}) %collective-permute-start.8) | collective-permute-done | bytes 524320 | tf_op jit(solution)/shard_map/ppermute | solution.py:82
  49.8 6.4 %carry.1 = (bf16[1024,1024]{1,0:T(8,128)(2,1)S(1)}, bf16[512,1024]{1,0:T(8,128)(2,1)S(1)}, bf16[17408,128]{1,0:T(8,128)(2,1)S(1)}) custom-call(s32[8,64]{1,0:T(8,128)S(1)} %get-tuple-element.22.table_ref, bf16[17408,128]{1,0:T(8,128)(2,1)S(1)} %make_sigma.1.sigma_in_ref, ...), custom_call_target="tpu_custom_call", output_to_operand_aliasing={{2}: (1, {})} | custom-call | flops 5368709120 | bytes 12582912 | tf_op jit(solution)/shard_map/carry/pallas_call | solution.py:354
  56.3 9.5 %collective-permute-start.9 = (bf16[512,1024]{1,0:T(8,128)(2,1)S(1)}, bf16[512,1024]{1,0:T(8,128)(2,1)S(1)}, u32[]{:S(2)}, u32[]{:S(2)}) collective-permute-start(bf16[512,1024]{1,0:T(8,128)(2,1)S(1)} %get-tuple-element.25), channel_id=1, source_target_pairs={{0,1},{1,0},{2,3},{3,2},{4,5},{5,4},{6,7},{7,6},{8,9},{9,8},{10,11... | collective-permute-start | bytes 3145736 | tf_op jit(solution)/shard_map/ppermute | solution.py:417
  65.8 1.2 %own_product.1.own_ref = f32[512,1024]{1,0:T(8,128)S(1)} custom-call(bf16[1024,1024]{1,0:T(8,128)(2,1)S(1)} %get-tuple-element.21.turned_ref, bf16[1024,1024]{1,0:T(8,128)(2,1)S(1)} %get-tuple-element.24.carried_ref, f32[512,1024]{1,0:T(8,128)S(1)} %make_square.1.square_ref), custom_call_target="tpu_custom_call" | custom-call | flops 1073741824 | bytes 8388608 | tf_op jit(solution)/shard_map/own_product/pallas_call | solution.py:379
  67.0 1.0 %collective-permute-done.9.received_ref = bf16[512,1024]{1,0:T(8,128)(2,1)S(1)} collective-permute-done((bf16[512,1024]{1,0:T(8,128)(2,1)S(1)}, bf16[512,1024]{1,0:T(8,128)(2,1)S(1)}, u32[]{:S(2)}, u32[]{:S(2)}) %collective-permute-start.9) | collective-permute-done | bytes 1048608 | tf_op jit(solution)/shard_map/ppermute | solution.py:417
  68.1 1.9 %finish.1 = (f32[512,1024]{1,0:T(8,128)}, f32[1,512]{1,0:T(1,128)}) custom-call(f32[512,1024]{1,0:T(8,128)S(1)} %own_product.1.own_ref, bf16[512,1024]{1,0:T(8,128)(2,1)S(1)} %collective-permute-done.9.received_ref), custom_call_target="tpu_custom_call" | custom-call | bytes 6291456 | tf_op jit(solution)/shard_map/finish/pallas_call | solution.py:401
Async XLA Ops:
  0.6 13.3 %collective-permute-start = (bf16[512,1024]{1,0:T(8,128)(2,1)}, bf16[512,1024]{1,0:T(8,128)(2,1)S(1)}, u32[]{:S(2)}, u32[]{:S(2)}) collective-permute-start(bf16[512,1024]{1,0:T(8,128)(2,1)} %mine_hbm.1), channel_id=1, source_target_pairs={{0,1},{1,0},{2,3},{3,2},{4,5},{5,4},{6,7},{7,6},{8,9},{9,8},{10,11... | collective-permute-start | bytes 3145736 | tf_op jit(solution)/shard_map/ppermute | solution.py:417
  4.2 20.7 %all-to-all-start = ((bf16[8,256,128]{2,1,0:T(8,128)(2,1)}), bf16[8,256,128]{2,1,0:T(8,128)(2,1)S(1)}, u32[]{:S(2)}, u32[]{:S(2)}) async-start(bf16[8,256,128]{2,1,0:T(8,128)(2,1)} %bitcast.2), calls=%async_computation | async-start | bytes 1048576 | tf_op jit(solution)/shard_map/all_to_all | solution.py:71
  14.0 1.0 %copy-start.5 = (bf16[512,1024]{1,0:T(8,128)(2,1)}, bf16[512,1024]{1,0:T(8,128)(2,1)S(1)}, u32[]{:S(2)}) copy-start(bf16[512,1024]{1,0:T(8,128)(2,1)S(1)} %collective-permute-done.other_hbm) | copy-start | bytes 3145732
  24.8 16.9 %collective-permute-start.1 = (bf16[1024,1024]{1,0:T(8,128)(2,1)}, bf16[1024,1024]{1,0:T(8,128)(2,1)S(1)}, u32[]{:S(2)}, u32[]{:S(2)}) collective-permute-start(bf16[1024,1024]{1,0:T(8,128)(2,1)} %get-tuple-element.16.mine_ref), channel_id=1, source_target_pairs={{0,1},{1,0},{2,3},{3,2},{4,5},{5,4},{6,7},{7,6},{8,9},{9,8},{10,11... | collective-permute-start | bytes 6291464 | tf_op jit(solution)/shard_map/ppermute | solution.py:417
  24.8 8.3 %collective-permute-start.2 = (bf16[2048,128]{1,0:T(8,128)(2,1)S(1)}, bf16[2048,128]{1,0:T(8,128)(2,1)S(1)}, u32[]{:S(2)}, u32[]{:S(2)}) collective-permute-start(bf16[2048,128]{1,0:T(8,128)(2,1)S(1)} %bitcast.5), channel_id=1, source_target_pairs={{0,6},{1,3},{2,4},{3,1},{4,2},{5,7},{6,0},{7,5},{8,14},{9,11},{10,... | collective-permute-start | bytes 1572872 | tf_op jit(solution)/shard_map/ppermute | solution.py:82
  24.8 8.3 %collective-permute-start.4 = (bf16[2048,128]{1,0:T(8,128)(2,1)S(1)}, bf16[2048,128]{1,0:T(8,128)(2,1)S(1)}, u32[]{:S(2)}, u32[]{:S(2)}) collective-permute-start(bf16[2048,128]{1,0:T(8,128)(2,1)S(1)} %bitcast.6), channel_id=1, source_target_pairs={{0,96},{1,33},{2,98},{3,35},{4,100},{5,37},{6,102},{7,39},{8,104},... | collective-permute-start | bytes 1572872 | tf_op jit(solution)/shard_map/ppermute | solution.py:82
  24.8 9.8 %collective-permute-start.3 = (bf16[2048,128]{1,0:T(8,128)(2,1)S(1)}, bf16[2048,128]{1,0:T(8,128)(2,1)S(1)}, u32[]{:S(2)}, u32[]{:S(2)}) collective-permute-start(bf16[2048,128]{1,0:T(8,128)(2,1)S(1)} %bitcast.7), channel_id=1, source_target_pairs={{0,24},{1,9},{2,26},{3,11},{4,28},{5,13},{6,30},{7,15},{8,16},{9,1... | collective-permute-start | bytes 1572872 | tf_op jit(solution)/shard_map/ppermute | solution.py:82
  33.2 8.3 %collective-permute-start.5 = (bf16[2048,128]{1,0:T(8,128)(2,1)S(1)}, bf16[2048,128]{1,0:T(8,128)(2,1)S(1)}, u32[]{:S(2)}, u32[]{:S(2)}) collective-permute-start(bf16[2048,128]{1,0:T(8,128)(2,1)S(1)} %collective-permute-done.2.x_ref.refs_1_), channel_id=1, source_target_pairs={{0,24},{1,9},{2,26},{3,11},{4,28},{5,13},{6,30},{7,15},{8,16},{9,1... | collective-permute-start | bytes 1572872 | tf_op jit(solution)/shard_map/ppermute | solution.py:82
  33.2 10.5 %collective-permute-start.6 = (bf16[2048,128]{1,0:T(8,128)(2,1)S(1)}, bf16[2048,128]{1,0:T(8,128)(2,1)S(1)}, u32[]{:S(2)}, u32[]{:S(2)}) collective-permute-start(bf16[2048,128]{1,0:T(8,128)(2,1)S(1)} %collective-permute-done.4.z_ref.refs_4_), channel_id=1, source_target_pairs={{0,6},{1,3},{2,4},{3,1},{4,2},{5,7},{6,0},{7,5},{8,14},{9,11},{10,... | collective-permute-start | bytes 1572872 | tf_op jit(solution)/shard_map/ppermute | solution.py:82
  34.6 9.0 %collective-permute-start.7 = (bf16[2048,128]{1,0:T(8,128)(2,1)S(1)}, bf16[2048,128]{1,0:T(8,128)(2,1)S(1)}, u32[]{:S(2)}, u32[]{:S(2)}) collective-permute-start(bf16[2048,128]{1,0:T(8,128)(2,1)S(1)} %collective-permute-done.3.y_ref.refs_2_), channel_id=1, source_target_pairs={{0,96},{1,33},{2,98},{3,35},{4,100},{5,37},{6,102},{7,39},{8,104},... | collective-permute-start | bytes 1572872 | tf_op jit(solution)/shard_map/ppermute | solution.py:82
  34.6 1.6 %copy-start.1 = (bf16[1024,1024]{1,0:T(8,128)(2,1)S(1)}, bf16[1024,1024]{1,0:T(8,128)(2,1)}, u32[]{:S(2)}) copy-start(bf16[1024,1024]{1,0:T(8,128)(2,1)} %get-tuple-element.18.hi_ref) | copy-start | bytes 6291460
  36.2 1.6 %copy-start.2 = (bf16[1024,1024]{1,0:T(8,128)(2,1)S(1)}, bf16[1024,1024]{1,0:T(8,128)(2,1)}, u32[]{:S(2)}) copy-start(bf16[1024,1024]{1,0:T(8,128)(2,1)} %get-tuple-element.19.lo_ref) | copy-start | bytes 6291460
  37.8 3.9 %copy-start = (bf16[1024,1024]{1,0:T(8,128)(2,1)S(1)}, bf16[1024,1024]{1,0:T(8,128)(2,1)}, u32[]{:S(2)}) copy-start(bf16[1024,1024]{1,0:T(8,128)(2,1)} %get-tuple-element.16.mine_ref) | copy-start | bytes 6291460
  37.8 3.9 %copy-start.3 = (s32[64,16]{0,1:T(8,128)S(1)}, s32[64,16]{0,1:T(8,128)}, u32[]{:S(2)}) copy-start(s32[64,16]{0,1:T(8,128)} %param.8) | copy-start | bytes 12292
  37.8 3.9 %copy-start.4 = (s32[64,16]{0,1:T(8,128)S(1)}, s32[64,16]{0,1:T(8,128)}, u32[]{:S(2)}) copy-start(s32[64,16]{0,1:T(8,128)} %param.7) | copy-start | bytes 12292
  41.5 8.3 %collective-permute-start.8 = (bf16[2048,128]{1,0:T(8,128)(2,1)S(1)}, bf16[2048,128]{1,0:T(8,128)(2,1)S(1)}, u32[]{:S(2)}, u32[]{:S(2)}) collective-permute-start(bf16[2048,128]{1,0:T(8,128)(2,1)S(1)} %collective-permute-done.5.refs_3_), channel_id=1, source_target_pairs={{0,96},{1,33},{2,98},{3,35},{4,100},{5,37},{6,102},{7,39},{8,104},... | collective-permute-start | bytes 1572872 | tf_op jit(solution)/shard_map/ppermute | solution.py:82
  56.3 11.8 %collective-permute-start.9 = (bf16[512,1024]{1,0:T(8,128)(2,1)S(1)}, bf16[512,1024]{1,0:T(8,128)(2,1)S(1)}, u32[]{:S(2)}, u32[]{:S(2)}) collective-permute-start(bf16[512,1024]{1,0:T(8,128)(2,1)S(1)} %get-tuple-element.25), channel_id=1, source_target_pairs={{0,1},{1,0},{2,3},{3,2},{4,5},{5,4},{6,7},{7,6},{8,9},{9,8},{10,11... | collective-permute-start | bytes 3145736 | tf_op jit(solution)/shard_map/ppermute | solution.py:417

commit v4 on v3

--- a/solution.py
+++ b/solution.py
@@ -119,8 +119,8 @@
 
 
 def solve_kernel(
-    mine_hbm, other_hbm, coupling_hbm, after_ref, hi_out, lo_out, wide_out,
-    hi_ref, lo_ref, low_ref, coupling_ref, wide_ref, sems,
+    mine_hbm, other_hbm, coupling_hbm, after_ref, wide_out, square_out,
+    hi_ref, lo_ref, low_ref, coupling_ref, wide_ref, square_ref, sems,
 ):
     core = lax.axis_index("panel")
     mine, other = (pl.ds(pl.multiple_of(half * ROWS, ROWS), ROWS) for half in (core, 1 - core))
@@ -180,19 +180,21 @@
                 -(dot(hi, t_hi) + dot(hi, t_lo) + dot(lo, t_hi))
             )
         size *= 2
-    copies = [
-        pltpu.make_async_copy(hi_ref, hi_out, sems.at[3]),
-        pltpu.make_async_copy(lo_ref, lo_out, sems.at[4]),
-    ]
-    for copy in copies:
-        copy.start()
     fetches[2].wait()
     tile = 256
+    copies = []
     for n in range(0, SIDE, tile):
         columns = slice(n, n + tile)
         wide_ref[:, columns] = dot(coupling_ref[:, n:], hi_ref[n:, columns]).astype(BF16)
         copies.append(
-            pltpu.make_async_copy(wide_ref.at[:, columns], wide_out.at[:, columns], sems.at[5 + n // tile])
+            pltpu.make_async_copy(wide_ref.at[:, columns], wide_out.at[:, columns], sems.at[3 + n // tile])
+        )
+        copies[-1].start()
+    for n in range(0, SIDE, tile):
+        columns = slice(n, n + tile)
+        square_ref[:, columns] = dot_tn(hi_ref[n:, mine], hi_ref[n:, columns])
+        copies.append(
+            pltpu.make_async_copy(square_ref.at[:, columns], square_out.at[:, columns], sems.at[7 + n // tile])
         )
         copies[-1].start()
     for copy in copies:
@@ -200,14 +202,17 @@
 
 
 def solve(mine, other, coupling, after):
-    full = jax.ShapeDtypeStruct((SIDE, SIDE), BF16)
     return pl.pallas_call(
         solve_kernel,
-        out_shape=(full, full, full),
+        out_shape=(
+            jax.ShapeDtypeStruct((SIDE, SIDE), BF16),
+            jax.ShapeDtypeStruct((ROWS, SIDE), F32),
+        ),
         in_specs=[HBM, HBM, HBM, ANY],
-        out_specs=(HBM, HBM, HBM),
-        scratch_shapes=[pltpu.VMEM((SIDE, SIDE), BF16)] * 5 + [pltpu.SemaphoreType.DMA((9,))],
-        compiler_params=params(60),
+        out_specs=(HBM, HBM),
+        scratch_shapes=[pltpu.VMEM((SIDE, SIDE), BF16)] * 5
+        + [pltpu.VMEM((ROWS, SIDE), F32), pltpu.SemaphoreType.DMA((11,))],
+        compiler_params=params(58),
         cost_estimate=cost(4 << 30, 12 << 20),
         name="solve",
     )(
@@ -218,29 +223,7 @@
     )
 
 
-def square_kernel(hi_ref, lo_ref, x_ref, y_ref, z_ref, square_ref):
-    mine = pl.ds(pl.multiple_of(lax.axis_index("panel") * ROWS, ROWS), ROWS)
-    tile = 256
-    for n in range(0, SIDE, tile):
-        columns = slice(n, n + tile)
-        hi, lo = hi_ref[n:, columns], lo_ref[n:, columns]
-        left = hi_ref[n:, mine]
-        square_ref[:, columns] = dot_tn(left, hi) + dot_tn(left, lo) + dot_tn(lo_ref[n:, mine], hi)
-
-
-def make_square(hi, lo, after):
-    return pl.pallas_call(
-        square_kernel,
-        out_shape=jax.ShapeDtypeStruct((ROWS, SIDE), F32),
-        in_specs=[VMEM, VMEM, ANY, ANY, ANY],
-        out_specs=VMEM,
-        compiler_params=params(10),
-        cost_estimate=cost(1 << 20, 1 << 16),
-        name="make_square",
-    )(hi, lo, *after)
-
-
-def turn_kernel(list_ref, slots_ref, mine_ref, other_ref, x_ref, y_ref, z_ref, square_ref, out_ref, table_ref):
+def turn_kernel(list_ref, slots_ref, mine_ref, other_ref, x_ref, y_ref, z_ref, out_ref, table_ref):
     core, group = lax.axis_index("panel"), lax.axis_index("front")
     ids = slots_ref[...]
     rows = [
@@ -276,7 +259,7 @@
             jax.ShapeDtypeStruct((SIDE, SIDE), BF16),
             jax.ShapeDtypeStruct((HALF, 64), jnp.int32),
         ),
-        in_specs=[SMEM, VMEM, VMEM, VMEM, ANY, ANY, ANY, ANY],
+        in_specs=[SMEM, VMEM, VMEM, VMEM, ANY, ANY, ANY],
         out_specs=(VMEM, VMEM),
         compiler_params=params(12),
         cost_estimate=cost(1 << 20, 1 << 16),
@@ -422,14 +405,12 @@
     sep_other = swap(sep_factor)
     picked = pick_strips(slots, anc_tiles)
     near = gather_cube(picked, 0)
-    hi, lo, wide_mine = solve(sep_factor, sep_other, coup_factor, picked)
+    wide_mine, square = solve(sep_factor, sep_other, coup_factor, picked)
     near, wide_mine = lax.optimization_barrier((near, wide_mine))
     x, y, z = across(near, 1), across(near, 2), across(near, 4)
     wide_other = swap(wide_mine)
     xy, yz, zx = across(x, 2), across(y, 4), across(z, 1)
-    square = make_square(hi, lo, (x, y, z))
-    xy, square = lax.optimization_barrier((xy, square))
-    turned, table = turn_wide(lists, slots, wide_mine, wide_other, (x, y, z, square))
+    turned, table = turn_wide(lists, slots, wide_mine, wide_other, (x, y, z))
     sigma = make_sigma(lists, table, (near, x, y, xy, z, zx, yz))
     carried, to_send, _ = carry(table, sigma, across(xy, 4), wide_mine, wide_other, turned)
     received = swap(to_send)

time: 70.2 us -> 68.8 us (0.980)
  waiting for transfers between devices: 14.8 us -> 17.6 us
  starting transfers between devices: 22.6 us -> 20.6 us
  local copies, waits for them, and re-layouts: 4.16 us -> 2.57 us
  Pallas kernels: 27.7 us -> 26.9 us
    ppermute x7, waiting for transfers between devices: 12.9 us -> 16.6 us  [across(): return lax.ppermute(x, AXES, pairs)]
    ppermute x3, starting transfers between devices: 11 us -> 9.12 us  [swap(): return lax.ppermute(x, 'panel', [(0, 1), (1, 0)])]
    unnamed x12, local copies, waits for them, and re-layouts: 4.16 us -> 2.57 us
    pallas_call x2 -> x1, Pallas kernels: 11.4 us -> 10.2 us  [solve(): pl.pallas_call(solve_kernel, out_shape=(jax.ShapeDtypeStruct((SIDE, SIDE)...]
    all_to_all x1, waiting for transfers between devices: 0.84 us -> 0.01 us  [gather_cube(): lax.all_to_all(parts, AXES, split_axis=0, concat_axis=0, tiled=True, axis...]
  transfers between devices with their start and end apart: 11 -> 11, of which waited for: 5 -> 5; matrix products, arithmetic and copies ran while one was open for 0% -> 0% of each run, Pallas kernels for 28% -> 27%
where the time goes in v4:
time: 68.8 us; the launch traced here: 68.5 us
  Pallas kernels  26.9 us (39%)
  starting transfers between devices  20.6 us (30%)
  waiting for transfers between devices  17.6 us (26%)
  local copies, waits for them, and re-layouts  2.57 us (4%)
  between operations  0.79 us (1%)
    ppermute x7, waiting for transfers between devices, across(): return lax.ppermute(x, AXES, pairs)  16.6 us
    pallas_call x1, Pallas kernels, solve(): pl.pallas_call(solve_kernel, out_shape=(jax.ShapeDtypeStruct((SIDE, SIDE)...  10.2 us
    all_to_all x1, starting transfers between devices, gather_cube(): lax.all_to_all(parts, AXES, split_axis=0, concat_axis=0, tiled=True, axis...  9.77 us
    ppermute x3, starting transfers between devices, swap(): return lax.ppermute(x, 'panel', [(0, 1), (1, 0)])  9.12 us
    pallas_call x1, Pallas kernels, carry(): pl.pallas_call(carry_kernel, out_shape=(jax.ShapeDtypeStruct((SIDE, SIDE)...  6.45 us
    pallas_call x1, Pallas kernels, make_sigma(): pl.pallas_call(sigma_kernel, out_shape=SIGMA, in_specs=[SMEM, SMEM] + [VM...  2.75 us
    unnamed x12, local copies, waits for them, and re-layouts  2.57 us
    pallas_call x1, Pallas kernels, turn_wide(): pl.pallas_call(turn_kernel, out_shape=(jax.ShapeDtypeStruct((SIDE, SIDE),...  2.28 us
  transfers between devices with their start and end apart: 11, of which 5 were waited for; matrix products, arithmetic and copies ran while one was open for 0% of the time, Pallas kernels for 27%

profile of v4, /device:TPU:1, one launch (start us, length us, event | category | flops | bytes accessed | tf_op | source)
XLA Modules:
  0.0 68.5 jit_solution(6064922544088394478)
XLA Ops:
  0.6 1.5 %collective-permute-start = (bf16[512,1024]{1,0:T(8,128)(2,1)}, bf16[512,1024]{1,0:T(8,128)(2,1)S(1)}, u32[]{:S(2)}, u32[]{:S(2)}) collective-permute-start(bf16[512,1024]{1,0:T(8,128)(2,1)} %mine_hbm.1), channel_id=1, source_target_pairs={{0,1},{1,0},{2,3},{3,2},{4,5},{5,4},{6,7},{7,6},{8,9},{9,8},{10,11... | collective-permute-start | bytes 3145736 | tf_op jit(solution)/shard_map/ppermute | solution.py:400
  2.1 2.0 %pick_strips.1.after_ref = bf16[2048,128]{1,0:T(8,128)(2,1)} custom-call(s32[16,64]{1,0:T(8,128)} %bitcast.9, bf16[512,128]{1,0:T(8,128)(2,1)} %strips_hbm.1), custom_call_target="tpu_custom_call" | custom-call | bytes 1048576 | tf_op jit(solution)/shard_map/pick_strips/pallas_call | solution.py:105
  4.1 9.8 %all-to-all-start = ((bf16[8,256,128]{2,1,0:T(8,128)(2,1)}), bf16[8,256,128]{2,1,0:T(8,128)(2,1)S(1)}, u32[]{:S(2)}, u32[]{:S(2)}) async-start(bf16[8,256,128]{2,1,0:T(8,128)(2,1)} %bitcast.2), calls=%async_computation | async-start | bytes 1048576 | tf_op jit(solution)/shard_map/all_to_all | solution.py:71
  13.9 0.0 copy-start.3
  13.9 0.0 copy-start.4
  13.9 0.0 collective-permute-done.other_hbm
  13.9 0.0 copy-start.5
  13.9 1.0 %copy-done.5 = bf16[512,1024]{1,0:T(8,128)(2,1)} copy-done((bf16[512,1024]{1,0:T(8,128)(2,1)}, bf16[512,1024]{1,0:T(8,128)(2,1)S(1)}, u32[]{:S(2)}) %copy-start.5) | copy-done | bytes 1048600
  14.9 10.2 %solve.1 = (bf16[1024,1024]{1,0:T(8,128)(2,1)}, f32[512,1024]{1,0:T(8,128)}) custom-call(bf16[512,1024]{1,0:T(8,128)(2,1)} %mine_hbm.1, bf16[512,1024]{1,0:T(8,128)(2,1)} %copy-done.5, bf16[1024,1024]{1,0:T(8,128)(2,1)} %coupling_hbm.1, bf16[2048,128]{1,0:T(8,128)(2,1)} %pick_strips.1.after_ref), custom_call_target="tpu_custom_call" | custom-call | flops 8589934592 | bytes 12582912 | tf_op jit(solution)/shard_map/solve/pallas_call | solution.py:205
  25.2 0.0 all-to-all-done
  25.2 0.1 collective-permute-start.1
  25.3 0.1 collective-permute-start.2
  25.3 0.1 collective-permute-start.4
  25.4 0.1 collective-permute-start.3
  25.5 8.1 %collective-permute-done.2.x_ref.refs_1_ = bf16[2048,128]{1,0:T(8,128)(2,1)S(1)} collective-permute-done((bf16[2048,128]{1,0:T(8,128)(2,1)S(1)}, bf16[2048,128]{1,0:T(8,128)(2,1)S(1)}, u32[]{:S(2)}, u32[]{:S(2)}) %collective-permute-start.2) | collective-permute-done | bytes 524320 | tf_op jit(solution)/shard_map/ppermute | solution.py:82
  33.7 0.0 collective-permute-start.5
  33.7 0.1 collective-permute-done.4.z_ref.refs_4_
  33.8 1.4 %collective-permute-start.6 = (bf16[2048,128]{1,0:T(8,128)(2,1)S(1)}, bf16[2048,128]{1,0:T(8,128)(2,1)S(1)}, u32[]{:S(2)}, u32[]{:S(2)}) collective-permute-start(bf16[2048,128]{1,0:T(8,128)(2,1)S(1)} %collective-permute-done.4.z_ref.refs_4_), channel_id=1, source_target_pairs={{0,6},{1,3},{2,4},{3,1},{4,2},{5,7},{6,0},{7,5},{8,14},{9,11},{10,... | collective-permute-start | bytes 1572872 | tf_op jit(solution)/shard_map/ppermute | solution.py:82
  35.1 0.0 collective-permute-done.3.y_ref.refs_2_
  35.1 0.1 collective-permute-start.7
  35.2 6.8 %collective-permute-done.5.refs_3_ = bf16[2048,128]{1,0:T(8,128)(2,1)S(1)} collective-permute-done((bf16[2048,128]{1,0:T(8,128)(2,1)S(1)}, bf16[2048,128]{1,0:T(8,128)(2,1)S(1)}, u32[]{:S(2)}, u32[]{:S(2)}) %collective-permute-start.5) | collective-permute-done | bytes 524320 | tf_op jit(solution)/shard_map/ppermute | solution.py:82
  42.0 0.0 collective-permute-start.8
  42.0 0.0 collective-permute-done.1.other_ref
  42.0 0.0 copy-done.3
  42.0 0.0 copy-done.4
  42.0 0.0 copy-start.1
  42.0 1.6 %copy-done.1 = bf16[1024,1024]{1,0:T(8,128)(2,1)S(1)} copy-done((bf16[1024,1024]{1,0:T(8,128)(2,1)S(1)}, bf16[1024,1024]{1,0:T(8,128)(2,1)}, u32[]{:S(2)}) %copy-start.1) | copy-done | bytes 2097176
  43.6 2.3 %turn_wide.1 = (bf16[1024,1024]{1,0:T(8,128)(2,1)S(1)}, s32[8,64]{1,0:T(8,128)S(1)}) custom-call(s32[16,64]{1,0:T(8,128)S(1)} %bitcast.11, s32[16,64]{1,0:T(8,128)S(1)} %bitcast.10, bf16[1024,1024]{1,0:T(8,128)(2,1)S(1)} %copy-done.1, bf16[1024,1024]{1,0:T(8,128)(2,1)S(1)} %collective-permute-done.1.other_ref, ...), custom_call_target="tpu_custom_call" | custom-call | flops 2097152 | bytes 65536 | tf_op jit(solution)/shard_map/turn_wide/pallas_call | solution.py:256
  45.9 0.0 collective-permute-done.6.refs_5_
  45.9 0.0 collective-permute-done.7.refs_6_
  45.9 0.0 copy-start.2
  45.9 2.8 %make_sigma.1.sigma_in_ref = bf16[17408,128]{1,0:T(8,128)(2,1)S(1)} custom-call(s32[16,64]{1,0:T(8,128)S(1)} %bitcast.12, s32[8,64]{1,0:T(8,128)S(1)} %get-tuple-element.16.table_ref, bf16[2048,128]{1,0:T(8,128)(2,1)S(1)} %bitcast.8, bf16[2048,128]{1,0:T(8,128)(2,1)S(1)} %collective-permute-done.2.x_ref.refs_1_, ...), custom_call_target="tpu_custom_call" | custom-call | flops 2097152 | bytes 65536 | tf_op jit(solution)/shard_map/make_sigma/pallas_call | solution.py:303
  48.7 1.6 %collective-permute-done.8.strips_ref = bf16[2048,128]{1,0:T(8,128)(2,1)S(1)} collective-permute-done((bf16[2048,128]{1,0:T(8,128)(2,1)S(1)}, bf16[2048,128]{1,0:T(8,128)(2,1)S(1)}, u32[]{:S(2)}, u32[]{:S(2)}) %collective-permute-start.8) | collective-permute-done | bytes 524320 | tf_op jit(solution)/shard_map/ppermute | solution.py:82
  50.3 0.0 copy-done.2
  50.3 0.0 copy-start
  50.3 6.5 %carry.1 = (bf16[1024,1024]{1,0:T(8,128)(2,1)S(1)}, bf16[512,1024]{1,0:T(8,128)(2,1)S(1)}, bf16[17408,128]{1,0:T(8,128)(2,1)S(1)}) custom-call(s32[8,64]{1,0:T(8,128)S(1)} %get-tuple-element.16.table_ref, bf16[17408,128]{1,0:T(8,128)(2,1)S(1)} %make_sigma.1.sigma_in_ref, ...), custom_call_target="tpu_custom_call", output_to_operand_aliasing={{2}: (1, {})} | custom-call | flops 5368709120 | bytes 12582912 | tf_op jit(solution)/shard_map/carry/pallas_call | solution.py:337
  56.8 7.5 %collective-permute-start.9 = (bf16[512,1024]{1,0:T(8,128)(2,1)S(1)}, bf16[512,1024]{1,0:T(8,128)(2,1)S(1)}, u32[]{:S(2)}, u32[]{:S(2)}) collective-permute-start(bf16[512,1024]{1,0:T(8,128)(2,1)S(1)} %get-tuple-element.19), channel_id=1, source_target_pairs={{0,1},{1,0},{2,3},{3,2},{4,5},{5,4},{6,7},{7,6},{8,9},{9,8},{10,11... | collective-permute-start | bytes 3145736 | tf_op jit(solution)/shard_map/ppermute | solution.py:400
  64.3 0.0 copy-done
  64.3 1.3 %own_product.1.own_ref = f32[512,1024]{1,0:T(8,128)S(1)} custom-call(bf16[1024,1024]{1,0:T(8,128)(2,1)S(1)} %get-tuple-element.15.turned_ref, bf16[1024,1024]{1,0:T(8,128)(2,1)S(1)} %get-tuple-element.17.carried_ref, f32[512,1024]{1,0:T(8,128)S(1)} %copy-done), custom_call_target="tpu_custom_call" | custom-call | flops 1073741824 | bytes 8388608 | tf_op jit(solution)/shard_map/own_product/pallas_call | solution.py:362
  65.6 1.0 %collective-permute-done.9.received_ref = bf16[512,1024]{1,0:T(8,128)(2,1)S(1)} collective-permute-done((bf16[512,1024]{1,0:T(8,128)(2,1)S(1)}, bf16[512,1024]{1,0:T(8,128)(2,1)S(1)}, u32[]{:S(2)}, u32[]{:S(2)}) %collective-permute-start.9) | collective-permute-done | bytes 1048608 | tf_op jit(solution)/shard_map/ppermute | solution.py:400
  66.6 1.9 %finish.1 = (f32[512,1024]{1,0:T(8,128)}, f32[1,512]{1,0:T(1,128)}) custom-call(f32[512,1024]{1,0:T(8,128)S(1)} %own_product.1.own_ref, bf16[512,1024]{1,0:T(8,128)(2,1)S(1)} %collective-permute-done.9.received_ref), custom_call_target="tpu_custom_call" | custom-call | bytes 6291456 | tf_op jit(solution)/shard_map/finish/pallas_call | solution.py:384
Async XLA Ops:
  0.6 13.3 %collective-permute-start = (bf16[512,1024]{1,0:T(8,128)(2,1)}, bf16[512,1024]{1,0:T(8,128)(2,1)S(1)}, u32[]{:S(2)}, u32[]{:S(2)}) collective-permute-start(bf16[512,1024]{1,0:T(8,128)(2,1)} %mine_hbm.1), channel_id=1, source_target_pairs={{0,1},{1,0},{2,3},{3,2},{4,5},{5,4},{6,7},{7,6},{8,9},{9,8},{10,11... | collective-permute-start | bytes 3145736 | tf_op jit(solution)/shard_map/ppermute | solution.py:400
  4.1 21.0 %all-to-all-start = ((bf16[8,256,128]{2,1,0:T(8,128)(2,1)}), bf16[8,256,128]{2,1,0:T(8,128)(2,1)S(1)}, u32[]{:S(2)}, u32[]{:S(2)}) async-start(bf16[8,256,128]{2,1,0:T(8,128)(2,1)} %bitcast.2), calls=%async_computation | async-start | bytes 1048576 | tf_op jit(solution)/shard_map/all_to_all | solution.py:71
  13.9 28.1 %copy-start.3 = (s32[64,16]{0,1:T(8,128)S(1)}, s32[64,16]{0,1:T(8,128)}, u32[]{:S(2)}) copy-start(s32[64,16]{0,1:T(8,128)} %param.8) | copy-start | bytes 12292
  13.9 28.1 %copy-start.4 = (s32[64,16]{0,1:T(8,128)S(1)}, s32[64,16]{0,1:T(8,128)}, u32[]{:S(2)}) copy-start(s32[64,16]{0,1:T(8,128)} %param.7) | copy-start | bytes 12292
  13.9 1.0 %copy-start.5 = (bf16[512,1024]{1,0:T(8,128)(2,1)}, bf16[512,1024]{1,0:T(8,128)(2,1)S(1)}, u32[]{:S(2)}) copy-start(bf16[512,1024]{1,0:T(8,128)(2,1)S(1)} %collective-permute-done.other_hbm) | copy-start | bytes 3145732
  25.2 16.8 %collective-permute-start.1 = (bf16[1024,1024]{1,0:T(8,128)(2,1)}, bf16[1024,1024]{1,0:T(8,128)(2,1)S(1)}, u32[]{:S(2)}, u32[]{:S(2)}) collective-permute-start(bf16[1024,1024]{1,0:T(8,128)(2,1)} %get-tuple-element.13.mine_ref), channel_id=1, source_target_pairs={{0,1},{1,0},{2,3},{3,2},{4,5},{5,4},{6,7},{7,6},{8,9},{9,8},{10,11... | collective-permute-start | bytes 6291464 | tf_op jit(solution)/shard_map/ppermute | solution.py:400
  25.3 8.4 %collective-permute-start.2 = (bf16[2048,128]{1,0:T(8,128)(2,1)S(1)}, bf16[2048,128]{1,0:T(8,128)(2,1)S(1)}, u32[]{:S(2)}, u32[]{:S(2)}) collective-permute-start(bf16[2048,128]{1,0:T(8,128)(2,1)S(1)} %bitcast.5), channel_id=1, source_target_pairs={{0,6},{1,3},{2,4},{3,1},{4,2},{5,7},{6,0},{7,5},{8,14},{9,11},{10,... | collective-permute-start | bytes 1572872 | tf_op jit(solution)/shard_map/ppermute | solution.py:82
  25.3 8.4 %collective-permute-start.4 = (bf16[2048,128]{1,0:T(8,128)(2,1)S(1)}, bf16[2048,128]{1,0:T(8,128)(2,1)S(1)}, u32[]{:S(2)}, u32[]{:S(2)}) collective-permute-start(bf16[2048,128]{1,0:T(8,128)(2,1)S(1)} %bitcast.6), channel_id=1, source_target_pairs={{0,96},{1,33},{2,98},{3,35},{4,100},{5,37},{6,102},{7,39},{8,104},... | collective-permute-start | bytes 1572872 | tf_op jit(solution)/shard_map/ppermute | solution.py:82
  25.4 9.7 %collective-permute-start.3 = (bf16[2048,128]{1,0:T(8,128)(2,1)S(1)}, bf16[2048,128]{1,0:T(8,128)(2,1)S(1)}, u32[]{:S(2)}, u32[]{:S(2)}) collective-permute-start(bf16[2048,128]{1,0:T(8,128)(2,1)S(1)} %bitcast.7), channel_id=1, source_target_pairs={{0,24},{1,9},{2,26},{3,11},{4,28},{5,13},{6,30},{7,15},{8,16},{9,1... | collective-permute-start | bytes 1572872 | tf_op jit(solution)/shard_map/ppermute | solution.py:82
  33.7 8.3 %collective-permute-start.5 = (bf16[2048,128]{1,0:T(8,128)(2,1)S(1)}, bf16[2048,128]{1,0:T(8,128)(2,1)S(1)}, u32[]{:S(2)}, u32[]{:S(2)}) collective-permute-start(bf16[2048,128]{1,0:T(8,128)(2,1)S(1)} %collective-permute-done.2.x_ref.refs_1_), channel_id=1, source_target_pairs={{0,24},{1,9},{2,26},{3,11},{4,28},{5,13},{6,30},{7,15},{8,16},{9,1... | collective-permute-start | bytes 1572872 | tf_op jit(solution)/shard_map/ppermute | solution.py:82
  33.8 12.1 %collective-permute-start.6 = (bf16[2048,128]{1,0:T(8,128)(2,1)S(1)}, bf16[2048,128]{1,0:T(8,128)(2,1)S(1)}, u32[]{:S(2)}, u32[]{:S(2)}) collective-permute-start(bf16[2048,128]{1,0:T(8,128)(2,1)S(1)} %collective-permute-done.4.z_ref.refs_4_), channel_id=1, source_target_pairs={{0,6},{1,3},{2,4},{3,1},{4,2},{5,7},{6,0},{7,5},{8,14},{9,11},{10,... | collective-permute-start | bytes 1572872 | tf_op jit(solution)/shard_map/ppermute | solution.py:82
  35.1 10.8 %collective-permute-start.7 = (bf16[2048,128]{1,0:T(8,128)(2,1)S(1)}, bf16[2048,128]{1,0:T(8,128)(2,1)S(1)}, u32[]{:S(2)}, u32[]{:S(2)}) collective-permute-start(bf16[2048,128]{1,0:T(8,128)(2,1)S(1)} %collective-permute-done.3.y_ref.refs_2_), channel_id=1, source_target_pairs={{0,96},{1,33},{2,98},{3,35},{4,100},{5,37},{6,102},{7,39},{8,104},... | collective-permute-start | bytes 1572872 | tf_op jit(solution)/shard_map/ppermute | solution.py:82
  42.0 8.3 %collective-permute-start.8 = (bf16[2048,128]{1,0:T(8,128)(2,1)S(1)}, bf16[2048,128]{1,0:T(8,128)(2,1)S(1)}, u32[]{:S(2)}, u32[]{:S(2)}) collective-permute-start(bf16[2048,128]{1,0:T(8,128)(2,1)S(1)} %collective-permute-done.5.refs_3_), channel_id=1, source_target_pairs={{0,96},{1,33},{2,98},{3,35},{4,100},{5,37},{6,102},{7,39},{8,104},... | collective-permute-start | bytes 1572872 | tf_op jit(solution)/shard_map/ppermute | solution.py:82
  42.0 1.6 %copy-start.1 = (bf16[1024,1024]{1,0:T(8,128)(2,1)S(1)}, bf16[1024,1024]{1,0:T(8,128)(2,1)}, u32[]{:S(2)}) copy-start(bf16[1024,1024]{1,0:T(8,128)(2,1)} %get-tuple-element.13.mine_ref) | copy-start | bytes 6291460
  45.9 4.4 %copy-start.2 = (bf16[1024,1024]{1,0:T(8,128)(2,1)S(1)}, bf16[1024,1024]{1,0:T(8,128)(2,1)}, u32[]{:S(2)}) copy-start(bf16[1024,1024]{1,0:T(8,128)(2,1)} %get-tuple-element.13.mine_ref) | copy-start | bytes 6291460
  50.3 14.0 %copy-start = (f32[512,1024]{1,0:T(8,128)S(1)}, f32[512,1024]{1,0:T(8,128)}, u32[]{:S(2)}) copy-start(f32[512,1024]{1,0:T(8,128)} %get-tuple-element.18.square_ref) | copy-start | bytes 6291460
  56.8 9.8 %collective-permute-start.9 = (bf16[512,1024]{1,0:T(8,128)(2,1)S(1)}, bf16[512,1024]{1,0:T(8,128)(2,1)S(1)}, u32[]{:S(2)}, u32[]{:S(2)}) collective-permute-start(bf16[512,1024]{1,0:T(8,128)(2,1)S(1)} %get-tuple-element.19), channel_id=1, source_target_pairs={{0,1},{1,0},{2,3},{3,2},{4,5},{5,4},{6,7},{7,6},{8,9},{9,8},{10,11... | collective-permute-start | bytes 3145736 | tf_op jit(solution)/shard_map/ppermute | solution.py:400

commit v5 on v4

--- a/solution.py
+++ b/solution.py
@@ -82,14 +82,18 @@
     return lax.ppermute(x, AXES, pairs)
 
 
-def pick_kernel(slots_hbm, strips_hbm, out_ref, slots_ref, held_ref, sems):
+def pick_kernel(slots_hbm, lists_hbm, strips_hbm, out_ref, table_ref, slots_ref, list_ref, ids_ref, held_ref, sems):
     core, group = lax.axis_index("panel"), lax.axis_index("front")
-    table = pltpu.make_async_copy(slots_hbm, slots_ref, sems.at[0])
-    fetch = pltpu.make_async_copy(strips_hbm, held_ref, sems.at[1])
-    table.start()
-    fetch.start()
-    table.wait()
-    fetch.wait()
+    fetches = [
+        pltpu.make_async_copy(slots_hbm, slots_ref, sems.at[0]),
+        pltpu.make_async_copy(strips_hbm, held_ref, sems.at[1]),
+        pltpu.make_async_copy(lists_hbm, list_ref, sems.at[2]),
+        pltpu.make_async_copy(slots_hbm, ids_ref, sems.at[3]),
+    ]
+    for fetch in fetches:
+        fetch.start()
+    for fetch in fetches:
+        fetch.wait()
     for slot in range(NABOVE):
         row = slots_ref[slot, group] // 64 - core * HALF
 
@@ -100,41 +104,45 @@
                 at = pl.multiple_of(copy * HALF * STRIP + row * STRIP, STRIP)
                 out_ref[pl.ds(at, STRIP), :] = strip
 
-
-def pick_strips(slots, strips):
+    ids = ids_ref[...]
+    rows = [
+        jnp.sum(jnp.where((ids >> 6) == core * HALF + row, ids & 63, 0), axis=0, keepdims=True)
+        for row in range(HALF)
+    ]
+    places = jnp.concatenate(rows, axis=0)
+    column = jnp.full(places.shape, NABOVE, jnp.int32)
+    for a in range(NABOVE):
+        column = jnp.where((places >> 2) == list_ref[a, group], a ^ (core * HALF), column)
+    row = lax.broadcasted_iota(jnp.int32, places.shape, 0)
+    table_ref[...] = column * SIDE + row * BLOCK + (places & 3) * STRIP
+
+
+def pick_strips(slots, lists, strips):
     return pl.pallas_call(
         pick_kernel,
-        out_shape=jax.ShapeDtypeStruct((8 * HALF * STRIP, BLOCK), BF16),
-        in_specs=[HBM, HBM],
-        out_specs=VMEM,
+        out_shape=(
+            jax.ShapeDtypeStruct((8 * HALF * STRIP, BLOCK), BF16),
+            jax.ShapeDtypeStruct((HALF, 64), jnp.int32),
+        ),
+        in_specs=[HBM, HBM, HBM],
+        out_specs=(VMEM, VMEM),
         scratch_shapes=[
             pltpu.SMEM((NABOVE, 64), jnp.int32),
+            pltpu.SMEM((NABOVE, 64), jnp.int32),
+            pltpu.VMEM((NABOVE, 64), jnp.int32),
             pltpu.VMEM((NABOVE * STRIP, BLOCK), BF16),
-            pltpu.SemaphoreType.DMA((2,)),
+            pltpu.SemaphoreType.DMA((4,)),
         ],
         compiler_params=params(4),
         cost_estimate=cost(0, 1 << 20),
         name="pick_strips",
-    )(*(pltpu.with_memory_space_constraint(x, pltpu.HBM) for x in (slots, strips)))
-
-
-def solve_kernel(
-    mine_hbm, other_hbm, coupling_hbm, after_ref, wide_out, square_out,
-    hi_ref, lo_ref, low_ref, coupling_ref, wide_ref, square_ref, sems,
-):
+    )(*(pltpu.with_memory_space_constraint(x, pltpu.HBM) for x in (slots, lists, strips)))
+
+
+def blocks_kernel(mine_ref, other_ref, after_ref, hi_ref, lo_ref, low_ref):
     core = lax.axis_index("panel")
-    mine, other = (pl.ds(pl.multiple_of(half * ROWS, ROWS), ROWS) for half in (core, 1 - core))
-    fetches = [
-        pltpu.make_async_copy(mine_hbm, low_ref.at[mine], sems.at[0]),
-        pltpu.make_async_copy(other_hbm, low_ref.at[other], sems.at[1]),
-        pltpu.make_async_copy(coupling_hbm, coupling_ref, sems.at[2]),
-    ]
-    for fetch in fetches:
-        fetch.start()
-    hi_ref[...] = jnp.zeros_like(hi_ref)
-    lo_ref[...] = jnp.zeros_like(lo_ref)
-    fetches[0].wait()
-    fetches[1].wait()
+    low_ref[pl.ds(pl.multiple_of(core * ROWS, ROWS), ROWS), :] = mine_ref[...]
+    low_ref[pl.ds(pl.multiple_of((1 - core) * ROWS, ROWS), ROWS), :] = other_ref[...]
     row = lax.broadcasted_iota(jnp.int32, (BLOCK, BLOCK), 0)
     col = lax.broadcasted_iota(jnp.int32, (BLOCK, BLOCK), 1)
     differ = row ^ col
@@ -169,7 +177,36 @@
         size *= 2
     for b in range(8):
         at = slice(b * BLOCK, (b + 1) * BLOCK)
-        hi_ref[at, at], lo_ref[at, at] = split(inverses[b])
+        hi_ref[at, :], lo_ref[at, :] = split(inverses[b])
+
+
+def invert_blocks(mine, other, after):
+    slim = jax.ShapeDtypeStruct((SIDE, BLOCK), BF16)
+    return pl.pallas_call(
+        blocks_kernel,
+        out_shape=(
+            slim,
+            slim,
+            jax.ShapeDtypeStruct((SIDE, SIDE), BF16),
+        ),
+        in_specs=[VMEM, VMEM, ANY],
+        out_specs=(VMEM, VMEM, VMEM),
+        compiler_params=params(12),
+        cost_estimate=cost(1 << 20, 1 << 16),
+        name="invert_blocks",
+    )(mine, other, after)
+
+
+def solve_kernel(
+    hi_slim_ref, lo_slim_ref, low_ref, coupling_ref, x_ref, y_ref, z_ref, wide_ref, square_ref, hi_ref, lo_ref
+):
+    mine = pl.ds(pl.multiple_of(lax.axis_index("panel") * ROWS, ROWS), ROWS)
+    hi_ref[...] = jnp.zeros_like(hi_ref)
+    lo_ref[...] = jnp.zeros_like(lo_ref)
+    for b in range(8):
+        at = slice(b * BLOCK, (b + 1) * BLOCK)
+        hi_ref[at, at], lo_ref[at, at] = hi_slim_ref[at, :], lo_slim_ref[at, :]
+    size = BLOCK
     while size < SIDE:
         for start in range(0, SIDE, 2 * size):
             first, second = slice(start, start + size), slice(start + size, start + 2 * size)
@@ -180,62 +217,33 @@
                 -(dot(hi, t_hi) + dot(hi, t_lo) + dot(lo, t_hi))
             )
         size *= 2
-    fetches[2].wait()
     tile = 256
-    copies = []
     for n in range(0, SIDE, tile):
         columns = slice(n, n + tile)
         wide_ref[:, columns] = dot(coupling_ref[:, n:], hi_ref[n:, columns]).astype(BF16)
-        copies.append(
-            pltpu.make_async_copy(wide_ref.at[:, columns], wide_out.at[:, columns], sems.at[3 + n // tile])
-        )
-        copies[-1].start()
     for n in range(0, SIDE, tile):
         columns = slice(n, n + tile)
         square_ref[:, columns] = dot_tn(hi_ref[n:, mine], hi_ref[n:, columns])
-        copies.append(
-            pltpu.make_async_copy(square_ref.at[:, columns], square_out.at[:, columns], sems.at[7 + n // tile])
-        )
-        copies[-1].start()
-    for copy in copies:
-        copy.wait()
-
-
-def solve(mine, other, coupling, after):
+
+
+def solve(hi, lo, low, coupling, after):
     return pl.pallas_call(
         solve_kernel,
         out_shape=(
             jax.ShapeDtypeStruct((SIDE, SIDE), BF16),
             jax.ShapeDtypeStruct((ROWS, SIDE), F32),
         ),
-        in_specs=[HBM, HBM, HBM, ANY],
-        out_specs=(HBM, HBM),
-        scratch_shapes=[pltpu.VMEM((SIDE, SIDE), BF16)] * 5
-        + [pltpu.VMEM((ROWS, SIDE), F32), pltpu.SemaphoreType.DMA((11,))],
-        compiler_params=params(58),
-        cost_estimate=cost(4 << 30, 12 << 20),
+        in_specs=[VMEM, VMEM, VMEM, VMEM, ANY, ANY, ANY],
+        out_specs=(VMEM, VMEM),
+        scratch_shapes=[pltpu.VMEM((SIDE, SIDE), BF16)] * 2,
+        compiler_params=params(20),
+        cost_estimate=cost(1 << 20, 1 << 16),
         name="solve",
-    )(
-        pltpu.with_memory_space_constraint(mine, pltpu.HBM),
-        other,
-        pltpu.with_memory_space_constraint(coupling, pltpu.HBM),
-        after,
-    )
-
-
-def turn_kernel(list_ref, slots_ref, mine_ref, other_ref, x_ref, y_ref, z_ref, out_ref, table_ref):
+    )(hi, lo, low, coupling, *after)
+
+
+def turn_kernel(list_ref, mine_ref, other_ref, out_ref):
     core, group = lax.axis_index("panel"), lax.axis_index("front")
-    ids = slots_ref[...]
-    rows = [
-        jnp.sum(jnp.where((ids >> 6) == core * HALF + row, ids & 63, 0), axis=0, keepdims=True)
-        for row in range(HALF)
-    ]
-    places = jnp.concatenate(rows, axis=0)
-    column = jnp.full(places.shape, NABOVE, jnp.int32)
-    for a in range(NABOVE):
-        column = jnp.where((places >> 2) == list_ref[a, group], a ^ (core * HALF), column)
-    row = lax.broadcasted_iota(jnp.int32, places.shape, 0)
-    table_ref[...] = column * SIDE + row * BLOCK + (places & 3) * STRIP
     out_ref[...] = jnp.zeros_like(out_ref)
     for a in range(NABOVE):
         owner, at = a // HALF, (a % HALF) * BLOCK
@@ -252,19 +260,16 @@
             out_ref[:, columns] = other_ref[at : at + BLOCK, :].astype(F32).T.astype(BF16)
 
 
-def turn_wide(lists, slots, mine, other, after):
+def turn_wide(lists, mine, other):
     return pl.pallas_call(
         turn_kernel,
-        out_shape=(
-            jax.ShapeDtypeStruct((SIDE, SIDE), BF16),
-            jax.ShapeDtypeStruct((HALF, 64), jnp.int32),
-        ),
-        in_specs=[SMEM, VMEM, VMEM, VMEM, ANY, ANY, ANY],
-        out_specs=(VMEM, VMEM),
+        out_shape=jax.ShapeDtypeStruct((SIDE, SIDE), BF16),
+        in_specs=[SMEM, VMEM, VMEM],
+        out_specs=VMEM,
         compiler_params=params(12),
-        cost_estimate=cost(1 << 20, 1 << 16),
+        cost_estimate=cost(0, 8 << 20),
         name="turn_wide",
-    )(lists, slots, mine, other, *after)
+    )(lists, mine, other)
 
 
 def place_strips(table_ref, sigma_ref, strips_ref, bits):
@@ -306,7 +311,7 @@
         in_specs=[SMEM, SMEM] + [VMEM] * 7,
         out_specs=VMEM,
         compiler_params=params(12),
-        cost_estimate=cost(1 << 20, 1 << 16),
+        cost_estimate=cost(0, 10 << 20),
         name="make_sigma",
     )(lists, table, *strips)
 
@@ -403,14 +408,16 @@
 def on_device(sep_factor, coup_factor, coup_list, slot_tiles, anc_tiles):
     lists, slots = coup_list.T, slot_tiles.T
     sep_other = swap(sep_factor)
-    picked = pick_strips(slots, anc_tiles)
+    picked, table = pick_strips(slots, lists, anc_tiles)
     near = gather_cube(picked, 0)
-    wide_mine, square = solve(sep_factor, sep_other, coup_factor, picked)
-    near, wide_mine = lax.optimization_barrier((near, wide_mine))
+    hi, lo, low = invert_blocks(sep_factor, sep_other, near)
     x, y, z = across(near, 1), across(near, 2), across(near, 4)
+    x, y, z, hi = lax.optimization_barrier((x, y, z, hi))
+    xy, yz, zx = across(x, 2), across(y, 4), across(z, 1)
+    wide_mine, square = solve(hi, lo, low, coup_factor, (x, y, z))
+    xy, yz, zx, wide_mine, square = lax.optimization_barrier((xy, yz, zx, wide_mine, square))
     wide_other = swap(wide_mine)
-    xy, yz, zx = across(x, 2), across(y, 4), across(z, 1)
-    turned, table = turn_wide(lists, slots, wide_mine, wide_other, (x, y, z))
+    turned = turn_wide(lists, wide_mine, wide_other)
     sigma = make_sigma(lists, table, (near, x, y, xy, z, zx, yz))
     carried, to_send, _ = carry(table, sigma, across(xy, 4), wide_mine, wide_other, turned)
     received = swap(to_send)

time: 68.8 us -> 65.6 us (0.953)
  blocking collectives: 0 us -> 20.5 us
  starting transfers between devices: 20.6 us -> 7.53 us
  waiting for transfers between devices: 17.6 us -> 11.6 us
  Pallas kernels: 26.9 us -> 23.8 us
  local copies, waits for them, and re-layouts: 2.57 us -> 1.23 us
    all_to_all x0 -> x1, blocking collectives: none -> 20.5 us  [gather_cube(): lax.all_to_all(parts, AXES, split_axis=0, concat_axis=0, tiled=True, axis...]
    all_to_all x1 -> x0, starting transfers between devices: 9.77 us -> none  [gather_cube(): lax.all_to_all(parts, AXES, split_axis=0, concat_axis=0, tiled=True, axis...]
    ppermute x7, waiting for transfers between devices: 16.6 us -> 9.55 us  [across(): return lax.ppermute(x, AXES, pairs)]
    pallas_call x1, Pallas kernels: 10.2 us -> 5.1 us  [solve(): pl.pallas_call(solve_kernel, out_shape=(jax.ShapeDtypeStruct((SIDE, SIDE)...]
    ppermute x3, starting transfers between devices: 9.12 us -> 4.57 us  [swap(): return lax.ppermute(x, 'panel', [(0, 1), (1, 0)])]
    pallas_call x2 -> x3, Pallas kernels: 4.26 us -> 6.46 us  [the longest x1 2.59 us: invert_blocks(): pl.pallas_call(blocks_kernel, out_shape=(slim, slim, jax.ShapeDtypeStruct...]
    unnamed x12 -> x6, local copies, waits for them, and re-layouts: 2.57 us -> 1.23 us
    ppermute x7, starting transfers between devices: 1.72 us -> 2.96 us  [across(): return lax.ppermute(x, AXES, pairs)]
  transfers between devices with their start and end apart: 11 -> 10, of which waited for: 5 -> 7; matrix products, arithmetic and copies ran while one was open for 0% -> 0% of each run, Pallas kernels for 27% -> 24%
where the time goes in v5:
time: 65.6 us; the launch traced here: 65.4 us
  Pallas kernels  23.8 us (36%)
  blocking collectives  20.5 us (31%)
  waiting for transfers between devices  11.6 us (18%)
  starting transfers between devices  7.53 us (11%)
  local copies, waits for them, and re-layouts  1.23 us (2%)
  between operations  0.72 us (1%)
    all_to_all x1, blocking collectives, gather_cube(): lax.all_to_all(parts, AXES, split_axis=0, concat_axis=0, tiled=True, axis...  20.5 us
    ppermute x7, waiting for transfers between devices, across(): return lax.ppermute(x, AXES, pairs)  9.55 us
    pallas_call x1, Pallas kernels, carry(): pl.pallas_call(carry_kernel, out_shape=(jax.ShapeDtypeStruct((SIDE, SIDE)...  6.44 us
    pallas_call x1, Pallas kernels, solve(): pl.pallas_call(solve_kernel, out_shape=(jax.ShapeDtypeStruct((SIDE, SIDE)...  5.1 us
    ppermute x3, starting transfers between devices, swap(): return lax.ppermute(x, 'panel', [(0, 1), (1, 0)])  4.57 us
    ppermute x7, starting transfers between devices, across(): return lax.ppermute(x, AXES, pairs)  2.96 us
    pallas_call x1, Pallas kernels, make_sigma(): pl.pallas_call(sigma_kernel, out_shape=SIGMA, in_specs=[SMEM, SMEM] + [VM...  2.68 us
    pallas_call x1, Pallas kernels, invert_blocks(): pl.pallas_call(blocks_kernel, out_shape=(slim, slim, jax.ShapeDtypeStruct...  2.59 us
  transfers between devices with their start and end apart: 10, of which 7 were waited for; matrix products, arithmetic and copies ran while one was open for 0% of the time, Pallas kernels for 24%

profile of v5, /device:TPU:1, one launch (start us, length us, event | category | flops | bytes accessed | tf_op | source)
XLA Modules:
  0.0 65.4 jit_solution(14444366772610858076)
XLA Ops:
  0.6 0.0 copy-start
  0.6 1.5 %collective-permute-start.3 = (bf16[512,1024]{1,0:T(8,128)(2,1)}, bf16[512,1024]{1,0:T(8,128)(2,1)S(1)}, u32[]{:S(2)}, u32[]{:S(2)}) collective-permute-start(bf16[512,1024]{1,0:T(8,128)(2,1)} %mine_ref.1), channel_id=1, source_target_pairs={{0,1},{1,0},{2,3},{3,2},{4,5},{5,4},{6,7},{7,6},{8,9},{9,8},{10,11... | collective-permute-start | bytes 3145736 | tf_op jit(solution)/shard_map/ppermute | solution.py:405
  2.1 1.5 %pick_strips.1 = (bf16[2048,128]{1,0:T(8,128)(2,1)S(1)}, s32[8,64]{1,0:T(8,128)S(1)}) custom-call(s32[16,64]{1,0:T(8,128)} %bitcast.14, s32[16,64]{1,0:T(8,128)} %bitcast.11, bf16[512,128]{1,0:T(8,128)(2,1)} %strips_hbm.1), custom_call_target="tpu_custom_call" | custom-call | bytes 1048576 | tf_op jit(solution)/shard_map/pick_strips/pallas_call | solution.py:121
  3.6 20.5 %all_to_all.11 = bf16[8,256,128]{2,1,0:T(8,128)(2,1)S(1)} all-to-all(bf16[8,256,128]{2,1,0:T(8,128)(2,1)S(1)} %bitcast.10), channel_id=1, replica_groups={{0,2,8,10,32,34,40,42},{4,6,12,14,36,38,44,46},{16,18,24,26,48,50,56,58..., dimensions={0} | all-to-all | bytes 1048576 | tf_op jit(solution)/shard_map/all_to_all | solution.py:71
  24.1 0.0 collective-permute-start.2
  24.1 0.0 collective-permute-start.1
  24.1 0.0 collective-permute-start
  24.1 0.0 collective-permute-done.3.other_ref
  24.1 0.0 copy-start.1
  24.1 1.2 %copy-done.1 = bf16[512,1024]{1,0:T(8,128)(2,1)S(1)} copy-done((bf16[512,1024]{1,0:T(8,128)(2,1)S(1)}, bf16[512,1024]{1,0:T(8,128)(2,1)}, u32[]{:S(2)}) %copy-start.1) | copy-done | bytes 1048600
  25.3 2.6 %invert_blocks.1 = (bf16[1024,128]{1,0:T(8,128)(2,1)S(1)}, bf16[1024,128]{1,0:T(8,128)(2,1)S(1)}, bf16[1024,1024]{1,0:T(8,128)(2,1)S(1)}) custom-call(bf16[512,1024]{1,0:T(8,128)(2,1)S(1)} %copy-done.1, bf16[512,1024]{1,0:T(8,128)(2,1)S(1)} %collective-permute-done.3.other_ref, bf16[2048,128]{1,0:T(8,128)(2,1)S(1)} %bitcast.8), custom_call_target="tpu_custom_call" | custom-call | flops 2097152 | bytes 65536 | tf_op jit(solution)/shard_map/invert_blocks/pallas_call | solution.py:185
  27.9 4.2 %collective-permute-done.2.z_ref.refs_4_ = bf16[2048,128]{1,0:T(8,128)(2,1)S(1)} collective-permute-done((bf16[2048,128]{1,0:T(8,128)(2,1)S(1)}, bf16[2048,128]{1,0:T(8,128)(2,1)S(1)}, u32[]{:S(2)}, u32[]{:S(2)}) %collective-permute-start.2) | collective-permute-done | bytes 524320 | tf_op jit(solution)/shard_map/ppermute | solution.py:82
  32.1 0.0 collective-permute-done.1.y_ref.refs_2_
  32.1 0.0 collective-permute-done.x_ref.refs_1_
  32.1 1.5 %collective-permute-start.4 = (bf16[2048,128]{1,0:T(8,128)(2,1)S(1)}, bf16[2048,128]{1,0:T(8,128)(2,1)S(1)}, u32[]{:S(2)}, u32[]{:S(2)}) collective-permute-start(bf16[2048,128]{1,0:T(8,128)(2,1)S(1)} %collective-permute-done.x_ref.refs_1_), channel_id=1, source_target_pairs={{0,24},{1,9},{2,26},{3,11},{4,28},{5,13},{6,30},{7,15},{8,16},{9,1... | collective-permute-start | bytes 1572872 | tf_op jit(solution)/shard_map/ppermute | solution.py:82
  33.6 1.5 %collective-permute-start.5 = (bf16[2048,128]{1,0:T(8,128)(2,1)S(1)}, bf16[2048,128]{1,0:T(8,128)(2,1)S(1)}, u32[]{:S(2)}, u32[]{:S(2)}) collective-permute-start(bf16[2048,128]{1,0:T(8,128)(2,1)S(1)} %collective-permute-done.1.y_ref.refs_2_), channel_id=1, source_target_pairs={{0,96},{1,33},{2,98},{3,35},{4,100},{5,37},{6,102},{7,39},{8,104},... | collective-permute-start | bytes 1572872 | tf_op jit(solution)/shard_map/ppermute | solution.py:82
  35.1 0.0 collective-permute-start.6
  35.1 0.0 copy-done
  35.1 0.0 copy-start.2
  35.1 5.1 %solve.1 = (bf16[1024,1024]{1,0:T(8,128)(2,1)S(1)}, f32[512,1024]{1,0:T(8,128)S(1)}) custom-call(bf16[1024,128]{1,0:T(8,128)(2,1)S(1)} %get-tuple-element.27.hi_slim_ref, bf16[1024,128]{1,0:T(8,128)(2,1)S(1)} %get-tuple-element.28.lo_slim_ref, bf16[1024,1024]{1,0:T(8,128)(2,1)S(1)} %get-tuple-element.29.low_ref, bf16[1024,1024]{1,0:T(8,128)(2,1)S(1)} %copy-done, ...), custom_call_target="tpu_custom_call" | custom-call | flops 2097152 | bytes 65536 | tf_op jit(solution)/shard_map/solve/pallas_call | solution.py:230
  40.2 0.3 collective-permute-done.4.refs_3_
  40.5 1.5 %collective-permute-done.5.refs_6_ = bf16[2048,128]{1,0:T(8,128)(2,1)S(1)} collective-permute-done((bf16[2048,128]{1,0:T(8,128)(2,1)S(1)}, bf16[2048,128]{1,0:T(8,128)(2,1)S(1)}, u32[]{:S(2)}, u32[]{:S(2)}) %collective-permute-start.5) | collective-permute-done | bytes 524320 | tf_op jit(solution)/shard_map/ppermute | solution.py:82
  41.9 1.5 %collective-permute-done.6.refs_5_ = bf16[2048,128]{1,0:T(8,128)(2,1)S(1)} collective-permute-done((bf16[2048,128]{1,0:T(8,128)(2,1)S(1)}, bf16[2048,128]{1,0:T(8,128)(2,1)S(1)}, u32[]{:S(2)}, u32[]{:S(2)}) %collective-permute-start.6) | collective-permute-done | bytes 524320 | tf_op jit(solution)/shard_map/ppermute | solution.py:82
  43.4 0.9 %collective-permute-start.7 = (bf16[1024,1024]{1,0:T(8,128)(2,1)S(1)}, bf16[1024,1024]{1,0:T(8,128)(2,1)S(1)}, u32[]{:S(2)}, u32[]{:S(2)}) collective-permute-start(bf16[1024,1024]{1,0:T(8,128)(2,1)S(1)} %get-tuple-element.32.mine_ref), channel_id=1, source_target_pairs={{0,1},{1,0},{2,3},{3,2},{4,5},{5,4},{6,7},{7,6},{8,9},{9,8},{10,11... | collective-permute-start | bytes 6291464 | tf_op jit(solution)/shard_map/ppermute | solution.py:405
  44.3 0.0 collective-permute-start.8
  44.3 0.0 copy-done.2
  44.3 2.7 %make_sigma.1.sigma_in_ref = bf16[17408,128]{1,0:T(8,128)(2,1)S(1)} custom-call(s32[16,64]{1,0:T(8,128)S(1)} %bitcast.12, s32[8,64]{1,0:T(8,128)S(1)} %get-tuple-element.33.table_ref, bf16[2048,128]{1,0:T(8,128)(2,1)S(1)} %bitcast.9, bf16[2048,128]{1,0:T(8,128)(2,1)S(1)} %collective-permute-done.x_ref.refs_1_, ...), custom_call_target="tpu_custom_call" | custom-call | bytes 10485760 | tf_op jit(solution)/shard_map/make_sigma/pallas_call | solution.py:308
  47.0 1.1 %collective-permute-done.7.other_ref = bf16[1024,1024]{1,0:T(8,128)(2,1)S(1)} collective-permute-done((bf16[1024,1024]{1,0:T(8,128)(2,1)S(1)}, bf16[1024,1024]{1,0:T(8,128)(2,1)S(1)}, u32[]{:S(2)}, u32[]{:S(2)}) %collective-permute-start.7) | collective-permute-done | bytes 2097184 | tf_op jit(solution)/shard_map/ppermute | solution.py:405
  48.1 2.4 %turn_wide.1.turned_ref = bf16[1024,1024]{1,0:T(8,128)(2,1)S(1)} custom-call(s32[16,64]{1,0:T(8,128)S(1)} %bitcast.13, bf16[1024,1024]{1,0:T(8,128)(2,1)S(1)} %get-tuple-element.32.mine_ref, bf16[1024,1024]{1,0:T(8,128)(2,1)S(1)} %collective-permute-done.7.other_ref), custom_call_target="tpu_custom_call" | custom-call | bytes 8388608 | tf_op jit(solution)/shard_map/turn_wide/pallas_call | solution.py:264
  50.5 2.1 %collective-permute-done.8.strips_ref = bf16[2048,128]{1,0:T(8,128)(2,1)S(1)} collective-permute-done((bf16[2048,128]{1,0:T(8,128)(2,1)S(1)}, bf16[2048,128]{1,0:T(8,128)(2,1)S(1)}, u32[]{:S(2)}, u32[]{:S(2)}) %collective-permute-start.8) | collective-permute-done | bytes 524320 | tf_op jit(solution)/shard_map/ppermute | solution.py:82
  52.6 6.4 %carry.1 = (bf16[1024,1024]{1,0:T(8,128)(2,1)S(1)}, bf16[512,1024]{1,0:T(8,128)(2,1)S(1)}, bf16[17408,128]{1,0:T(8,128)(2,1)S(1)}) custom-call(s32[8,64]{1,0:T(8,128)S(1)} %get-tuple-element.33.table_ref, bf16[17408,128]{1,0:T(8,128)(2,1)S(1)} %make_sigma.1.sigma_in_ref, ...), custom_call_target="tpu_custom_call", output_to_operand_aliasing={{2}: (1, {})} | custom-call | flops 5368709120 | bytes 12582912 | tf_op jit(solution)/shard_map/carry/pallas_call | solution.py:342
  59.1 2.1 %collective-permute-start.9 = (bf16[512,1024]{1,0:T(8,128)(2,1)S(1)}, bf16[512,1024]{1,0:T(8,128)(2,1)S(1)}, u32[]{:S(2)}, u32[]{:S(2)}) collective-permute-start(bf16[512,1024]{1,0:T(8,128)(2,1)S(1)} %get-tuple-element.39), channel_id=1, source_target_pairs={{0,1},{1,0},{2,3},{3,2},{4,5},{5,4},{6,7},{7,6},{8,9},{9,8},{10,11... | collective-permute-start | bytes 3145736 | tf_op jit(solution)/shard_map/ppermute | solution.py:405
  61.2 1.2 %own_product.1.own_ref = f32[512,1024]{1,0:T(8,128)S(1)} custom-call(bf16[1024,1024]{1,0:T(8,128)(2,1)S(1)} %turn_wide.1.turned_ref, bf16[1024,1024]{1,0:T(8,128)(2,1)S(1)} %get-tuple-element.37.carried_ref, f32[512,1024]{1,0:T(8,128)S(1)} %get-tuple-element.38.square_ref), custom_call_target="tpu_custom_call" | custom-call | flops 1073741824 | bytes 8388608 | tf_op jit(solution)/shard_map/own_product/pallas_call | solution.py:367
  62.5 1.0 %collective-permute-done.9.received_ref = bf16[512,1024]{1,0:T(8,128)(2,1)S(1)} collective-permute-done((bf16[512,1024]{1,0:T(8,128)(2,1)S(1)}, bf16[512,1024]{1,0:T(8,128)(2,1)S(1)}, u32[]{:S(2)}, u32[]{:S(2)}) %collective-permute-start.9) | collective-permute-done | bytes 1048608 | tf_op jit(solution)/shard_map/ppermute | solution.py:405
  63.5 1.9 %finish.1 = (f32[512,1024]{1,0:T(8,128)}, f32[1,512]{1,0:T(1,128)}) custom-call(f32[512,1024]{1,0:T(8,128)S(1)} %own_product.1.own_ref, bf16[512,1024]{1,0:T(8,128)(2,1)S(1)} %collective-permute-done.9.received_ref), custom_call_target="tpu_custom_call" | custom-call | bytes 6291456 | tf_op jit(solution)/shard_map/finish/pallas_call | solution.py:389
Async XLA Ops:
  0.6 34.4 %copy-start = (bf16[1024,1024]{1,0:T(8,128)(2,1)S(1)}, bf16[1024,1024]{1,0:T(8,128)(2,1)}, u32[]{:S(2)}) copy-start(bf16[1024,1024]{1,0:T(8,128)(2,1)} %coupling_ref.1) | copy-start | bytes 6291460
  0.6 23.5 %collective-permute-start.3 = (bf16[512,1024]{1,0:T(8,128)(2,1)}, bf16[512,1024]{1,0:T(8,128)(2,1)S(1)}, u32[]{:S(2)}, u32[]{:S(2)}) collective-permute-start(bf16[512,1024]{1,0:T(8,128)(2,1)} %mine_ref.1), channel_id=1, source_target_pairs={{0,1},{1,0},{2,3},{3,2},{4,5},{5,4},{6,7},{7,6},{8,9},{9,8},{10,11... | collective-permute-start | bytes 3145736 | tf_op jit(solution)/shard_map/ppermute | solution.py:405
  24.1 8.0 %collective-permute-start.2 = (bf16[2048,128]{1,0:T(8,128)(2,1)S(1)}, bf16[2048,128]{1,0:T(8,128)(2,1)S(1)}, u32[]{:S(2)}, u32[]{:S(2)}) collective-permute-start(bf16[2048,128]{1,0:T(8,128)(2,1)S(1)} %bitcast.5), channel_id=1, source_target_pairs={{0,96},{1,33},{2,98},{3,35},{4,100},{5,37},{6,102},{7,39},{8,104},... | collective-permute-start | bytes 1572872 | tf_op jit(solution)/shard_map/ppermute | solution.py:82
  24.1 8.0 %collective-permute-start.1 = (bf16[2048,128]{1,0:T(8,128)(2,1)S(1)}, bf16[2048,128]{1,0:T(8,128)(2,1)S(1)}, u32[]{:S(2)}, u32[]{:S(2)}) collective-permute-start(bf16[2048,128]{1,0:T(8,128)(2,1)S(1)} %bitcast.6), channel_id=1, source_target_pairs={{0,24},{1,9},{2,26},{3,11},{4,28},{5,13},{6,30},{7,15},{8,16},{9,1... | collective-permute-start | bytes 1572872 | tf_op jit(solution)/shard_map/ppermute | solution.py:82
  24.1 8.0 %collective-permute-start = (bf16[2048,128]{1,0:T(8,128)(2,1)S(1)}, bf16[2048,128]{1,0:T(8,128)(2,1)S(1)}, u32[]{:S(2)}, u32[]{:S(2)}) collective-permute-start(bf16[2048,128]{1,0:T(8,128)(2,1)S(1)} %bitcast.7), channel_id=1, source_target_pairs={{0,6},{1,3},{2,4},{3,1},{4,2},{5,7},{6,0},{7,5},{8,14},{9,11},{10,... | collective-permute-start | bytes 1572872 | tf_op jit(solution)/shard_map/ppermute | solution.py:82
  24.1 1.2 %copy-start.1 = (bf16[512,1024]{1,0:T(8,128)(2,1)S(1)}, bf16[512,1024]{1,0:T(8,128)(2,1)}, u32[]{:S(2)}) copy-start(bf16[512,1024]{1,0:T(8,128)(2,1)} %mine_ref.1) | copy-start | bytes 3145732
  32.1 8.3 %collective-permute-start.4 = (bf16[2048,128]{1,0:T(8,128)(2,1)S(1)}, bf16[2048,128]{1,0:T(8,128)(2,1)S(1)}, u32[]{:S(2)}, u32[]{:S(2)}) collective-permute-start(bf16[2048,128]{1,0:T(8,128)(2,1)S(1)} %collective-permute-done.x_ref.refs_1_), channel_id=1, source_target_pairs={{0,24},{1,9},{2,26},{3,11},{4,28},{5,13},{6,30},{7,15},{8,16},{9,1... | collective-permute-start | bytes 1572872 | tf_op jit(solution)/shard_map/ppermute | solution.py:82
  33.6 8.3 %collective-permute-start.5 = (bf16[2048,128]{1,0:T(8,128)(2,1)S(1)}, bf16[2048,128]{1,0:T(8,128)(2,1)S(1)}, u32[]{:S(2)}, u32[]{:S(2)}) collective-permute-start(bf16[2048,128]{1,0:T(8,128)(2,1)S(1)} %collective-permute-done.1.y_ref.refs_2_), channel_id=1, source_target_pairs={{0,96},{1,33},{2,98},{3,35},{4,100},{5,37},{6,102},{7,39},{8,104},... | collective-permute-start | bytes 1572872 | tf_op jit(solution)/shard_map/ppermute | solution.py:82
  35.1 8.3 %collective-permute-start.6 = (bf16[2048,128]{1,0:T(8,128)(2,1)S(1)}, bf16[2048,128]{1,0:T(8,128)(2,1)S(1)}, u32[]{:S(2)}, u32[]{:S(2)}) collective-permute-start(bf16[2048,128]{1,0:T(8,128)(2,1)S(1)} %collective-permute-done.2.z_ref.refs_4_), channel_id=1, source_target_pairs={{0,6},{1,3},{2,4},{3,1},{4,2},{5,7},{6,0},{7,5},{8,14},{9,11},{10,... | collective-permute-start | bytes 1572872 | tf_op jit(solution)/shard_map/ppermute | solution.py:82
  35.1 9.3 %copy-start.2 = (s32[64,16]{0,1:T(8,128)S(1)}, s32[64,16]{0,1:T(8,128)}, u32[]{:S(2)}) copy-start(s32[64,16]{0,1:T(8,128)} %param.7) | copy-start | bytes 12292
  43.4 4.7 %collective-permute-start.7 = (bf16[1024,1024]{1,0:T(8,128)(2,1)S(1)}, bf16[1024,1024]{1,0:T(8,128)(2,1)S(1)}, u32[]{:S(2)}, u32[]{:S(2)}) collective-permute-start(bf16[1024,1024]{1,0:T(8,128)(2,1)S(1)} %get-tuple-element.32.mine_ref), channel_id=1, source_target_pairs={{0,1},{1,0},{2,3},{3,2},{4,5},{5,4},{6,7},{7,6},{8,9},{9,8},{10,11... | collective-permute-start | bytes 6291464 | tf_op jit(solution)/shard_map/ppermute | solution.py:405
  44.3 8.3 %collective-permute-start.8 = (bf16[2048,128]{1,0:T(8,128)(2,1)S(1)}, bf16[2048,128]{1,0:T(8,128)(2,1)S(1)}, u32[]{:S(2)}, u32[]{:S(2)}) collective-permute-start(bf16[2048,128]{1,0:T(8,128)(2,1)S(1)} %collective-permute-done.4.refs_3_), channel_id=1, source_target_pairs={{0,96},{1,33},{2,98},{3,35},{4,100},{5,37},{6,102},{7,39},{8,104},... | collective-permute-start | bytes 1572872 | tf_op jit(solution)/shard_map/ppermute | solution.py:82
  59.1 4.4 %collective-permute-start.9 = (bf16[512,1024]{1,0:T(8,128)(2,1)S(1)}, bf16[512,1024]{1,0:T(8,128)(2,1)S(1)}, u32[]{:S(2)}, u32[]{:S(2)}) collective-permute-start(bf16[512,1024]{1,0:T(8,128)(2,1)S(1)} %get-tuple-element.39), channel_id=1, source_target_pairs={{0,1},{1,0},{2,3},{3,2},{4,5},{5,4},{6,7},{7,6},{8,9},{9,8},{10,11... | collective-permute-start | bytes 3145736 | tf_op jit(solution)/shard_map/ppermute | solution.py:405

commit v6 on v5

--- a/solution.py
+++ b/solution.py
@@ -412,7 +412,7 @@
     near = gather_cube(picked, 0)
     hi, lo, low = invert_blocks(sep_factor, sep_other, near)
     x, y, z = across(near, 1), across(near, 2), across(near, 4)
-    x, y, z, hi = lax.optimization_barrier((x, y, z, hi))
+    z, hi = lax.optimization_barrier((z, hi))
     xy, yz, zx = across(x, 2), across(y, 4), across(z, 1)
     wide_mine, square = solve(hi, lo, low, coup_factor, (x, y, z))
     xy, yz, zx, wide_mine, square = lax.optimization_barrier((xy, yz, zx, wide_mine, square))

time: 65.6 us -> 67.8 us (1.034)
  waiting for transfers between devices: 11.6 us -> 15.3 us
  starting transfers between devices: 7.53 us -> 6.23 us
    ppermute x7, waiting for transfers between devices: 9.55 us -> 13.4 us  [across(): return lax.ppermute(x, AXES, pairs)]
    ppermute x7, starting transfers between devices: 2.96 us -> 2.08 us  [across(): return lax.ppermute(x, AXES, pairs)]
  transfers between devices with their start and end apart: 10 -> 10, of which waited for: 7 -> 5; matrix products, arithmetic and copies ran while one was open for 0% -> 0% of each run, Pallas kernels for 24% -> 23%
where the time goes in v6:
time: 67.8 us; the launch traced here: 67.6 us
  Pallas kernels  23.6 us (35%)
  blocking collectives  20.5 us (30%)
  waiting for transfers between devices  15.3 us (23%)
  starting transfers between devices  6.23 us (9%)
  local copies, waits for them, and re-layouts  1.24 us (2%)
  between operations  0.75 us (1%)
    all_to_all x1, blocking collectives, gather_cube(): lax.all_to_all(parts, AXES, split_axis=0, concat_axis=0, tiled=True, axis...  20.5 us
    ppermute x7, waiting for transfers between devices, across(): return lax.ppermute(x, AXES, pairs)  13.4 us
    pallas_call x1, Pallas kernels, carry(): pl.pallas_call(carry_kernel, out_shape=(jax.ShapeDtypeStruct((SIDE, SIDE)...  6.44 us
    pallas_call x1, Pallas kernels, solve(): pl.pallas_call(solve_kernel, out_shape=(jax.ShapeDtypeStruct((SIDE, SIDE)...  5.11 us
    ppermute x3, starting transfers between devices, swap(): return lax.ppermute(x, 'panel', [(0, 1), (1, 0)])  4.16 us
    pallas_call x1, Pallas kernels, make_sigma(): pl.pallas_call(sigma_kernel, out_shape=SIGMA, in_specs=[SMEM, SMEM] + [VM...  2.75 us
    pallas_call x1, Pallas kernels, invert_blocks(): pl.pallas_call(blocks_kernel, out_shape=(slim, slim, jax.ShapeDtypeStruct...  2.59 us
    pallas_call x1, Pallas kernels, turn_wide(): pl.pallas_call(turn_kernel, out_shape=jax.ShapeDtypeStruct((SIDE, SIDE),...  2.11 us
  transfers between devices with their start and end apart: 10, of which 5 were waited for; matrix products, arithmetic and copies ran while one was open for 0% of the time, Pallas kernels for 23%

profile of v6, /device:TPU:1, one launch (start us, length us, event | category | flops | bytes accessed | tf_op | source)
XLA Modules:
  0.0 67.6 jit_solution(2652373849362659330)
XLA Ops:
  0.6 0.0 copy-start
  0.6 1.5 %collective-permute-start.5 = (bf16[512,1024]{1,0:T(8,128)(2,1)}, bf16[512,1024]{1,0:T(8,128)(2,1)S(1)}, u32[]{:S(2)}, u32[]{:S(2)}) collective-permute-start(bf16[512,1024]{1,0:T(8,128)(2,1)} %mine_ref.1), channel_id=1, source_target_pairs={{0,1},{1,0},{2,3},{3,2},{4,5},{5,4},{6,7},{7,6},{8,9},{9,8},{10,11... | collective-permute-start | bytes 3145736 | tf_op jit(solution)/shard_map/ppermute | solution.py:405
  2.1 1.5 %pick_strips.1 = (bf16[2048,128]{1,0:T(8,128)(2,1)S(1)}, s32[8,64]{1,0:T(8,128)S(1)}) custom-call(s32[16,64]{1,0:T(8,128)} %bitcast.14, s32[16,64]{1,0:T(8,128)} %bitcast.11, bf16[512,128]{1,0:T(8,128)(2,1)} %strips_hbm.1), custom_call_target="tpu_custom_call" | custom-call | bytes 1048576 | tf_op jit(solution)/shard_map/pick_strips/pallas_call | solution.py:121
  3.6 20.5 %all_to_all.11 = bf16[8,256,128]{2,1,0:T(8,128)(2,1)S(1)} all-to-all(bf16[8,256,128]{2,1,0:T(8,128)(2,1)S(1)} %bitcast.10), channel_id=1, replica_groups={{0,2,8,10,32,34,40,42},{4,6,12,14,36,38,44,46},{16,18,24,26,48,50,56,58..., dimensions={0} | all-to-all | bytes 1048576 | tf_op jit(solution)/shard_map/all_to_all | solution.py:71
  24.2 0.0 collective-permute-start.2
  24.2 0.0 collective-permute-start
  24.2 0.0 collective-permute-start.4
  24.2 8.0 %collective-permute-done.2.y_ref.refs_2_ = bf16[2048,128]{1,0:T(8,128)(2,1)S(1)} collective-permute-done((bf16[2048,128]{1,0:T(8,128)(2,1)S(1)}, bf16[2048,128]{1,0:T(8,128)(2,1)S(1)}, u32[]{:S(2)}, u32[]{:S(2)}) %collective-permute-start.2) | collective-permute-done | bytes 524320 | tf_op jit(solution)/shard_map/ppermute | solution.py:82
  32.2 0.0 collective-permute-start.3
  32.2 0.0 collective-permute-done.x_ref.refs_1_
  32.2 1.8 %collective-permute-start.1 = (bf16[2048,128]{1,0:T(8,128)(2,1)S(1)}, bf16[2048,128]{1,0:T(8,128)(2,1)S(1)}, u32[]{:S(2)}, u32[]{:S(2)}) collective-permute-start(bf16[2048,128]{1,0:T(8,128)(2,1)S(1)} %collective-permute-done.x_ref.refs_1_), channel_id=1, source_target_pairs={{0,24},{1,9},{2,26},{3,11},{4,28},{5,13},{6,30},{7,15},{8,16},{9,1... | collective-permute-start | bytes 1572872 | tf_op jit(solution)/shard_map/ppermute | solution.py:82
  34.0 0.0 collective-permute-done.5.other_ref
  34.0 0.0 copy-start.1
  34.0 1.2 %copy-done.1 = bf16[512,1024]{1,0:T(8,128)(2,1)S(1)} copy-done((bf16[512,1024]{1,0:T(8,128)(2,1)S(1)}, bf16[512,1024]{1,0:T(8,128)(2,1)}, u32[]{:S(2)}) %copy-start.1) | copy-done | bytes 1048600
  35.2 2.6 %invert_blocks.1 = (bf16[1024,128]{1,0:T(8,128)(2,1)S(1)}, bf16[1024,128]{1,0:T(8,128)(2,1)S(1)}, bf16[1024,1024]{1,0:T(8,128)(2,1)S(1)}) custom-call(bf16[512,1024]{1,0:T(8,128)(2,1)S(1)} %copy-done.1, bf16[512,1024]{1,0:T(8,128)(2,1)S(1)} %collective-permute-done.5.other_ref, bf16[2048,128]{1,0:T(8,128)(2,1)S(1)} %bitcast.8), custom_call_target="tpu_custom_call" | custom-call | flops 2097152 | bytes 65536 | tf_op jit(solution)/shard_map/invert_blocks/pallas_call | solution.py:185
  37.8 0.0 collective-permute-done.4.z_ref.refs_4_
  37.8 0.1 collective-permute-start.6
  37.9 0.0 copy-done
  37.9 0.0 copy-start.2
  37.9 5.1 %solve.1 = (bf16[1024,1024]{1,0:T(8,128)(2,1)S(1)}, f32[512,1024]{1,0:T(8,128)S(1)}) custom-call(bf16[1024,128]{1,0:T(8,128)(2,1)S(1)} %get-tuple-element.23.hi_slim_ref, bf16[1024,128]{1,0:T(8,128)(2,1)S(1)} %get-tuple-element.24.lo_slim_ref, bf16[1024,1024]{1,0:T(8,128)(2,1)S(1)} %get-tuple-element.25.low_ref, bf16[1024,1024]{1,0:T(8,128)(2,1)S(1)} %copy-done, ...), custom_call_target="tpu_custom_call" | custom-call | flops 2097152 | bytes 65536 | tf_op jit(solution)/shard_map/solve/pallas_call | solution.py:230
  43.0 0.0 collective-permute-done.3.refs_6_
  43.0 0.0 collective-permute-done.1.refs_3_
  43.0 3.0 %collective-permute-done.6.refs_5_ = bf16[2048,128]{1,0:T(8,128)(2,1)S(1)} collective-permute-done((bf16[2048,128]{1,0:T(8,128)(2,1)S(1)}, bf16[2048,128]{1,0:T(8,128)(2,1)S(1)}, u32[]{:S(2)}, u32[]{:S(2)}) %collective-permute-start.6) | collective-permute-done | bytes 524320 | tf_op jit(solution)/shard_map/ppermute | solution.py:82
  46.0 0.4 collective-permute-start.7
  46.4 0.2 collective-permute-start.8
  46.7 0.0 copy-done.2
  46.7 2.7 %make_sigma.1.sigma_in_ref = bf16[17408,128]{1,0:T(8,128)(2,1)S(1)} custom-call(s32[16,64]{1,0:T(8,128)S(1)} %bitcast.12, s32[8,64]{1,0:T(8,128)S(1)} %get-tuple-element.29.table_ref, bf16[2048,128]{1,0:T(8,128)(2,1)S(1)} %bitcast.9, bf16[2048,128]{1,0:T(8,128)(2,1)S(1)} %collective-permute-done.x_ref.refs_1_, ...), custom_call_target="tpu_custom_call" | custom-call | bytes 10485760 | tf_op jit(solution)/shard_map/make_sigma/pallas_call | solution.py:308
  49.4 0.8 %collective-permute-done.7.other_ref = bf16[1024,1024]{1,0:T(8,128)(2,1)S(1)} collective-permute-done((bf16[1024,1024]{1,0:T(8,128)(2,1)S(1)}, bf16[1024,1024]{1,0:T(8,128)(2,1)S(1)}, u32[]{:S(2)}, u32[]{:S(2)}) %collective-permute-start.7) | collective-permute-done | bytes 2097184 | tf_op jit(solution)/shard_map/ppermute | solution.py:405
  50.2 2.1 %turn_wide.1.turned_ref = bf16[1024,1024]{1,0:T(8,128)(2,1)S(1)} custom-call(s32[16,64]{1,0:T(8,128)S(1)} %bitcast.13, bf16[1024,1024]{1,0:T(8,128)(2,1)S(1)} %get-tuple-element.28.mine_ref, bf16[1024,1024]{1,0:T(8,128)(2,1)S(1)} %collective-permute-done.7.other_ref), custom_call_target="tpu_custom_call" | custom-call | bytes 8388608 | tf_op jit(solution)/shard_map/turn_wide/pallas_call | solution.py:264
  52.3 2.4 %collective-permute-done.8.strips_ref = bf16[2048,128]{1,0:T(8,128)(2,1)S(1)} collective-permute-done((bf16[2048,128]{1,0:T(8,128)(2,1)S(1)}, bf16[2048,128]{1,0:T(8,128)(2,1)S(1)}, u32[]{:S(2)}, u32[]{:S(2)}) %collective-permute-start.8) | collective-permute-done | bytes 524320 | tf_op jit(solution)/shard_map/ppermute | solution.py:82
  54.7 6.4 %carry.1 = (bf16[1024,1024]{1,0:T(8,128)(2,1)S(1)}, bf16[512,1024]{1,0:T(8,128)(2,1)S(1)}, bf16[17408,128]{1,0:T(8,128)(2,1)S(1)}) custom-call(s32[8,64]{1,0:T(8,128)S(1)} %get-tuple-element.29.table_ref, bf16[17408,128]{1,0:T(8,128)(2,1)S(1)} %make_sigma.1.sigma_in_ref, ...), custom_call_target="tpu_custom_call", output_to_operand_aliasing={{2}: (1, {})} | custom-call | flops 5368709120 | bytes 12582912 | tf_op jit(solution)/shard_map/carry/pallas_call | solution.py:342
  61.2 2.3 %collective-permute-start.9 = (bf16[512,1024]{1,0:T(8,128)(2,1)S(1)}, bf16[512,1024]{1,0:T(8,128)(2,1)S(1)}, u32[]{:S(2)}, u32[]{:S(2)}) collective-permute-start(bf16[512,1024]{1,0:T(8,128)(2,1)S(1)} %get-tuple-element.35), channel_id=1, source_target_pairs={{0,1},{1,0},{2,3},{3,2},{4,5},{5,4},{6,7},{7,6},{8,9},{9,8},{10,11... | collective-permute-start | bytes 3145736 | tf_op jit(solution)/shard_map/ppermute | solution.py:405
  63.5 1.2 %own_product.1.own_ref = f32[512,1024]{1,0:T(8,128)S(1)} custom-call(bf16[1024,1024]{1,0:T(8,128)(2,1)S(1)} %turn_wide.1.turned_ref, bf16[1024,1024]{1,0:T(8,128)(2,1)S(1)} %get-tuple-element.33.carried_ref, f32[512,1024]{1,0:T(8,128)S(1)} %get-tuple-element.34.square_ref), custom_call_target="tpu_custom_call" | custom-call | flops 1073741824 | bytes 8388608 | tf_op jit(solution)/shard_map/own_product/pallas_call | solution.py:367
  64.7 1.0 %collective-permute-done.9.received_ref = bf16[512,1024]{1,0:T(8,128)(2,1)S(1)} collective-permute-done((bf16[512,1024]{1,0:T(8,128)(2,1)S(1)}, bf16[512,1024]{1,0:T(8,128)(2,1)S(1)}, u32[]{:S(2)}, u32[]{:S(2)}) %collective-permute-start.9) | collective-permute-done | bytes 1048608 | tf_op jit(solution)/shard_map/ppermute | solution.py:405
  65.7 1.9 %finish.1 = (f32[512,1024]{1,0:T(8,128)}, f32[1,512]{1,0:T(1,128)}) custom-call(f32[512,1024]{1,0:T(8,128)S(1)} %own_product.1.own_ref, bf16[512,1024]{1,0:T(8,128)(2,1)S(1)} %collective-permute-done.9.received_ref), custom_call_target="tpu_custom_call" | custom-call | bytes 6291456 | tf_op jit(solution)/shard_map/finish/pallas_call | solution.py:389
Async XLA Ops:
  0.6 37.2 %copy-start = (bf16[1024,1024]{1,0:T(8,128)(2,1)S(1)}, bf16[1024,1024]{1,0:T(8,128)(2,1)}, u32[]{:S(2)}) copy-start(bf16[1024,1024]{1,0:T(8,128)(2,1)} %coupling_ref.1) | copy-start | bytes 6291460
  0.6 33.3 %collective-permute-start.5 = (bf16[512,1024]{1,0:T(8,128)(2,1)}, bf16[512,1024]{1,0:T(8,128)(2,1)S(1)}, u32[]{:S(2)}, u32[]{:S(2)}) collective-permute-start(bf16[512,1024]{1,0:T(8,128)(2,1)} %mine_ref.1), channel_id=1, source_target_pairs={{0,1},{1,0},{2,3},{3,2},{4,5},{5,4},{6,7},{7,6},{8,9},{9,8},{10,11... | collective-permute-start | bytes 3145736 | tf_op jit(solution)/shard_map/ppermute | solution.py:405
  24.2 8.0 %collective-permute-start.2 = (bf16[2048,128]{1,0:T(8,128)(2,1)S(1)}, bf16[2048,128]{1,0:T(8,128)(2,1)S(1)}, u32[]{:S(2)}, u32[]{:S(2)}) collective-permute-start(bf16[2048,128]{1,0:T(8,128)(2,1)S(1)} %bitcast.5), channel_id=1, source_target_pairs={{0,24},{1,9},{2,26},{3,11},{4,28},{5,13},{6,30},{7,15},{8,16},{9,1... | collective-permute-start | bytes 1572872 | tf_op jit(solution)/shard_map/ppermute | solution.py:82
  24.2 8.0 %collective-permute-start = (bf16[2048,128]{1,0:T(8,128)(2,1)S(1)}, bf16[2048,128]{1,0:T(8,128)(2,1)S(1)}, u32[]{:S(2)}, u32[]{:S(2)}) collective-permute-start(bf16[2048,128]{1,0:T(8,128)(2,1)S(1)} %bitcast.6), channel_id=1, source_target_pairs={{0,6},{1,3},{2,4},{3,1},{4,2},{5,7},{6,0},{7,5},{8,14},{9,11},{10,... | collective-permute-start | bytes 1572872 | tf_op jit(solution)/shard_map/ppermute | solution.py:82
  24.2 13.6 %collective-permute-start.4 = (bf16[2048,128]{1,0:T(8,128)(2,1)S(1)}, bf16[2048,128]{1,0:T(8,128)(2,1)S(1)}, u32[]{:S(2)}, u32[]{:S(2)}) collective-permute-start(bf16[2048,128]{1,0:T(8,128)(2,1)S(1)} %bitcast.7), channel_id=1, source_target_pairs={{0,96},{1,33},{2,98},{3,35},{4,100},{5,37},{6,102},{7,39},{8,104},... | collective-permute-start | bytes 1572872 | tf_op jit(solution)/shard_map/ppermute | solution.py:82
  32.2 10.8 %collective-permute-start.3 = (bf16[2048,128]{1,0:T(8,128)(2,1)S(1)}, bf16[2048,128]{1,0:T(8,128)(2,1)S(1)}, u32[]{:S(2)}, u32[]{:S(2)}) collective-permute-start(bf16[2048,128]{1,0:T(8,128)(2,1)S(1)} %collective-permute-done.2.y_ref.refs_2_), channel_id=1, source_target_pairs={{0,96},{1,33},{2,98},{3,35},{4,100},{5,37},{6,102},{7,39},{8,104},... | collective-permute-start | bytes 1572872 | tf_op jit(solution)/shard_map/ppermute | solution.py:82
  32.2 10.8 %collective-permute-start.1 = (bf16[2048,128]{1,0:T(8,128)(2,1)S(1)}, bf16[2048,128]{1,0:T(8,128)(2,1)S(1)}, u32[]{:S(2)}, u32[]{:S(2)}) collective-permute-start(bf16[2048,128]{1,0:T(8,128)(2,1)S(1)} %collective-permute-done.x_ref.refs_1_), channel_id=1, source_target_pairs={{0,24},{1,9},{2,26},{3,11},{4,28},{5,13},{6,30},{7,15},{8,16},{9,1... | collective-permute-start | bytes 1572872 | tf_op jit(solution)/shard_map/ppermute | solution.py:82
  34.0 1.2 %copy-start.1 = (bf16[512,1024]{1,0:T(8,128)(2,1)S(1)}, bf16[512,1024]{1,0:T(8,128)(2,1)}, u32[]{:S(2)}) copy-start(bf16[512,1024]{1,0:T(8,128)(2,1)} %mine_ref.1) | copy-start | bytes 3145732
  37.8 8.2 %collective-permute-start.6 = (bf16[2048,128]{1,0:T(8,128)(2,1)S(1)}, bf16[2048,128]{1,0:T(8,128)(2,1)S(1)}, u32[]{:S(2)}, u32[]{:S(2)}) collective-permute-start(bf16[2048,128]{1,0:T(8,128)(2,1)S(1)} %collective-permute-done.4.z_ref.refs_4_), channel_id=1, source_target_pairs={{0,6},{1,3},{2,4},{3,1},{4,2},{5,7},{6,0},{7,5},{8,14},{9,11},{10,... | collective-permute-start | bytes 1572872 | tf_op jit(solution)/shard_map/ppermute | solution.py:82
  37.9 8.8 %copy-start.2 = (s32[64,16]{0,1:T(8,128)S(1)}, s32[64,16]{0,1:T(8,128)}, u32[]{:S(2)}) copy-start(s32[64,16]{0,1:T(8,128)} %param.7) | copy-start | bytes 12292
  46.0 4.2 %collective-permute-start.7 = (bf16[1024,1024]{1,0:T(8,128)(2,1)S(1)}, bf16[1024,1024]{1,0:T(8,128)(2,1)S(1)}, u32[]{:S(2)}, u32[]{:S(2)}) collective-permute-start(bf16[1024,1024]{1,0:T(8,128)(2,1)S(1)} %get-tuple-element.28.mine_ref), channel_id=1, source_target_pairs={{0,1},{1,0},{2,3},{3,2},{4,5},{5,4},{6,7},{7,6},{8,9},{9,8},{10,11... | collective-permute-start | bytes 6291464 | tf_op jit(solution)/shard_map/ppermute | solution.py:405
  46.4 8.3 %collective-permute-start.8 = (bf16[2048,128]{1,0:T(8,128)(2,1)S(1)}, bf16[2048,128]{1,0:T(8,128)(2,1)S(1)}, u32[]{:S(2)}, u32[]{:S(2)}) collective-permute-start(bf16[2048,128]{1,0:T(8,128)(2,1)S(1)} %collective-permute-done.1.refs_3_), channel_id=1, source_target_pairs={{0,96},{1,33},{2,98},{3,35},{4,100},{5,37},{6,102},{7,39},{8,104},... | collective-permute-start | bytes 1572872 | tf_op jit(solution)/shard_map/ppermute | solution.py:82
  61.2 4.5 %collective-permute-start.9 = (bf16[512,1024]{1,0:T(8,128)(2,1)S(1)}, bf16[512,1024]{1,0:T(8,128)(2,1)S(1)}, u32[]{:S(2)}, u32[]{:S(2)}) collective-permute-start(bf16[512,1024]{1,0:T(8,128)(2,1)S(1)} %get-tuple-element.35), channel_id=1, source_target_pairs={{0,1},{1,0},{2,3},{3,2},{4,5},{5,4},{6,7},{7,6},{8,9},{9,8},{10,11... | collective-permute-start | bytes 3145736 | tf_op jit(solution)/shard_map/ppermute | solution.py:405

commit v7 on v5

--- a/solution.py
+++ b/solution.py
@@ -272,18 +272,18 @@
     )(lists, mine, other)
 
 
-def place_strips(table_ref, sigma_ref, strips_ref, bits):
+def place_strips(table_ref, sigma_ref, strips_ref, bits, low=0, high=8):
     core, group = lax.axis_index("panel"), lax.axis_index("front")
     first, second = jnp.where(core == 0, 1, 3), jnp.where(core == 0, 3, 1)
     middle = group ^ spread(bits, second)
     start = jnp.where(first == 1, middle & 0b101010, middle ^ (3 * ((middle >> 1) & 0b010101)))
 
-    @pl.loop(0, 8)
+    @pl.loop(low, high)
     def _(n):
         source = start ^ spread(n, first)
         for row in range(HALF):
             to = pl.multiple_of(table_ref[row, source], STRIP)
-            at = pl.multiple_of(n * HALF * STRIP + row * STRIP, STRIP)
+            at = pl.multiple_of((n - low) * HALF * STRIP + row * STRIP, STRIP)
             sigma_ref[pl.ds(to, STRIP), :] = strips_ref[pl.ds(at, STRIP), :]
 
 
@@ -317,10 +317,11 @@
 
 
 def carry_kernel(
-    table_ref, sigma_in_ref, strips_ref, mine_ref, other_ref, turned_ref, carried_ref, send_ref, sigma_ref
+    table_ref, sigma_in_ref, top_ref, bottom_ref, mine_ref, other_ref, turned_ref, carried_ref, send_ref, sigma_ref
 ):
     core = lax.axis_index("panel")
-    place_strips(table_ref, sigma_ref, strips_ref, 7)
+    place_strips(table_ref, sigma_ref, top_ref, 7, 0, 4)
+    place_strips(table_ref, sigma_ref, bottom_ref, 7, 4, 8)
 
     def sigma(at):
         blocks = [sigma_ref[c * SIDE : (c + 1) * SIDE, :] for c in range(at, at + HALF)]
@@ -346,13 +347,13 @@
             jax.ShapeDtypeStruct((ROWS, SIDE), BF16),
             SIGMA,
         ),
-        in_specs=[SMEM] + [VMEM] * 5,
+        in_specs=[SMEM] + [VMEM] * 6,
         out_specs=(VMEM, VMEM, VMEM),
         input_output_aliases={1: 2},
         compiler_params=params(20),
         cost_estimate=cost(5 << 29, 12 << 20),
         name="carry",
-    )(table, sigma, last, mine, other, turned)
+    )(table, sigma, *last, mine, other, turned)
 
 
 def own_kernel(turned_ref, carried_ref, square_ref, out_ref):
@@ -419,7 +420,7 @@
     wide_other = swap(wide_mine)
     turned = turn_wide(lists, wide_mine, wide_other)
     sigma = make_sigma(lists, table, (near, x, y, xy, z, zx, yz))
-    carried, to_send, _ = carry(table, sigma, across(xy, 4), wide_mine, wide_other, turned)
+    carried, to_send, _ = carry(table, sigma, (across(xy[:SIDE], 4), across(zx[SIDE:], 2)), wide_mine, wide_other, turned)
     received = swap(to_send)
     own = own_product(turned, carried, square)
     selected, variances = finish(own, received)

time: 65.6 us -> 64.7 us (0.986)
  waiting for transfers between devices: 11.6 us -> 9.19 us
  starting transfers between devices: 7.53 us -> 8.78 us
    ppermute x7 -> x8, waiting for transfers between devices: 9.55 us -> 7.41 us  [across(): return lax.ppermute(x, AXES, pairs)]
    ppermute x3, starting transfers between devices: 4.57 us -> 5.65 us  [swap(): return lax.ppermute(x, 'panel', [(0, 1), (1, 0)])]
    ppermute x7 -> x8, starting transfers between devices: 2.96 us -> 3.13 us  [across(): return lax.ppermute(x, AXES, pairs)]
  transfers between devices with their start and end apart: 10 -> 11, of which waited for: 7 -> 6; matrix products, arithmetic and copies ran while one was open for 0% -> 0% of each run, Pallas kernels for 24% -> 24%
where the time goes in v7:
time: 64.7 us; the launch traced here: 64.4 us
  Pallas kernels  23.9 us (37%)
  blocking collectives  20.5 us (32%)
  waiting for transfers between devices  9.19 us (14%)
  starting transfers between devices  8.78 us (14%)
  local copies, waits for them, and re-layouts  1.26 us (2%)
  between operations  0.75 us (1%)
    all_to_all x1, blocking collectives, gather_cube(): lax.all_to_all(parts, AXES, split_axis=0, concat_axis=0, tiled=True, axis...  20.5 us
    ppermute x8, waiting for transfers between devices, across(): return lax.ppermute(x, AXES, pairs)  7.41 us
    pallas_call x1, Pallas kernels, carry(): pl.pallas_call(carry_kernel, out_shape=(jax.ShapeDtypeStruct((SIDE, SIDE)...  6.45 us
    ppermute x3, starting transfers between devices, swap(): return lax.ppermute(x, 'panel', [(0, 1), (1, 0)])  5.65 us
    pallas_call x1, Pallas kernels, solve(): pl.pallas_call(solve_kernel, out_shape=(jax.ShapeDtypeStruct((SIDE, SIDE)...  5.1 us
    ppermute x8, starting transfers between devices, across(): return lax.ppermute(x, AXES, pairs)  3.13 us
    pallas_call x1, Pallas kernels, make_sigma(): pl.pallas_call(sigma_kernel, out_shape=SIGMA, in_specs=[SMEM, SMEM] + [VM...  2.78 us
    pallas_call x1, Pallas kernels, invert_blocks(): pl.pallas_call(blocks_kernel, out_shape=(slim, slim, jax.ShapeDtypeStruct...  2.59 us
  transfers between devices with their start and end apart: 11, of which 6 were waited for; matrix products, arithmetic and copies ran while one was open for 0% of the time, Pallas kernels for 24%

profile of v7, /device:TPU:1, one launch (start us, length us, event | category | flops | bytes accessed | tf_op | source)
XLA Modules:
  0.0 64.4 jit_solution(17747275111278935846)
XLA Ops:
  0.6 0.0 copy-start
  0.6 1.5 %collective-permute-start.3 = (bf16[512,1024]{1,0:T(8,128)(2,1)}, bf16[512,1024]{1,0:T(8,128)(2,1)S(1)}, u32[]{:S(2)}, u32[]{:S(2)}) collective-permute-start(bf16[512,1024]{1,0:T(8,128)(2,1)} %mine_ref.1), channel_id=1, source_target_pairs={{0,1},{1,0},{2,3},{3,2},{4,5},{5,4},{6,7},{7,6},{8,9},{9,8},{10,11... | collective-permute-start | bytes 3145736 | tf_op jit(solution)/shard_map/ppermute | solution.py:406
  2.1 1.5 %pick_strips.1 = (bf16[2048,128]{1,0:T(8,128)(2,1)S(1)}, s32[8,64]{1,0:T(8,128)S(1)}) custom-call(s32[16,64]{1,0:T(8,128)} %bitcast.14, s32[16,64]{1,0:T(8,128)} %bitcast.11, bf16[512,128]{1,0:T(8,128)(2,1)} %strips_hbm.1), custom_call_target="tpu_custom_call" | custom-call | bytes 1048576 | tf_op jit(solution)/shard_map/pick_strips/pallas_call | solution.py:121
  3.6 20.5 %all_to_all.11 = bf16[8,256,128]{2,1,0:T(8,128)(2,1)S(1)} all-to-all(bf16[8,256,128]{2,1,0:T(8,128)(2,1)S(1)} %bitcast.10), channel_id=1, replica_groups={{0,2,8,10,32,34,40,42},{4,6,12,14,36,38,44,46},{16,18,24,26,48,50,56,58..., dimensions={0} | all-to-all | bytes 1048576 | tf_op jit(solution)/shard_map/all_to_all | solution.py:71
  24.1 0.0 collective-permute-start.2
  24.1 0.0 collective-permute-start.1
  24.1 0.0 collective-permute-start
  24.1 0.0 collective-permute-done.3.other_ref
  24.1 0.0 copy-start.1
  24.1 1.2 %copy-done.1 = bf16[512,1024]{1,0:T(8,128)(2,1)S(1)} copy-done((bf16[512,1024]{1,0:T(8,128)(2,1)S(1)}, bf16[512,1024]{1,0:T(8,128)(2,1)}, u32[]{:S(2)}) %copy-start.1) | copy-done | bytes 1048600
  25.3 2.6 %invert_blocks.1 = (bf16[1024,128]{1,0:T(8,128)(2,1)S(1)}, bf16[1024,128]{1,0:T(8,128)(2,1)S(1)}, bf16[1024,1024]{1,0:T(8,128)(2,1)S(1)}) custom-call(bf16[512,1024]{1,0:T(8,128)(2,1)S(1)} %copy-done.1, bf16[512,1024]{1,0:T(8,128)(2,1)S(1)} %collective-permute-done.3.other_ref, bf16[2048,128]{1,0:T(8,128)(2,1)S(1)} %bitcast.8), custom_call_target="tpu_custom_call" | custom-call | flops 2097152 | bytes 65536 | tf_op jit(solution)/shard_map/invert_blocks/pallas_call | solution.py:185
  27.9 4.2 %collective-permute-done.2.z_ref.refs_4_ = bf16[2048,128]{1,0:T(8,128)(2,1)S(1)} collective-permute-done((bf16[2048,128]{1,0:T(8,128)(2,1)S(1)}, bf16[2048,128]{1,0:T(8,128)(2,1)S(1)}, u32[]{:S(2)}, u32[]{:S(2)}) %collective-permute-start.2) | collective-permute-done | bytes 524320 | tf_op jit(solution)/shard_map/ppermute | solution.py:82
  32.1 0.0 collective-permute-done.1.y_ref.refs_2_
  32.1 0.0 collective-permute-done.x_ref.refs_1_
  32.1 1.5 %collective-permute-start.4 = (bf16[2048,128]{1,0:T(8,128)(2,1)S(1)}, bf16[2048,128]{1,0:T(8,128)(2,1)S(1)}, u32[]{:S(2)}, u32[]{:S(2)}) collective-permute-start(bf16[2048,128]{1,0:T(8,128)(2,1)S(1)} %collective-permute-done.x_ref.refs_1_), channel_id=1, source_target_pairs={{0,24},{1,9},{2,26},{3,11},{4,28},{5,13},{6,30},{7,15},{8,16},{9,1... | collective-permute-start | bytes 1572872 | tf_op jit(solution)/shard_map/ppermute | solution.py:82
  33.6 1.5 %collective-permute-start.5 = (bf16[2048,128]{1,0:T(8,128)(2,1)S(1)}, bf16[2048,128]{1,0:T(8,128)(2,1)S(1)}, u32[]{:S(2)}, u32[]{:S(2)}) collective-permute-start(bf16[2048,128]{1,0:T(8,128)(2,1)S(1)} %collective-permute-done.1.y_ref.refs_2_), channel_id=1, source_target_pairs={{0,96},{1,33},{2,98},{3,35},{4,100},{5,37},{6,102},{7,39},{8,104},... | collective-permute-start | bytes 1572872 | tf_op jit(solution)/shard_map/ppermute | solution.py:82
  35.1 0.0 collective-permute-start.6
  35.1 0.0 copy-done
  35.1 0.0 copy-start.2
  35.1 5.1 %solve.1 = (bf16[1024,1024]{1,0:T(8,128)(2,1)S(1)}, f32[512,1024]{1,0:T(8,128)S(1)}) custom-call(bf16[1024,128]{1,0:T(8,128)(2,1)S(1)} %get-tuple-element.27.hi_slim_ref, bf16[1024,128]{1,0:T(8,128)(2,1)S(1)} %get-tuple-element.28.lo_slim_ref, bf16[1024,1024]{1,0:T(8,128)(2,1)S(1)} %get-tuple-element.29.low_ref, bf16[1024,1024]{1,0:T(8,128)(2,1)S(1)} %copy-done, ...), custom_call_target="tpu_custom_call" | custom-call | flops 2097152 | bytes 65536 | tf_op jit(solution)/shard_map/solve/pallas_call | solution.py:230
  40.2 0.3 collective-permute-done.4.refs_3_
  40.5 1.5 %collective-permute-done.5.refs_6_ = bf16[2048,128]{1,0:T(8,128)(2,1)S(1)} collective-permute-done((bf16[2048,128]{1,0:T(8,128)(2,1)S(1)}, bf16[2048,128]{1,0:T(8,128)(2,1)S(1)}, u32[]{:S(2)}, u32[]{:S(2)}) %collective-permute-start.5) | collective-permute-done | bytes 524320 | tf_op jit(solution)/shard_map/ppermute | solution.py:82
  41.9 1.5 %collective-permute-done.6.refs_5_ = bf16[2048,128]{1,0:T(8,128)(2,1)S(1)} collective-permute-done((bf16[2048,128]{1,0:T(8,128)(2,1)S(1)}, bf16[2048,128]{1,0:T(8,128)(2,1)S(1)}, u32[]{:S(2)}, u32[]{:S(2)}) %collective-permute-start.6) | collective-permute-done | bytes 524320 | tf_op jit(solution)/shard_map/ppermute | solution.py:82
  43.4 0.9 %collective-permute-start.7 = (bf16[1024,1024]{1,0:T(8,128)(2,1)S(1)}, bf16[1024,1024]{1,0:T(8,128)(2,1)S(1)}, u32[]{:S(2)}, u32[]{:S(2)}) collective-permute-start(bf16[1024,1024]{1,0:T(8,128)(2,1)S(1)} %get-tuple-element.32.mine_ref), channel_id=1, source_target_pairs={{0,1},{1,0},{2,3},{3,2},{4,5},{5,4},{6,7},{7,6},{8,9},{9,8},{10,11... | collective-permute-start | bytes 6291464 | tf_op jit(solution)/shard_map/ppermute | solution.py:406
  44.3 0.1 collective-permute-start.9
  44.4 0.1 collective-permute-start.8
  44.5 0.0 copy-done.2
  44.5 2.8 %make_sigma.1.sigma_in_ref = bf16[17408,128]{1,0:T(8,128)(2,1)S(1)} custom-call(s32[16,64]{1,0:T(8,128)S(1)} %bitcast.12, s32[8,64]{1,0:T(8,128)S(1)} %get-tuple-element.33.table_ref, bf16[2048,128]{1,0:T(8,128)(2,1)S(1)} %bitcast.9, bf16[2048,128]{1,0:T(8,128)(2,1)S(1)} %collective-permute-done.x_ref.refs_1_, ...), custom_call_target="tpu_custom_call" | custom-call | bytes 10485760 | tf_op jit(solution)/shard_map/make_sigma/pallas_call | solution.py:308
  47.3 0.7 %collective-permute-done.7.other_ref = bf16[1024,1024]{1,0:T(8,128)(2,1)S(1)} collective-permute-done((bf16[1024,1024]{1,0:T(8,128)(2,1)S(1)}, bf16[1024,1024]{1,0:T(8,128)(2,1)S(1)}, u32[]{:S(2)}, u32[]{:S(2)}) %collective-permute-start.7) | collective-permute-done | bytes 2097184 | tf_op jit(solution)/shard_map/ppermute | solution.py:406
  48.1 2.4 %turn_wide.1.turned_ref = bf16[1024,1024]{1,0:T(8,128)(2,1)S(1)} custom-call(s32[16,64]{1,0:T(8,128)S(1)} %bitcast.13, bf16[1024,1024]{1,0:T(8,128)(2,1)S(1)} %get-tuple-element.32.mine_ref, bf16[1024,1024]{1,0:T(8,128)(2,1)S(1)} %collective-permute-done.7.other_ref), custom_call_target="tpu_custom_call" | custom-call | bytes 8388608 | tf_op jit(solution)/shard_map/turn_wide/pallas_call | solution.py:264
  50.5 0.0 collective-permute-done.9.bottom_ref
  50.5 0.0 collective-permute-done.8.top_ref
  50.5 6.4 %carry.1 = (bf16[1024,1024]{1,0:T(8,128)(2,1)S(1)}, bf16[512,1024]{1,0:T(8,128)(2,1)S(1)}, bf16[17408,128]{1,0:T(8,128)(2,1)S(1)}) custom-call(s32[8,64]{1,0:T(8,128)S(1)} %get-tuple-element.33.table_ref, bf16[17408,128]{1,0:T(8,128)(2,1)S(1)} %make_sigma.1.sigma_in_ref, ...), custom_call_target="tpu_custom_call", output_to_operand_aliasing={{2}: (1, {})} | custom-call | flops 5368709120 | bytes 12582912 | tf_op jit(solution)/shard_map/carry/pallas_call | solution.py:343
  57.0 3.2 %collective-permute-start.10 = (bf16[512,1024]{1,0:T(8,128)(2,1)S(1)}, bf16[512,1024]{1,0:T(8,128)(2,1)S(1)}, u32[]{:S(2)}, u32[]{:S(2)}) collective-permute-start(bf16[512,1024]{1,0:T(8,128)(2,1)S(1)} %get-tuple-element.39), channel_id=1, source_target_pairs={{0,1},{1,0},{2,3},{3,2},{4,5},{5,4},{6,7},{7,6},{8,9},{9,8},{10,11... | collective-permute-start | bytes 3145736 | tf_op jit(solution)/shard_map/ppermute | solution.py:406
  60.2 1.2 %own_product.1.own_ref = f32[512,1024]{1,0:T(8,128)S(1)} custom-call(bf16[1024,1024]{1,0:T(8,128)(2,1)S(1)} %turn_wide.1.turned_ref, bf16[1024,1024]{1,0:T(8,128)(2,1)S(1)} %get-tuple-element.37.carried_ref, f32[512,1024]{1,0:T(8,128)S(1)} %get-tuple-element.38.square_ref), custom_call_target="tpu_custom_call" | custom-call | flops 1073741824 | bytes 8388608 | tf_op jit(solution)/shard_map/own_product/pallas_call | solution.py:368
  61.4 1.0 %collective-permute-done.10.received_ref = bf16[512,1024]{1,0:T(8,128)(2,1)S(1)} collective-permute-done((bf16[512,1024]{1,0:T(8,128)(2,1)S(1)}, bf16[512,1024]{1,0:T(8,128)(2,1)S(1)}, u32[]{:S(2)}, u32[]{:S(2)}) %collective-permute-start.10) | collective-permute-done | bytes 1048608 | tf_op jit(solution)/shard_map/ppermute | solution.py:406
  62.5 1.9 %finish.1 = (f32[512,1024]{1,0:T(8,128)}, f32[1,512]{1,0:T(1,128)}) custom-call(f32[512,1024]{1,0:T(8,128)S(1)} %own_product.1.own_ref, bf16[512,1024]{1,0:T(8,128)(2,1)S(1)} %collective-permute-done.10.received_ref), custom_call_target="tpu_custom_call" | custom-call | bytes 6291456 | tf_op jit(solution)/shard_map/finish/pallas_call | solution.py:390
  (2 shorter events, 0.0 us)
Async XLA Ops:
  0.6 34.4 %copy-start = (bf16[1024,1024]{1,0:T(8,128)(2,1)S(1)}, bf16[1024,1024]{1,0:T(8,128)(2,1)}, u32[]{:S(2)}) copy-start(bf16[1024,1024]{1,0:T(8,128)(2,1)} %coupling_ref.1) | copy-start | bytes 6291460
  0.6 23.5 %collective-permute-start.3 = (bf16[512,1024]{1,0:T(8,128)(2,1)}, bf16[512,1024]{1,0:T(8,128)(2,1)S(1)}, u32[]{:S(2)}, u32[]{:S(2)}) collective-permute-start(bf16[512,1024]{1,0:T(8,128)(2,1)} %mine_ref.1), channel_id=1, source_target_pairs={{0,1},{1,0},{2,3},{3,2},{4,5},{5,4},{6,7},{7,6},{8,9},{9,8},{10,11... | collective-permute-start | bytes 3145736 | tf_op jit(solution)/shard_map/ppermute | solution.py:406
  24.1 8.0 %collective-permute-start.2 = (bf16[2048,128]{1,0:T(8,128)(2,1)S(1)}, bf16[2048,128]{1,0:T(8,128)(2,1)S(1)}, u32[]{:S(2)}, u32[]{:S(2)}) collective-permute-start(bf16[2048,128]{1,0:T(8,128)(2,1)S(1)} %bitcast.5), channel_id=1, source_target_pairs={{0,96},{1,33},{2,98},{3,35},{4,100},{5,37},{6,102},{7,39},{8,104},... | collective-permute-start | bytes 1572872 | tf_op jit(solution)/shard_map/ppermute | solution.py:82
  24.1 8.0 %collective-permute-start.1 = (bf16[2048,128]{1,0:T(8,128)(2,1)S(1)}, bf16[2048,128]{1,0:T(8,128)(2,1)S(1)}, u32[]{:S(2)}, u32[]{:S(2)}) collective-permute-start(bf16[2048,128]{1,0:T(8,128)(2,1)S(1)} %bitcast.6), channel_id=1, source_target_pairs={{0,24},{1,9},{2,26},{3,11},{4,28},{5,13},{6,30},{7,15},{8,16},{9,1... | collective-permute-start | bytes 1572872 | tf_op jit(solution)/shard_map/ppermute | solution.py:82
  24.1 8.0 %collective-permute-start = (bf16[2048,128]{1,0:T(8,128)(2,1)S(1)}, bf16[2048,128]{1,0:T(8,128)(2,1)S(1)}, u32[]{:S(2)}, u32[]{:S(2)}) collective-permute-start(bf16[2048,128]{1,0:T(8,128)(2,1)S(1)} %bitcast.7), channel_id=1, source_target_pairs={{0,6},{1,3},{2,4},{3,1},{4,2},{5,7},{6,0},{7,5},{8,14},{9,11},{10,... | collective-permute-start | bytes 1572872 | tf_op jit(solution)/shard_map/ppermute | solution.py:82
  24.1 1.2 %copy-start.1 = (bf16[512,1024]{1,0:T(8,128)(2,1)S(1)}, bf16[512,1024]{1,0:T(8,128)(2,1)}, u32[]{:S(2)}) copy-start(bf16[512,1024]{1,0:T(8,128)(2,1)} %mine_ref.1) | copy-start | bytes 3145732
  32.1 8.3 %collective-permute-start.4 = (bf16[2048,128]{1,0:T(8,128)(2,1)S(1)}, bf16[2048,128]{1,0:T(8,128)(2,1)S(1)}, u32[]{:S(2)}, u32[]{:S(2)}) collective-permute-start(bf16[2048,128]{1,0:T(8,128)(2,1)S(1)} %collective-permute-done.x_ref.refs_1_), channel_id=1, source_target_pairs={{0,24},{1,9},{2,26},{3,11},{4,28},{5,13},{6,30},{7,15},{8,16},{9,1... | collective-permute-start | bytes 1572872 | tf_op jit(solution)/shard_map/ppermute | solution.py:82
  33.6 8.3 %collective-permute-start.5 = (bf16[2048,128]{1,0:T(8,128)(2,1)S(1)}, bf16[2048,128]{1,0:T(8,128)(2,1)S(1)}, u32[]{:S(2)}, u32[]{:S(2)}) collective-permute-start(bf16[2048,128]{1,0:T(8,128)(2,1)S(1)} %collective-permute-done.1.y_ref.refs_2_), channel_id=1, source_target_pairs={{0,96},{1,33},{2,98},{3,35},{4,100},{5,37},{6,102},{7,39},{8,104},... | collective-permute-start | bytes 1572872 | tf_op jit(solution)/shard_map/ppermute | solution.py:82
  35.1 8.3 %collective-permute-start.6 = (bf16[2048,128]{1,0:T(8,128)(2,1)S(1)}, bf16[2048,128]{1,0:T(8,128)(2,1)S(1)}, u32[]{:S(2)}, u32[]{:S(2)}) collective-permute-start(bf16[2048,128]{1,0:T(8,128)(2,1)S(1)} %collective-permute-done.2.z_ref.refs_4_), channel_id=1, source_target_pairs={{0,6},{1,3},{2,4},{3,1},{4,2},{5,7},{6,0},{7,5},{8,14},{9,11},{10,... | collective-permute-start | bytes 1572872 | tf_op jit(solution)/shard_map/ppermute | solution.py:82
  35.1 9.5 %copy-start.2 = (s32[64,16]{0,1:T(8,128)S(1)}, s32[64,16]{0,1:T(8,128)}, u32[]{:S(2)}) copy-start(s32[64,16]{0,1:T(8,128)} %param.7) | copy-start | bytes 12292
  43.4 4.7 %collective-permute-start.7 = (bf16[1024,1024]{1,0:T(8,128)(2,1)S(1)}, bf16[1024,1024]{1,0:T(8,128)(2,1)S(1)}, u32[]{:S(2)}, u32[]{:S(2)}) collective-permute-start(bf16[1024,1024]{1,0:T(8,128)(2,1)S(1)} %get-tuple-element.32.mine_ref), channel_id=1, source_target_pairs={{0,1},{1,0},{2,3},{3,2},{4,5},{5,4},{6,7},{7,6},{8,9},{9,8},{10,11... | collective-permute-start | bytes 6291464 | tf_op jit(solution)/shard_map/ppermute | solution.py:406
  44.3 6.1 %collective-permute-start.9 = (bf16[1024,128]{1,0:T(8,128)(2,1)S(1)}, bf16[1024,128]{1,0:T(8,128)(2,1)S(1)}, u32[]{:S(2)}, u32[]{:S(2)}) collective-permute-start(bf16[1024,128]{1,0:T(8,128)(2,1)S(1)} %slice.7), channel_id=1, source_target_pairs={{0,24},{1,9},{2,26},{3,11},{4,28},{5,13},{6,30},{7,15},{8,16},{9,1... | collective-permute-start | bytes 786440 | tf_op jit(solution)/shard_map/ppermute | solution.py:82
  44.4 6.1 %collective-permute-start.8 = (bf16[1024,128]{1,0:T(8,128)(2,1)S(1)}, bf16[1024,128]{1,0:T(8,128)(2,1)S(1)}, u32[]{:S(2)}, u32[]{:S(2)}) collective-permute-start(bf16[1024,128]{1,0:T(8,128)(2,1)S(1)} %slice.6), channel_id=1, source_target_pairs={{0,96},{1,33},{2,98},{3,35},{4,100},{5,37},{6,102},{7,39},{8,104},... | collective-permute-start | bytes 786440 | tf_op jit(solution)/shard_map/ppermute | solution.py:82
  57.0 5.5 %collective-permute-start.10 = (bf16[512,1024]{1,0:T(8,128)(2,1)S(1)}, bf16[512,1024]{1,0:T(8,128)(2,1)S(1)}, u32[]{:S(2)}, u32[]{:S(2)}) collective-permute-start(bf16[512,1024]{1,0:T(8,128)(2,1)S(1)} %get-tuple-element.39), channel_id=1, source_target_pairs={{0,1},{1,0},{2,3},{3,2},{4,5},{5,4},{6,7},{7,6},{8,9},{9,8},{10,11... | collective-permute-start | bytes 3145736 | tf_op jit(solution)/shard_map/ppermute | solution.py:406

commit v8 on v7

--- a/solution.py
+++ b/solution.py
@@ -288,7 +288,7 @@
 
 
 def sigma_kernel(list_ref, table_ref, *refs):
-    strips_refs, sigma_ref = refs[:7], refs[7]
+    strips_refs, sigma_ref = refs[:4], refs[4]
     core, group = lax.axis_index("panel"), lax.axis_index("front")
     for a in range(NABOVE):
         column = pl.multiple_of((a ^ (core * HALF)) * SIDE, SIDE)
@@ -297,8 +297,13 @@
         def _():
             sigma_ref[pl.ds(column, SIDE), :] = jnp.zeros((SIDE, BLOCK), BF16)
 
-    for bits in range(7):
-        place_strips(table_ref, sigma_ref, strips_refs[bits], bits)
+    for bits, strips_ref in zip((0, 1, 2, 4), strips_refs):
+        place_strips(table_ref, sigma_ref, strips_ref, bits)
+
+
+def more_kernel(table_ref, sigma_in_ref, xy_ref, zx_ref, yz_ref, sigma_ref):
+    for bits, strips_ref in zip((3, 5, 6), (xy_ref, zx_ref, yz_ref)):
+        place_strips(table_ref, sigma_ref, strips_ref, bits)
 
 
 SIGMA = jax.ShapeDtypeStruct(((NABOVE + 1) * SIDE, BLOCK), BF16)
@@ -308,12 +313,25 @@
     return pl.pallas_call(
         sigma_kernel,
         out_shape=SIGMA,
-        in_specs=[SMEM, SMEM] + [VMEM] * 7,
+        in_specs=[SMEM, SMEM] + [VMEM] * 4,
         out_specs=VMEM,
         compiler_params=params(12),
-        cost_estimate=cost(0, 10 << 20),
+        cost_estimate=cost(1 << 20, 1 << 16),
         name="make_sigma",
     )(lists, table, *strips)
+
+
+def more_sigma(table, sigma, strips):
+    return pl.pallas_call(
+        more_kernel,
+        out_shape=SIGMA,
+        in_specs=[SMEM] + [VMEM] * 4,
+        out_specs=VMEM,
+        input_output_aliases={1: 0},
+        compiler_params=params(12),
+        cost_estimate=cost(0, 5 << 20),
+        name="more_sigma",
+    )(table, sigma, *strips)
 
 
 def carry_kernel(
@@ -416,10 +434,11 @@
     x, y, z, hi = lax.optimization_barrier((x, y, z, hi))
     xy, yz, zx = across(x, 2), across(y, 4), across(z, 1)
     wide_mine, square = solve(hi, lo, low, coup_factor, (x, y, z))
-    xy, yz, zx, wide_mine, square = lax.optimization_barrier((xy, yz, zx, wide_mine, square))
+    sigma = make_sigma(lists, table, (near, x, y, z))
+    xy, yz, zx, wide_mine, square, sigma = lax.optimization_barrier((xy, yz, zx, wide_mine, square, sigma))
     wide_other = swap(wide_mine)
     turned = turn_wide(lists, wide_mine, wide_other)
-    sigma = make_sigma(lists, table, (near, x, y, xy, z, zx, yz))
+    sigma = more_sigma(table, sigma, (xy, zx, yz))
     carried, to_send, _ = carry(table, sigma, (across(xy[:SIDE], 4), across(zx[SIDE:], 2)), wide_mine, wide_other, turned)
     received = swap(to_send)
     own = own_product(turned, carried, square)

time: 64.7 us -> 65.6 us (1.014)
  starting transfers between devices: 8.78 us -> 10.3 us
    ppermute x8, waiting for transfers between devices: 7.41 us -> 5.54 us  [across(): return lax.ppermute(x, AXES, pairs)]
    ppermute x3, starting transfers between devices: 5.65 us -> 7.15 us  [swap(): return lax.ppermute(x, 'panel', [(0, 1), (1, 0)])]
    ppermute x3, waiting for transfers between devices: 1.78 us -> 3.22 us  [swap(): return lax.ppermute(x, 'panel', [(0, 1), (1, 0)])]
    pallas_call x0 -> x1, Pallas kernels: none -> 1.36 us  [more_sigma(): pl.pallas_call(more_kernel, out_shape=SIGMA, in_specs=[SMEM] + [VMEM] * 4...]
    pallas_call x1, Pallas kernels: 2.39 us -> 1.56 us  [turn_wide(): pl.pallas_call(turn_kernel, out_shape=jax.ShapeDtypeStruct((SIDE, SIDE),...]
where the time goes in v8:
time: 65.6 us; the launch traced here: 65.4 us
  Pallas kernels  23.9 us (36%)
  blocking collectives  20.5 us (31%)
  starting transfers between devices  10.3 us (16%)
  waiting for transfers between devices  8.76 us (13%)
  local copies, waits for them, and re-layouts  1.26 us (2%)
  between operations  0.77 us (1%)
    all_to_all x1, blocking collectives, gather_cube(): lax.all_to_all(parts, AXES, split_axis=0, concat_axis=0, tiled=True, axis...  20.5 us
    ppermute x3, starting transfers between devices, swap(): return lax.ppermute(x, 'panel', [(0, 1), (1, 0)])  7.15 us
    pallas_call x1, Pallas kernels, carry(): pl.pallas_call(carry_kernel, out_shape=(jax.ShapeDtypeStruct((SIDE, SIDE)...  6.44 us
    ppermute x8, waiting for transfers between devices, across(): return lax.ppermute(x, AXES, pairs)  5.54 us
    pallas_call x1, Pallas kernels, solve(): pl.pallas_call(solve_kernel, out_shape=(jax.ShapeDtypeStruct((SIDE, SIDE)...  5.11 us
    ppermute x3, waiting for transfers between devices, swap(): return lax.ppermute(x, 'panel', [(0, 1), (1, 0)])  3.22 us
    ppermute x8, starting transfers between devices, across(): return lax.ppermute(x, AXES, pairs)  3.11 us
    pallas_call x1, Pallas kernels, invert_blocks(): pl.pallas_call(blocks_kernel, out_shape=(slim, slim, jax.ShapeDtypeStruct...  2.59 us
  transfers between devices with their start and end apart: 11, of which 6 were waited for; matrix products, arithmetic and copies ran while one was open for 0% of the time, Pallas kernels for 24%

profile of v8, /device:TPU:1, one launch (start us, length us, event | category | flops | bytes accessed | tf_op | source)
XLA Modules:
  0.0 65.4 jit_solution(7651649983085147501)
XLA Ops:
  0.6 0.0 copy-start.2
  0.6 1.5 %collective-permute-start.3 = (bf16[512,1024]{1,0:T(8,128)(2,1)}, bf16[512,1024]{1,0:T(8,128)(2,1)S(1)}, u32[]{:S(2)}, u32[]{:S(2)}) collective-permute-start(bf16[512,1024]{1,0:T(8,128)(2,1)} %mine_ref.1), channel_id=1, source_target_pairs={{0,1},{1,0},{2,3},{3,2},{4,5},{5,4},{6,7},{7,6},{8,9},{9,8},{10,11... | collective-permute-start | bytes 3145736 | tf_op jit(solution)/shard_map/ppermute | solution.py:424
  2.1 1.5 %pick_strips.1 = (bf16[2048,128]{1,0:T(8,128)(2,1)S(1)}, s32[8,64]{1,0:T(8,128)S(1)}) custom-call(s32[16,64]{1,0:T(8,128)} %bitcast.14, s32[16,64]{1,0:T(8,128)} %bitcast.11, bf16[512,128]{1,0:T(8,128)(2,1)} %strips_hbm.1), custom_call_target="tpu_custom_call" | custom-call | bytes 1048576 | tf_op jit(solution)/shard_map/pick_strips/pallas_call | solution.py:121
  3.6 20.5 %all_to_all.11 = bf16[8,256,128]{2,1,0:T(8,128)(2,1)S(1)} all-to-all(bf16[8,256,128]{2,1,0:T(8,128)(2,1)S(1)} %bitcast.10), channel_id=1, replica_groups={{0,2,8,10,32,34,40,42},{4,6,12,14,36,38,44,46},{16,18,24,26,48,50,56,58..., dimensions={0} | all-to-all | bytes 1048576 | tf_op jit(solution)/shard_map/all_to_all | solution.py:71
  24.1 0.0 collective-permute-start.2
  24.1 0.0 collective-permute-start.1
  24.1 0.0 collective-permute-start
  24.1 0.0 collective-permute-done.3.other_ref
  24.1 0.0 copy-start.1
  24.1 1.2 %copy-done.1 = bf16[512,1024]{1,0:T(8,128)(2,1)S(1)} copy-done((bf16[512,1024]{1,0:T(8,128)(2,1)S(1)}, bf16[512,1024]{1,0:T(8,128)(2,1)}, u32[]{:S(2)}) %copy-start.1) | copy-done | bytes 1048600
  25.3 2.6 %invert_blocks.1 = (bf16[1024,128]{1,0:T(8,128)(2,1)S(1)}, bf16[1024,128]{1,0:T(8,128)(2,1)S(1)}, bf16[1024,1024]{1,0:T(8,128)(2,1)S(1)}) custom-call(bf16[512,1024]{1,0:T(8,128)(2,1)S(1)} %copy-done.1, bf16[512,1024]{1,0:T(8,128)(2,1)S(1)} %collective-permute-done.3.other_ref, bf16[2048,128]{1,0:T(8,128)(2,1)S(1)} %bitcast.8), custom_call_target="tpu_custom_call" | custom-call | flops 2097152 | bytes 65536 | tf_op jit(solution)/shard_map/invert_blocks/pallas_call | solution.py:185
  27.9 4.2 %collective-permute-done.2.z_ref.refs_3_ = bf16[2048,128]{1,0:T(8,128)(2,1)S(1)} collective-permute-done((bf16[2048,128]{1,0:T(8,128)(2,1)S(1)}, bf16[2048,128]{1,0:T(8,128)(2,1)S(1)}, u32[]{:S(2)}, u32[]{:S(2)}) %collective-permute-start.2) | collective-permute-done | bytes 524320 | tf_op jit(solution)/shard_map/ppermute | solution.py:82
  32.1 0.0 collective-permute-done.1.y_ref.refs_2_
  32.1 0.0 collective-permute-done.x_ref.refs_1_
  32.1 1.5 %collective-permute-start.4 = (bf16[2048,128]{1,0:T(8,128)(2,1)S(1)}, bf16[2048,128]{1,0:T(8,128)(2,1)S(1)}, u32[]{:S(2)}, u32[]{:S(2)}) collective-permute-start(bf16[2048,128]{1,0:T(8,128)(2,1)S(1)} %collective-permute-done.x_ref.refs_1_), channel_id=1, source_target_pairs={{0,24},{1,9},{2,26},{3,11},{4,28},{5,13},{6,30},{7,15},{8,16},{9,1... | collective-permute-start | bytes 1572872 | tf_op jit(solution)/shard_map/ppermute | solution.py:82
  33.6 1.5 %collective-permute-start.5 = (bf16[2048,128]{1,0:T(8,128)(2,1)S(1)}, bf16[2048,128]{1,0:T(8,128)(2,1)S(1)}, u32[]{:S(2)}, u32[]{:S(2)}) collective-permute-start(bf16[2048,128]{1,0:T(8,128)(2,1)S(1)} %collective-permute-done.1.y_ref.refs_2_), channel_id=1, source_target_pairs={{0,96},{1,33},{2,98},{3,35},{4,100},{5,37},{6,102},{7,39},{8,104},... | collective-permute-start | bytes 1572872 | tf_op jit(solution)/shard_map/ppermute | solution.py:82
  35.1 0.0 collective-permute-start.6
  35.1 0.0 copy-done.2
  35.1 0.0 copy-start
  35.1 2.2 %make_sigma.1.sigma_in_ref = bf16[17408,128]{1,0:T(8,128)(2,1)S(1)} custom-call(s32[16,64]{1,0:T(8,128)S(1)} %bitcast.12, s32[8,64]{1,0:T(8,128)S(1)} %get-tuple-element.33.table_ref, bf16[2048,128]{1,0:T(8,128)(2,1)S(1)} %bitcast.9, bf16[2048,128]{1,0:T(8,128)(2,1)S(1)} %collective-permute-done.x_ref.refs_1_, ...), custom_call_target="tpu_custom_call" | custom-call | flops 2097152 | bytes 65536 | tf_op jit(solution)/shard_map/make_sigma/pallas_call | solution.py:313
  37.3 0.0 copy-done
  37.3 5.1 %solve.1 = (bf16[1024,1024]{1,0:T(8,128)(2,1)S(1)}, f32[512,1024]{1,0:T(8,128)S(1)}) custom-call(bf16[1024,128]{1,0:T(8,128)(2,1)S(1)} %get-tuple-element.28.hi_slim_ref, bf16[1024,128]{1,0:T(8,128)(2,1)S(1)} %get-tuple-element.29.lo_slim_ref, bf16[1024,1024]{1,0:T(8,128)(2,1)S(1)} %get-tuple-element.30.low_ref, bf16[1024,1024]{1,0:T(8,128)(2,1)S(1)} %copy-done, ...), custom_call_target="tpu_custom_call" | custom-call | flops 2097152 | bytes 65536 | tf_op jit(solution)/shard_map/solve/pallas_call | solution.py:230
  42.4 0.0 collective-permute-done.4.xy_ref
  42.4 0.0 collective-permute-done.5.yz_ref
  42.4 1.0 %collective-permute-done.6.zx_ref = bf16[2048,128]{1,0:T(8,128)(2,1)S(1)} collective-permute-done((bf16[2048,128]{1,0:T(8,128)(2,1)S(1)}, bf16[2048,128]{1,0:T(8,128)(2,1)S(1)}, u32[]{:S(2)}, u32[]{:S(2)}) %collective-permute-start.6) | collective-permute-done | bytes 524320 | tf_op jit(solution)/shard_map/ppermute | solution.py:82
  43.4 0.9 %collective-permute-start.7 = (bf16[1024,1024]{1,0:T(8,128)(2,1)S(1)}, bf16[1024,1024]{1,0:T(8,128)(2,1)S(1)}, u32[]{:S(2)}, u32[]{:S(2)}) collective-permute-start(bf16[1024,1024]{1,0:T(8,128)(2,1)S(1)} %get-tuple-element.34.mine_ref), channel_id=1, source_target_pairs={{0,1},{1,0},{2,3},{3,2},{4,5},{5,4},{6,7},{7,6},{8,9},{9,8},{10,11... | collective-permute-start | bytes 6291464 | tf_op jit(solution)/shard_map/ppermute | solution.py:424
  44.3 0.1 collective-permute-start.8
  44.5 0.1 collective-permute-start.9
  44.5 1.4 %more_sigma.1.sigma_in_ref = bf16[17408,128]{1,0:T(8,128)(2,1)S(1)} custom-call(s32[8,64]{1,0:T(8,128)S(1)} %get-tuple-element.33.table_ref, bf16[17408,128]{1,0:T(8,128)(2,1)S(1)} %make_sigma.1.sigma_in_ref, bf16[2048,128]{1,0:T(8,128)(2,1)S(1)} %collective-permute-done.4.xy_ref, ...), custom_call_target="tpu_custom_call", output_to_operand_aliasing={{}: (1, {})} | custom-call | bytes 5242880 | tf_op jit(solution)/shard_map/more_sigma/pallas_call | solution.py:325
  45.9 2.2 %collective-permute-done.7.other_ref = bf16[1024,1024]{1,0:T(8,128)(2,1)S(1)} collective-permute-done((bf16[1024,1024]{1,0:T(8,128)(2,1)S(1)}, bf16[1024,1024]{1,0:T(8,128)(2,1)S(1)}, u32[]{:S(2)}, u32[]{:S(2)}) %collective-permute-start.7) | collective-permute-done | bytes 2097184 | tf_op jit(solution)/shard_map/ppermute | solution.py:424
  48.1 1.6 %turn_wide.1.turned_ref = bf16[1024,1024]{1,0:T(8,128)(2,1)S(1)} custom-call(s32[16,64]{1,0:T(8,128)S(1)} %bitcast.13, bf16[1024,1024]{1,0:T(8,128)(2,1)S(1)} %get-tuple-element.34.mine_ref, bf16[1024,1024]{1,0:T(8,128)(2,1)S(1)} %collective-permute-done.7.other_ref), custom_call_target="tpu_custom_call" | custom-call | bytes 8388608 | tf_op jit(solution)/shard_map/turn_wide/pallas_call | solution.py:264
  49.6 0.3 collective-permute-done.8.top_ref
  49.9 0.1 collective-permute-done.9.bottom_ref
  50.0 6.4 %carry.1 = (bf16[1024,1024]{1,0:T(8,128)(2,1)S(1)}, bf16[512,1024]{1,0:T(8,128)(2,1)S(1)}, bf16[17408,128]{1,0:T(8,128)(2,1)S(1)}) custom-call(s32[8,64]{1,0:T(8,128)S(1)} %get-tuple-element.33.table_ref, bf16[17408,128]{1,0:T(8,128)(2,1)S(1)} %more_sigma.1.sigma_in_ref, ...), custom_call_target="tpu_custom_call", output_to_operand_aliasing={{2}: (1, {})} | custom-call | flops 5368709120 | bytes 12582912 | tf_op jit(solution)/shard_map/carry/pallas_call | solution.py:361
  56.5 4.7 %collective-permute-start.10 = (bf16[512,1024]{1,0:T(8,128)(2,1)S(1)}, bf16[512,1024]{1,0:T(8,128)(2,1)S(1)}, u32[]{:S(2)}, u32[]{:S(2)}) collective-permute-start(bf16[512,1024]{1,0:T(8,128)(2,1)S(1)} %get-tuple-element.41), channel_id=1, source_target_pairs={{0,1},{1,0},{2,3},{3,2},{4,5},{5,4},{6,7},{7,6},{8,9},{9,8},{10,11... | collective-permute-start | bytes 3145736 | tf_op jit(solution)/shard_map/ppermute | solution.py:424
  61.2 1.2 %own_product.1.own_ref = f32[512,1024]{1,0:T(8,128)S(1)} custom-call(bf16[1024,1024]{1,0:T(8,128)(2,1)S(1)} %turn_wide.1.turned_ref, bf16[1024,1024]{1,0:T(8,128)(2,1)S(1)} %get-tuple-element.39.carried_ref, f32[512,1024]{1,0:T(8,128)S(1)} %get-tuple-element.40.square_ref), custom_call_target="tpu_custom_call" | custom-call | flops 1073741824 | bytes 8388608 | tf_op jit(solution)/shard_map/own_product/pallas_call | solution.py:386
  62.5 1.0 %collective-permute-done.10.received_ref = bf16[512,1024]{1,0:T(8,128)(2,1)S(1)} collective-permute-done((bf16[512,1024]{1,0:T(8,128)(2,1)S(1)}, bf16[512,1024]{1,0:T(8,128)(2,1)S(1)}, u32[]{:S(2)}, u32[]{:S(2)}) %collective-permute-start.10) | collective-permute-done | bytes 1048608 | tf_op jit(solution)/shard_map/ppermute | solution.py:424
  63.5 1.9 %finish.1 = (f32[512,1024]{1,0:T(8,128)}, f32[1,512]{1,0:T(1,128)}) custom-call(f32[512,1024]{1,0:T(8,128)S(1)} %own_product.1.own_ref, bf16[512,1024]{1,0:T(8,128)(2,1)S(1)} %collective-permute-done.10.received_ref), custom_call_target="tpu_custom_call" | custom-call | bytes 6291456 | tf_op jit(solution)/shard_map/finish/pallas_call | solution.py:408
  (2 shorter events, 0.0 us)
Async XLA Ops:
  0.6 34.4 %copy-start.2 = (s32[64,16]{0,1:T(8,128)S(1)}, s32[64,16]{0,1:T(8,128)}, u32[]{:S(2)}) copy-start(s32[64,16]{0,1:T(8,128)} %param.7) | copy-start | bytes 12292
  0.6 23.5 %collective-permute-start.3 = (bf16[512,1024]{1,0:T(8,128)(2,1)}, bf16[512,1024]{1,0:T(8,128)(2,1)S(1)}, u32[]{:S(2)}, u32[]{:S(2)}) collective-permute-start(bf16[512,1024]{1,0:T(8,128)(2,1)} %mine_ref.1), channel_id=1, source_target_pairs={{0,1},{1,0},{2,3},{3,2},{4,5},{5,4},{6,7},{7,6},{8,9},{9,8},{10,11... | collective-permute-start | bytes 3145736 | tf_op jit(solution)/shard_map/ppermute | solution.py:424
  24.1 8.0 %collective-permute-start.2 = (bf16[2048,128]{1,0:T(8,128)(2,1)S(1)}, bf16[2048,128]{1,0:T(8,128)(2,1)S(1)}, u32[]{:S(2)}, u32[]{:S(2)}) collective-permute-start(bf16[2048,128]{1,0:T(8,128)(2,1)S(1)} %bitcast.5), channel_id=1, source_target_pairs={{0,96},{1,33},{2,98},{3,35},{4,100},{5,37},{6,102},{7,39},{8,104},... | collective-permute-start | bytes 1572872 | tf_op jit(solution)/shard_map/ppermute | solution.py:82
  24.1 8.0 %collective-permute-start.1 = (bf16[2048,128]{1,0:T(8,128)(2,1)S(1)}, bf16[2048,128]{1,0:T(8,128)(2,1)S(1)}, u32[]{:S(2)}, u32[]{:S(2)}) collective-permute-start(bf16[2048,128]{1,0:T(8,128)(2,1)S(1)} %bitcast.6), channel_id=1, source_target_pairs={{0,24},{1,9},{2,26},{3,11},{4,28},{5,13},{6,30},{7,15},{8,16},{9,1... | collective-permute-start | bytes 1572872 | tf_op jit(solution)/shard_map/ppermute | solution.py:82
  24.1 8.0 %collective-permute-start = (bf16[2048,128]{1,0:T(8,128)(2,1)S(1)}, bf16[2048,128]{1,0:T(8,128)(2,1)S(1)}, u32[]{:S(2)}, u32[]{:S(2)}) collective-permute-start(bf16[2048,128]{1,0:T(8,128)(2,1)S(1)} %bitcast.7), channel_id=1, source_target_pairs={{0,6},{1,3},{2,4},{3,1},{4,2},{5,7},{6,0},{7,5},{8,14},{9,11},{10,... | collective-permute-start | bytes 1572872 | tf_op jit(solution)/shard_map/ppermute | solution.py:82
  24.1 1.2 %copy-start.1 = (bf16[512,1024]{1,0:T(8,128)(2,1)S(1)}, bf16[512,1024]{1,0:T(8,128)(2,1)}, u32[]{:S(2)}) copy-start(bf16[512,1024]{1,0:T(8,128)(2,1)} %mine_ref.1) | copy-start | bytes 3145732
  32.1 10.3 %collective-permute-start.4 = (bf16[2048,128]{1,0:T(8,128)(2,1)S(1)}, bf16[2048,128]{1,0:T(8,128)(2,1)S(1)}, u32[]{:S(2)}, u32[]{:S(2)}) collective-permute-start(bf16[2048,128]{1,0:T(8,128)(2,1)S(1)} %collective-permute-done.x_ref.refs_1_), channel_id=1, source_target_pairs={{0,24},{1,9},{2,26},{3,11},{4,28},{5,13},{6,30},{7,15},{8,16},{9,1... | collective-permute-start | bytes 1572872 | tf_op jit(solution)/shard_map/ppermute | solution.py:82
  33.6 8.8 %collective-permute-start.5 = (bf16[2048,128]{1,0:T(8,128)(2,1)S(1)}, bf16[2048,128]{1,0:T(8,128)(2,1)S(1)}, u32[]{:S(2)}, u32[]{:S(2)}) collective-permute-start(bf16[2048,128]{1,0:T(8,128)(2,1)S(1)} %collective-permute-done.1.y_ref.refs_2_), channel_id=1, source_target_pairs={{0,96},{1,33},{2,98},{3,35},{4,100},{5,37},{6,102},{7,39},{8,104},... | collective-permute-start | bytes 1572872 | tf_op jit(solution)/shard_map/ppermute | solution.py:82
  35.1 8.3 %collective-permute-start.6 = (bf16[2048,128]{1,0:T(8,128)(2,1)S(1)}, bf16[2048,128]{1,0:T(8,128)(2,1)S(1)}, u32[]{:S(2)}, u32[]{:S(2)}) collective-permute-start(bf16[2048,128]{1,0:T(8,128)(2,1)S(1)} %collective-permute-done.2.z_ref.refs_3_), channel_id=1, source_target_pairs={{0,6},{1,3},{2,4},{3,1},{4,2},{5,7},{6,0},{7,5},{8,14},{9,11},{10,... | collective-permute-start | bytes 1572872 | tf_op jit(solution)/shard_map/ppermute | solution.py:82
  35.1 2.2 %copy-start = (bf16[1024,1024]{1,0:T(8,128)(2,1)S(1)}, bf16[1024,1024]{1,0:T(8,128)(2,1)}, u32[]{:S(2)}) copy-start(bf16[1024,1024]{1,0:T(8,128)(2,1)} %coupling_ref.1) | copy-start | bytes 6291460
  43.4 4.7 %collective-permute-start.7 = (bf16[1024,1024]{1,0:T(8,128)(2,1)S(1)}, bf16[1024,1024]{1,0:T(8,128)(2,1)S(1)}, u32[]{:S(2)}, u32[]{:S(2)}) collective-permute-start(bf16[1024,1024]{1,0:T(8,128)(2,1)S(1)} %get-tuple-element.34.mine_ref), channel_id=1, source_target_pairs={{0,1},{1,0},{2,3},{3,2},{4,5},{5,4},{6,7},{7,6},{8,9},{9,8},{10,11... | collective-permute-start | bytes 6291464 | tf_op jit(solution)/shard_map/ppermute | solution.py:424
  44.3 5.6 %collective-permute-start.8 = (bf16[1024,128]{1,0:T(8,128)(2,1)S(1)}, bf16[1024,128]{1,0:T(8,128)(2,1)S(1)}, u32[]{:S(2)}, u32[]{:S(2)}) collective-permute-start(bf16[1024,128]{1,0:T(8,128)(2,1)S(1)} %slice.6), channel_id=1, source_target_pairs={{0,96},{1,33},{2,98},{3,35},{4,100},{5,37},{6,102},{7,39},{8,104},... | collective-permute-start | bytes 786440 | tf_op jit(solution)/shard_map/ppermute | solution.py:82
  44.5 5.6 %collective-permute-start.9 = (bf16[1024,128]{1,0:T(8,128)(2,1)S(1)}, bf16[1024,128]{1,0:T(8,128)(2,1)S(1)}, u32[]{:S(2)}, u32[]{:S(2)}) collective-permute-start(bf16[1024,128]{1,0:T(8,128)(2,1)S(1)} %slice.7), channel_id=1, source_target_pairs={{0,24},{1,9},{2,26},{3,11},{4,28},{5,13},{6,30},{7,15},{8,16},{9,1... | collective-permute-start | bytes 786440 | tf_op jit(solution)/shard_map/ppermute | solution.py:82
  56.5 7.0 %collective-permute-start.10 = (bf16[512,1024]{1,0:T(8,128)(2,1)S(1)}, bf16[512,1024]{1,0:T(8,128)(2,1)S(1)}, u32[]{:S(2)}, u32[]{:S(2)}) collective-permute-start(bf16[512,1024]{1,0:T(8,128)(2,1)S(1)} %get-tuple-element.41), channel_id=1, source_target_pairs={{0,1},{1,0},{2,3},{3,2},{4,5},{5,4},{6,7},{7,6},{8,9},{9,8},{10,11... | collective-permute-start | bytes 3145736 | tf_op jit(solution)/shard_map/ppermute | solution.py:424

commit v9 on v7

--- a/solution.py
+++ b/solution.py
@@ -327,7 +327,7 @@
         blocks = [sigma_ref[c * SIDE : (c + 1) * SIDE, :] for c in range(at, at + HALF)]
         return jnp.concatenate(blocks, axis=1)
 
-    tile = 256
+    tile = 512
     for n in range(0, SIDE, tile):
         columns = slice(n, n + tile)
         carried_ref[:, columns] = (

time: 64.7 us -> 64.8 us (level)
  transfers between devices with their start and end apart: 11 -> 11, of which waited for: 6 -> 7; matrix products, arithmetic and copies ran while one was open for 0% -> 0% of each run, Pallas kernels for 24% -> 24%
where the time goes in v9:
time: 64.8 us; the launch traced here: 64.4 us
  Pallas kernels  23.5 us (36%)
  blocking collectives  20.5 us (32%)
  starting transfers between devices  9.25 us (14%)
  waiting for transfers between devices  9.11 us (14%)
  local copies, waits for them, and re-layouts  1.26 us (2%)
  between operations  0.74 us (1%)
    all_to_all x1, blocking collectives, gather_cube(): lax.all_to_all(parts, AXES, split_axis=0, concat_axis=0, tiled=True, axis...  20.5 us
    ppermute x8, waiting for transfers between devices, across(): return lax.ppermute(x, AXES, pairs)  7.51 us
    pallas_call x1, Pallas kernels, carry(): pl.pallas_call(carry_kernel, out_shape=(jax.ShapeDtypeStruct((SIDE, SIDE)...  6.44 us
    ppermute x3, starting transfers between devices, swap(): return lax.ppermute(x, 'panel', [(0, 1), (1, 0)])  6.12 us
    pallas_call x1, Pallas kernels, solve(): pl.pallas_call(solve_kernel, out_shape=(jax.ShapeDtypeStruct((SIDE, SIDE)...  5.1 us
    ppermute x8, starting transfers between devices, across(): return lax.ppermute(x, AXES, pairs)  3.13 us
    pallas_call x1, Pallas kernels, make_sigma(): pl.pallas_call(sigma_kernel, out_shape=SIGMA, in_specs=[SMEM, SMEM] + [VM...  2.96 us
    pallas_call x1, Pallas kernels, invert_blocks(): pl.pallas_call(blocks_kernel, out_shape=(slim, slim, jax.ShapeDtypeStruct...  2.59 us
  transfers between devices with their start and end apart: 11, of which 7 were waited for; matrix products, arithmetic and copies ran while one was open for 0% of the time, Pallas kernels for 24%

profile of v9, /device:TPU:1, one launch (start us, length us, event | category | flops | bytes accessed | tf_op | source)
XLA Modules:
  0.0 64.4 jit_solution(12474495582020223928)
XLA Ops:
  0.6 0.0 copy-start
  0.6 1.5 %collective-permute-start.3 = (bf16[512,1024]{1,0:T(8,128)(2,1)}, bf16[512,1024]{1,0:T(8,128)(2,1)S(1)}, u32[]{:S(2)}, u32[]{:S(2)}) collective-permute-start(bf16[512,1024]{1,0:T(8,128)(2,1)} %mine_ref.1), channel_id=1, source_target_pairs={{0,1},{1,0},{2,3},{3,2},{4,5},{5,4},{6,7},{7,6},{8,9},{9,8},{10,11... | collective-permute-start | bytes 3145736 | tf_op jit(solution)/shard_map/ppermute | solution.py:406
  2.1 1.5 %pick_strips.1 = (bf16[2048,128]{1,0:T(8,128)(2,1)S(1)}, s32[8,64]{1,0:T(8,128)S(1)}) custom-call(s32[16,64]{1,0:T(8,128)} %bitcast.14, s32[16,64]{1,0:T(8,128)} %bitcast.11, bf16[512,128]{1,0:T(8,128)(2,1)} %strips_hbm.1), custom_call_target="tpu_custom_call" | custom-call | bytes 1048576 | tf_op jit(solution)/shard_map/pick_strips/pallas_call | solution.py:121
  3.6 20.5 %all_to_all.11 = bf16[8,256,128]{2,1,0:T(8,128)(2,1)S(1)} all-to-all(bf16[8,256,128]{2,1,0:T(8,128)(2,1)S(1)} %bitcast.10), channel_id=1, replica_groups={{0,2,8,10,32,34,40,42},{4,6,12,14,36,38,44,46},{16,18,24,26,48,50,56,58..., dimensions={0} | all-to-all | bytes 1048576 | tf_op jit(solution)/shard_map/all_to_all | solution.py:71
  24.1 0.0 collective-permute-start.2
  24.1 0.0 collective-permute-start.1
  24.1 0.0 collective-permute-start
  24.1 0.0 collective-permute-done.3.other_ref
  24.1 0.0 copy-start.1
  24.1 1.2 %copy-done.1 = bf16[512,1024]{1,0:T(8,128)(2,1)S(1)} copy-done((bf16[512,1024]{1,0:T(8,128)(2,1)S(1)}, bf16[512,1024]{1,0:T(8,128)(2,1)}, u32[]{:S(2)}) %copy-start.1) | copy-done | bytes 1048600
  25.3 2.6 %invert_blocks.1 = (bf16[1024,128]{1,0:T(8,128)(2,1)S(1)}, bf16[1024,128]{1,0:T(8,128)(2,1)S(1)}, bf16[1024,1024]{1,0:T(8,128)(2,1)S(1)}) custom-call(bf16[512,1024]{1,0:T(8,128)(2,1)S(1)} %copy-done.1, bf16[512,1024]{1,0:T(8,128)(2,1)S(1)} %collective-permute-done.3.other_ref, bf16[2048,128]{1,0:T(8,128)(2,1)S(1)} %bitcast.8), custom_call_target="tpu_custom_call" | custom-call | flops 2097152 | bytes 65536 | tf_op jit(solution)/shard_map/invert_blocks/pallas_call | solution.py:185
  27.9 4.2 %collective-permute-done.2.z_ref.refs_4_ = bf16[2048,128]{1,0:T(8,128)(2,1)S(1)} collective-permute-done((bf16[2048,128]{1,0:T(8,128)(2,1)S(1)}, bf16[2048,128]{1,0:T(8,128)(2,1)S(1)}, u32[]{:S(2)}, u32[]{:S(2)}) %collective-permute-start.2) | collective-permute-done | bytes 524320 | tf_op jit(solution)/shard_map/ppermute | solution.py:82
  32.1 0.0 collective-permute-done.1.y_ref.refs_2_
  32.1 0.0 collective-permute-done.x_ref.refs_1_
  32.1 1.5 %collective-permute-start.4 = (bf16[2048,128]{1,0:T(8,128)(2,1)S(1)}, bf16[2048,128]{1,0:T(8,128)(2,1)S(1)}, u32[]{:S(2)}, u32[]{:S(2)}) collective-permute-start(bf16[2048,128]{1,0:T(8,128)(2,1)S(1)} %collective-permute-done.x_ref.refs_1_), channel_id=1, source_target_pairs={{0,24},{1,9},{2,26},{3,11},{4,28},{5,13},{6,30},{7,15},{8,16},{9,1... | collective-permute-start | bytes 1572872 | tf_op jit(solution)/shard_map/ppermute | solution.py:82
  33.6 1.5 %collective-permute-start.5 = (bf16[2048,128]{1,0:T(8,128)(2,1)S(1)}, bf16[2048,128]{1,0:T(8,128)(2,1)S(1)}, u32[]{:S(2)}, u32[]{:S(2)}) collective-permute-start(bf16[2048,128]{1,0:T(8,128)(2,1)S(1)} %collective-permute-done.1.y_ref.refs_2_), channel_id=1, source_target_pairs={{0,96},{1,33},{2,98},{3,35},{4,100},{5,37},{6,102},{7,39},{8,104},... | collective-permute-start | bytes 1572872 | tf_op jit(solution)/shard_map/ppermute | solution.py:82
  35.1 0.0 collective-permute-start.6
  35.1 0.0 copy-done
  35.1 0.0 copy-start.2
  35.1 5.1 %solve.1 = (bf16[1024,1024]{1,0:T(8,128)(2,1)S(1)}, f32[512,1024]{1,0:T(8,128)S(1)}) custom-call(bf16[1024,128]{1,0:T(8,128)(2,1)S(1)} %get-tuple-element.27.hi_slim_ref, bf16[1024,128]{1,0:T(8,128)(2,1)S(1)} %get-tuple-element.28.lo_slim_ref, bf16[1024,1024]{1,0:T(8,128)(2,1)S(1)} %get-tuple-element.29.low_ref, bf16[1024,1024]{1,0:T(8,128)(2,1)S(1)} %copy-done, ...), custom_call_target="tpu_custom_call" | custom-call | flops 2097152 | bytes 65536 | tf_op jit(solution)/shard_map/solve/pallas_call | solution.py:230
  40.2 0.3 collective-permute-done.4.refs_3_
  40.5 1.5 %collective-permute-done.5.refs_6_ = bf16[2048,128]{1,0:T(8,128)(2,1)S(1)} collective-permute-done((bf16[2048,128]{1,0:T(8,128)(2,1)S(1)}, bf16[2048,128]{1,0:T(8,128)(2,1)S(1)}, u32[]{:S(2)}, u32[]{:S(2)}) %collective-permute-start.5) | collective-permute-done | bytes 524320 | tf_op jit(solution)/shard_map/ppermute | solution.py:82
  41.9 1.5 %collective-permute-done.6.refs_5_ = bf16[2048,128]{1,0:T(8,128)(2,1)S(1)} collective-permute-done((bf16[2048,128]{1,0:T(8,128)(2,1)S(1)}, bf16[2048,128]{1,0:T(8,128)(2,1)S(1)}, u32[]{:S(2)}, u32[]{:S(2)}) %collective-permute-start.6) | collective-permute-done | bytes 524320 | tf_op jit(solution)/shard_map/ppermute | solution.py:82
  43.4 0.9 %collective-permute-start.7 = (bf16[1024,1024]{1,0:T(8,128)(2,1)S(1)}, bf16[1024,1024]{1,0:T(8,128)(2,1)S(1)}, u32[]{:S(2)}, u32[]{:S(2)}) collective-permute-start(bf16[1024,1024]{1,0:T(8,128)(2,1)S(1)} %get-tuple-element.32.mine_ref), channel_id=1, source_target_pairs={{0,1},{1,0},{2,3},{3,2},{4,5},{5,4},{6,7},{7,6},{8,9},{9,8},{10,11... | collective-permute-start | bytes 6291464 | tf_op jit(solution)/shard_map/ppermute | solution.py:406
  44.3 0.1 collective-permute-start.9
  44.4 0.1 collective-permute-start.8
  44.5 0.0 copy-done.2
  44.5 3.0 %make_sigma.1.sigma_in_ref = bf16[17408,128]{1,0:T(8,128)(2,1)S(1)} custom-call(s32[16,64]{1,0:T(8,128)S(1)} %bitcast.12, s32[8,64]{1,0:T(8,128)S(1)} %get-tuple-element.33.table_ref, bf16[2048,128]{1,0:T(8,128)(2,1)S(1)} %bitcast.9, bf16[2048,128]{1,0:T(8,128)(2,1)S(1)} %collective-permute-done.x_ref.refs_1_, ...), custom_call_target="tpu_custom_call" | custom-call | bytes 10485760 | tf_op jit(solution)/shard_map/make_sigma/pallas_call | solution.py:308
  47.5 0.6 collective-permute-done.7.other_ref
  48.1 1.8 %turn_wide.1.turned_ref = bf16[1024,1024]{1,0:T(8,128)(2,1)S(1)} custom-call(s32[16,64]{1,0:T(8,128)S(1)} %bitcast.13, bf16[1024,1024]{1,0:T(8,128)(2,1)S(1)} %get-tuple-element.32.mine_ref, bf16[1024,1024]{1,0:T(8,128)(2,1)S(1)} %collective-permute-done.7.other_ref), custom_call_target="tpu_custom_call" | custom-call | bytes 8388608 | tf_op jit(solution)/shard_map/turn_wide/pallas_call | solution.py:264
  49.9 0.0 collective-permute-done.9.bottom_ref
  49.9 0.1 collective-permute-done.8.top_ref
  50.0 6.4 %carry.1 = (bf16[1024,1024]{1,0:T(8,128)(2,1)S(1)}, bf16[512,1024]{1,0:T(8,128)(2,1)S(1)}, bf16[17408,128]{1,0:T(8,128)(2,1)S(1)}) custom-call(s32[8,64]{1,0:T(8,128)S(1)} %get-tuple-element.33.table_ref, bf16[17408,128]{1,0:T(8,128)(2,1)S(1)} %make_sigma.1.sigma_in_ref, ...), custom_call_target="tpu_custom_call", output_to_operand_aliasing={{2}: (1, {})} | custom-call | flops 5368709120 | bytes 12582912 | tf_op jit(solution)/shard_map/carry/pallas_call | solution.py:343
  56.5 3.7 %collective-permute-start.10 = (bf16[512,1024]{1,0:T(8,128)(2,1)S(1)}, bf16[512,1024]{1,0:T(8,128)(2,1)S(1)}, u32[]{:S(2)}, u32[]{:S(2)}) collective-permute-start(bf16[512,1024]{1,0:T(8,128)(2,1)S(1)} %get-tuple-element.39), channel_id=1, source_target_pairs={{0,1},{1,0},{2,3},{3,2},{4,5},{5,4},{6,7},{7,6},{8,9},{9,8},{10,11... | collective-permute-start | bytes 3145736 | tf_op jit(solution)/shard_map/ppermute | solution.py:406
  60.2 1.2 %own_product.1.own_ref = f32[512,1024]{1,0:T(8,128)S(1)} custom-call(bf16[1024,1024]{1,0:T(8,128)(2,1)S(1)} %turn_wide.1.turned_ref, bf16[1024,1024]{1,0:T(8,128)(2,1)S(1)} %get-tuple-element.37.carried_ref, f32[512,1024]{1,0:T(8,128)S(1)} %get-tuple-element.38.square_ref), custom_call_target="tpu_custom_call" | custom-call | flops 1073741824 | bytes 8388608 | tf_op jit(solution)/shard_map/own_product/pallas_call | solution.py:368
  61.4 1.0 %collective-permute-done.10.received_ref = bf16[512,1024]{1,0:T(8,128)(2,1)S(1)} collective-permute-done((bf16[512,1024]{1,0:T(8,128)(2,1)S(1)}, bf16[512,1024]{1,0:T(8,128)(2,1)S(1)}, u32[]{:S(2)}, u32[]{:S(2)}) %collective-permute-start.10) | collective-permute-done | bytes 1048608 | tf_op jit(solution)/shard_map/ppermute | solution.py:406
  62.5 1.9 %finish.1 = (f32[512,1024]{1,0:T(8,128)}, f32[1,512]{1,0:T(1,128)}) custom-call(f32[512,1024]{1,0:T(8,128)S(1)} %own_product.1.own_ref, bf16[512,1024]{1,0:T(8,128)(2,1)S(1)} %collective-permute-done.10.received_ref), custom_call_target="tpu_custom_call" | custom-call | bytes 6291456 | tf_op jit(solution)/shard_map/finish/pallas_call | solution.py:390
  (2 shorter events, 0.0 us)
Async XLA Ops:
  0.6 34.4 %copy-start = (bf16[1024,1024]{1,0:T(8,128)(2,1)S(1)}, bf16[1024,1024]{1,0:T(8,128)(2,1)}, u32[]{:S(2)}) copy-start(bf16[1024,1024]{1,0:T(8,128)(2,1)} %coupling_ref.1) | copy-start | bytes 6291460
  0.6 23.5 %collective-permute-start.3 = (bf16[512,1024]{1,0:T(8,128)(2,1)}, bf16[512,1024]{1,0:T(8,128)(2,1)S(1)}, u32[]{:S(2)}, u32[]{:S(2)}) collective-permute-start(bf16[512,1024]{1,0:T(8,128)(2,1)} %mine_ref.1), channel_id=1, source_target_pairs={{0,1},{1,0},{2,3},{3,2},{4,5},{5,4},{6,7},{7,6},{8,9},{9,8},{10,11... | collective-permute-start | bytes 3145736 | tf_op jit(solution)/shard_map/ppermute | solution.py:406
  24.1 8.0 %collective-permute-start.2 = (bf16[2048,128]{1,0:T(8,128)(2,1)S(1)}, bf16[2048,128]{1,0:T(8,128)(2,1)S(1)}, u32[]{:S(2)}, u32[]{:S(2)}) collective-permute-start(bf16[2048,128]{1,0:T(8,128)(2,1)S(1)} %bitcast.5), channel_id=1, source_target_pairs={{0,96},{1,33},{2,98},{3,35},{4,100},{5,37},{6,102},{7,39},{8,104},... | collective-permute-start | bytes 1572872 | tf_op jit(solution)/shard_map/ppermute | solution.py:82
  24.1 8.0 %collective-permute-start.1 = (bf16[2048,128]{1,0:T(8,128)(2,1)S(1)}, bf16[2048,128]{1,0:T(8,128)(2,1)S(1)}, u32[]{:S(2)}, u32[]{:S(2)}) collective-permute-start(bf16[2048,128]{1,0:T(8,128)(2,1)S(1)} %bitcast.6), channel_id=1, source_target_pairs={{0,24},{1,9},{2,26},{3,11},{4,28},{5,13},{6,30},{7,15},{8,16},{9,1... | collective-permute-start | bytes 1572872 | tf_op jit(solution)/shard_map/ppermute | solution.py:82
  24.1 8.0 %collective-permute-start = (bf16[2048,128]{1,0:T(8,128)(2,1)S(1)}, bf16[2048,128]{1,0:T(8,128)(2,1)S(1)}, u32[]{:S(2)}, u32[]{:S(2)}) collective-permute-start(bf16[2048,128]{1,0:T(8,128)(2,1)S(1)} %bitcast.7), channel_id=1, source_target_pairs={{0,6},{1,3},{2,4},{3,1},{4,2},{5,7},{6,0},{7,5},{8,14},{9,11},{10,... | collective-permute-start | bytes 1572872 | tf_op jit(solution)/shard_map/ppermute | solution.py:82
  24.1 1.2 %copy-start.1 = (bf16[512,1024]{1,0:T(8,128)(2,1)S(1)}, bf16[512,1024]{1,0:T(8,128)(2,1)}, u32[]{:S(2)}) copy-start(bf16[512,1024]{1,0:T(8,128)(2,1)} %mine_ref.1) | copy-start | bytes 3145732
  32.1 8.3 %collective-permute-start.4 = (bf16[2048,128]{1,0:T(8,128)(2,1)S(1)}, bf16[2048,128]{1,0:T(8,128)(2,1)S(1)}, u32[]{:S(2)}, u32[]{:S(2)}) collective-permute-start(bf16[2048,128]{1,0:T(8,128)(2,1)S(1)} %collective-permute-done.x_ref.refs_1_), channel_id=1, source_target_pairs={{0,24},{1,9},{2,26},{3,11},{4,28},{5,13},{6,30},{7,15},{8,16},{9,1... | collective-permute-start | bytes 1572872 | tf_op jit(solution)/shard_map/ppermute | solution.py:82
  33.6 8.3 %collective-permute-start.5 = (bf16[2048,128]{1,0:T(8,128)(2,1)S(1)}, bf16[2048,128]{1,0:T(8,128)(2,1)S(1)}, u32[]{:S(2)}, u32[]{:S(2)}) collective-permute-start(bf16[2048,128]{1,0:T(8,128)(2,1)S(1)} %collective-permute-done.1.y_ref.refs_2_), channel_id=1, source_target_pairs={{0,96},{1,33},{2,98},{3,35},{4,100},{5,37},{6,102},{7,39},{8,104},... | collective-permute-start | bytes 1572872 | tf_op jit(solution)/shard_map/ppermute | solution.py:82
  35.1 8.3 %collective-permute-start.6 = (bf16[2048,128]{1,0:T(8,128)(2,1)S(1)}, bf16[2048,128]{1,0:T(8,128)(2,1)S(1)}, u32[]{:S(2)}, u32[]{:S(2)}) collective-permute-start(bf16[2048,128]{1,0:T(8,128)(2,1)S(1)} %collective-permute-done.2.z_ref.refs_4_), channel_id=1, source_target_pairs={{0,6},{1,3},{2,4},{3,1},{4,2},{5,7},{6,0},{7,5},{8,14},{9,11},{10,... | collective-permute-start | bytes 1572872 | tf_op jit(solution)/shard_map/ppermute | solution.py:82
  35.1 9.5 %copy-start.2 = (s32[64,16]{0,1:T(8,128)S(1)}, s32[64,16]{0,1:T(8,128)}, u32[]{:S(2)}) copy-start(s32[64,16]{0,1:T(8,128)} %param.7) | copy-start | bytes 12292
  43.4 4.7 %collective-permute-start.7 = (bf16[1024,1024]{1,0:T(8,128)(2,1)S(1)}, bf16[1024,1024]{1,0:T(8,128)(2,1)S(1)}, u32[]{:S(2)}, u32[]{:S(2)}) collective-permute-start(bf16[1024,1024]{1,0:T(8,128)(2,1)S(1)} %get-tuple-element.32.mine_ref), channel_id=1, source_target_pairs={{0,1},{1,0},{2,3},{3,2},{4,5},{5,4},{6,7},{7,6},{8,9},{9,8},{10,11... | collective-permute-start | bytes 6291464 | tf_op jit(solution)/shard_map/ppermute | solution.py:406
  44.3 5.6 %collective-permute-start.9 = (bf16[1024,128]{1,0:T(8,128)(2,1)S(1)}, bf16[1024,128]{1,0:T(8,128)(2,1)S(1)}, u32[]{:S(2)}, u32[]{:S(2)}) collective-permute-start(bf16[1024,128]{1,0:T(8,128)(2,1)S(1)} %slice.7), channel_id=1, source_target_pairs={{0,24},{1,9},{2,26},{3,11},{4,28},{5,13},{6,30},{7,15},{8,16},{9,1... | collective-permute-start | bytes 786440 | tf_op jit(solution)/shard_map/ppermute | solution.py:82
  44.4 5.6 %collective-permute-start.8 = (bf16[1024,128]{1,0:T(8,128)(2,1)S(1)}, bf16[1024,128]{1,0:T(8,128)(2,1)S(1)}, u32[]{:S(2)}, u32[]{:S(2)}) collective-permute-start(bf16[1024,128]{1,0:T(8,128)(2,1)S(1)} %slice.6), channel_id=1, source_target_pairs={{0,96},{1,33},{2,98},{3,35},{4,100},{5,37},{6,102},{7,39},{8,104},... | collective-permute-start | bytes 786440 | tf_op jit(solution)/shard_map/ppermute | solution.py:82
  56.5 6.0 %collective-permute-start.10 = (bf16[512,1024]{1,0:T(8,128)(2,1)S(1)}, bf16[512,1024]{1,0:T(8,128)(2,1)S(1)}, u32[]{:S(2)}, u32[]{:S(2)}) collective-permute-start(bf16[512,1024]{1,0:T(8,128)(2,1)S(1)} %get-tuple-element.39), channel_id=1, source_target_pairs={{0,1},{1,0},{2,3},{3,2},{4,5},{5,4},{6,7},{7,6},{8,9},{9,8},{10,11... | collective-permute-start | bytes 3145736 | tf_op jit(solution)/shard_map/ppermute | solution.py:406
